TPU v7x, 32 devices: a whole 2x2x4 slice. The times are simulated.
32 devices in a mesh: dp: 4 (over x, core), fsdp: 8 (over z, y).
Axes of the slice: x: 2, y: 2, z: 4, core: 2. Of those that a mesh axis runs over, the one named last changes fastest.
Arguments:
- tokens: bfloat16 [23040, 512], P(('dp', 'fsdp')), may hold values from -6 to 6
- cotangent: bfloat16 [23040, 512], P(('dp', 'fsdp')), may hold values from -6 to 6
- segment_ids: int32 [23040], P(('dp', 'fsdp')), may hold values from 0 to 14, as said below
- pad_mask: int32 [23040], P(('dp', 'fsdp')), may hold values from 0 to 1, as said below
- expert_ids: int32 [23040, 2], P(('dp', 'fsdp')), may hold values from 0 to 7, as said below
- priority: int32 [32, 720], P(('dp', 'fsdp')), may hold values from 0 to 719, each once within a row
- ln1_gain: bfloat16 [512], P('fsdp'), may hold values from 0.5 to 1.5
- ln1_shift: bfloat16 [512], P('fsdp'), may hold values from -1.25 to 1.25
- w_qkv: bfloat16 [512, 1536], P('fsdp'), may hold values from -0.25 to 0.25
- b_qv: bfloat16 [1024], P('fsdp'), may hold values from -1.25 to 1.25
- w_o: bfloat16 [512, 512], P('fsdp'), may hold values from -2 to 2
- b_o: bfloat16 [512], P('fsdp'), may hold values from -1.25 to 1.25
- ln2_gain: bfloat16 [512], P('fsdp'), may hold values from 0.5 to 1.5
- ln2_shift: bfloat16 [512], P('fsdp'), may hold values from -1.25 to 1.25
- w_router: bfloat16 [512, 8], P('fsdp'), may hold values from -0.1875 to 0.1875
- w_in: bfloat16 [8, 512, 2048], P('fsdp'), may hold values from -0.25 to 0.25
- b_in: bfloat16 [8, 2048], P('fsdp'), may hold values from -0.625 to 0.625
- w_out: bfloat16 [8, 2048, 512], P('fsdp'), may hold values from -0.5 to 0.5
- b_out: bfloat16 [8, 512], P('fsdp'), may hold values from -3 to 3
Outputs:
- output: bfloat16 [23040, 512], P(('dp', 'fsdp'))
- d_tokens: float32 [23040, 512], P(('dp', 'fsdp'))
- d_ln1_gain: float32 [512], P('fsdp')
- d_ln1_shift: float32 [512], P('fsdp')
- d_w_qkv: float32 [512, 1536], P('fsdp')
- d_b_qv: float32 [1024], P('fsdp')
- d_w_o: float32 [512, 512], P('fsdp')
- d_b_o: float32 [512], P('fsdp')
- d_ln2_gain: float32 [512], P('fsdp')
- d_ln2_shift: float32 [512], P('fsdp')
- d_w_router: float32 [512, 8], P('fsdp')
- d_w_in: float32 [8, 512, 2048], P('fsdp')
- d_b_in: float32 [8, 2048], P('fsdp')
- d_w_out: float32 [8, 2048, 512], P('fsdp')
- d_b_out: float32 [8, 512], P('fsdp')
Inputs may be any that keep to these rules, and one draw needn't show every extreme that they name: `segment_ids`: within each sequence of 720 slots the numbers never fall; each image holds 49 or 144 slots; padding slots carry 14 and come last. `pad_mask`: 1 exactly at the slots whose segment number is under 14. `expert_ids`: the two experts of a slot differ. `priority`: each row holds each of 0 to 719 once.
All inputs are finite; a program needn't handle non-finite values.
Results may differ from a plain program's by a relative error of at most 0.025.
Values may be sent and summed in bfloat16 or wider, within the bound.
A program may use at most 192 MiB of HBM per device.

v0:
```python
from functools import partial

import jax
import jax.numpy as jnp
from jax import lax
from jax.sharding import PartitionSpec as P

HEADS = 8
SLOTS = 720


EPS = 1e-06


def layer_norm(tensor, gain_vec, shift_vec):
    row_mean = jnp.mean(tensor, axis=-1, keepdims=True)
    centred = tensor - row_mean
    inv_std = lax.rsqrt(jnp.mean(centred * centred, axis=-1, keepdims=True) + EPS)
    normed = centred * inv_std
    return (normed * gain_vec + shift_vec, normed, inv_std)


def norm_back(grad_in, normed, inv_std, gain_vec):
    scaled = grad_in * gain_vec
    corrected = (
        scaled
        - jnp.mean(scaled, axis=-1, keepdims=True)
        - normed * jnp.mean(scaled * normed, axis=-1, keepdims=True)
    )
    return (inv_std * corrected, jnp.sum(grad_in * normed, axis=0), jnp.sum(grad_in, axis=0))


def split_heads(tensor):
    return tensor.reshape(tensor.shape[0], HEADS, -1)


def allowed_pairs(segment, live_mask):
    same_image = segment[:, None] == segment[None, :]
    self_pair = jnp.arange(segment.shape[0])[:, None] == jnp.arange(segment.shape[0])[None, :]
    return same_image & ((live_mask[None, :] > 0) | self_pair)


def masked_scores(query_seq, key_seq, segment_seq, live_seq, head_scale):
    raw_scores = (
        jnp.einsum(
            "qhd,khd->hqk",
            split_heads(query_seq),
            split_heads(key_seq),
            preferred_element_type=jnp.float32,
        )
        * head_scale
    )
    return jnp.where(allowed_pairs(segment_seq, live_seq)[None], raw_scores, -1e30)


def attend_block(pieces, head_scale):
    query_seq, key_seq, value_seq, segment_seq, live_seq = pieces
    scores = masked_scores(query_seq, key_seq, segment_seq, live_seq, head_scale)
    row_max = jnp.max(scores, axis=-1, keepdims=True)
    log_total = row_max + jnp.log(jnp.sum(jnp.exp(scores - row_max), axis=-1, keepdims=True))
    softmaxed = jnp.exp(scores - log_total).astype(jnp.bfloat16)
    mixed = jnp.einsum(
        "hqk,khd->qhd", softmaxed, split_heads(value_seq), preferred_element_type=jnp.float32
    )
    return (mixed.reshape(query_seq.shape).astype(jnp.bfloat16), log_total)


def attend_back(pieces, head_scale):
    query_seq, key_seq, value_seq, segment_seq, live_seq, log_total, grad_seq = pieces
    softmaxed = jnp.exp(
        masked_scores(query_seq, key_seq, segment_seq, live_seq, head_scale) - log_total
    )
    d_soft = jnp.einsum(
        "qhd,khd->hqk",
        split_heads(grad_seq),
        split_heads(value_seq),
        preferred_element_type=jnp.float32,
    )
    d_scores = (softmaxed * (d_soft - jnp.sum(softmaxed * d_soft, axis=-1, keepdims=True))).astype(
        jnp.bfloat16
    )
    d_query = (
        jnp.einsum(
            "hqk,khd->qhd", d_scores, split_heads(key_seq), preferred_element_type=jnp.float32
        )
        * head_scale
    )
    d_key = (
        jnp.einsum(
            "hqk,qhd->khd", d_scores, split_heads(query_seq), preferred_element_type=jnp.float32
        )
        * head_scale
    )
    d_value = jnp.einsum(
        "hqk,qhd->khd",
        softmaxed.astype(jnp.bfloat16),
        split_heads(grad_seq),
        preferred_element_type=jnp.float32,
    )
    seq_shape = query_seq.shape
    return (
        d_query.reshape(seq_shape).astype(jnp.bfloat16),
        d_key.reshape(seq_shape).astype(jnp.bfloat16),
        d_value.reshape(seq_shape).astype(jnp.bfloat16),
    )


def make_slots(expert_list, priority_row, live_mask, experts, capacity):
    count_tok = expert_list.shape[0]
    at_rank = (
        jnp.zeros((count_tok,), jnp.int32)
        .at[priority_row]
        .set(jnp.arange(count_tok, dtype=jnp.int32))
    )
    ranked = expert_list[at_rank]
    ranked_live = live_mask[at_rank]
    visit_ids = jnp.concatenate([ranked[:, 0], ranked[:, 1]])
    visit_live = jnp.concatenate([ranked_live, ranked_live])
    one_hot = (visit_ids[:, None] == jnp.arange(experts, dtype=jnp.int32)[None, :]).astype(
        jnp.int32
    ) * visit_live[:, None]
    position = jnp.sum(jnp.cumsum(one_hot, axis=0) * one_hot, axis=1) - 1
    slot_visit = jnp.where((visit_live > 0) & (position < capacity), position, capacity)
    by_rank = jnp.stack([slot_visit[:count_tok], slot_visit[count_tok:]], axis=1)
    return by_rank[priority_row]


def expert_hidden(grouped, w_in, b_in):
    return jnp.einsum("secd,edf->secf", grouped, w_in, preferred_element_type=jnp.float32) + b_in[
        None, :, None, :
    ].astype(jnp.float32)


def shards(
    tokens,
    cotangent,
    segment_ids,
    pad_mask,
    expert_ids,
    priority,
    ln1_gain,
    ln1_shift,
    w_qkv,
    b_qv,
    w_o,
    b_o,
    ln2_gain,
    ln2_shift,
    w_router,
    w_in,
    b_in,
    w_out,
    b_out,
):
    gathered = (
        lax.all_gather(ln1_gain, "fsdp", axis=0, tiled=True),
        lax.all_gather(ln1_shift, "fsdp", axis=0, tiled=True),
        lax.all_gather(w_qkv, "fsdp", axis=0, tiled=True),
        lax.all_gather(b_qv, "fsdp", axis=0, tiled=True),
        lax.all_gather(w_o, "fsdp", axis=0, tiled=True),
        lax.all_gather(b_o, "fsdp", axis=0, tiled=True),
        lax.all_gather(ln2_gain, "fsdp", axis=0, tiled=True),
        lax.all_gather(ln2_shift, "fsdp", axis=0, tiled=True),
        lax.all_gather(w_router, "fsdp", axis=0, tiled=True),
    )
    (
        gain_one,
        shift_one,
        full_qkv,
        full_bias,
        full_out,
        out_bias,
        gain_two,
        shift_two,
        full_router,
    ) = gathered
    count_tok, model_width = tokens.shape
    sequences = count_tok // SLOTS
    head_scale = (model_width // HEADS) ** (-0.5)
    experts = full_router.shape[1]
    capacity = (21 * count_tok + 10 * experts - 1) // (10 * experts)
    local_experts = w_in.shape[0]

    def per_seq(tensor):
        return tensor.reshape((sequences, SLOTS) + tensor.shape[1:])

    def by_expert(sent_rows):
        return sent_rows.reshape((-1, local_experts) + sent_rows.shape[1:])

    inputs_f32 = tokens.astype(jnp.float32)
    normed_in, normed_one, inv_one = layer_norm(
        inputs_f32, gain_one.astype(jnp.float32), shift_one.astype(jnp.float32)
    )
    normed_low = normed_in.astype(jnp.bfloat16)
    qkv = jnp.dot(normed_low, full_qkv, preferred_element_type=jnp.float32)
    bias_rows = full_bias.astype(jnp.float32)
    queries = (qkv[:, :model_width] + bias_rows[:model_width]).astype(jnp.bfloat16)
    key_rows = qkv[:, model_width : 2 * model_width].astype(jnp.bfloat16)
    value_rows = (qkv[:, 2 * model_width :] + bias_rows[model_width:]).astype(jnp.bfloat16)
    seq_inputs = (
        per_seq(queries),
        per_seq(key_rows),
        per_seq(value_rows),
        per_seq(segment_ids),
        per_seq(pad_mask),
    )
    mixed, log_total = lax.map(partial(attend_block, head_scale=head_scale), seq_inputs)
    mixed = mixed.reshape(count_tok, model_width)
    middle = (
        inputs_f32
        + jnp.dot(mixed, full_out, preferred_element_type=jnp.float32)
        + out_bias.astype(jnp.float32)
    )
    routed_f32, normed_two, inv_two = layer_norm(
        middle, gain_two.astype(jnp.float32), shift_two.astype(jnp.float32)
    )
    routed = routed_f32.astype(jnp.bfloat16)
    gate_probs = jax.nn.softmax(
        jnp.dot(routed, full_router, preferred_element_type=jnp.float32), axis=-1
    )
    slot_index = make_slots(expert_ids, priority[0], pad_mask, experts, capacity)
    flat_index = jnp.where(
        slot_index < capacity, expert_ids * capacity + slot_index, experts * capacity
    )
    chosen_hot = (
        expert_ids[:, :, None] == jnp.arange(experts, dtype=jnp.int32)[None, None, :]
    ).astype(jnp.float32)
    chosen = jnp.sum(chosen_hot * gate_probs[:, None, :], axis=-1)
    buffer_rows = (
        jnp.zeros((experts * capacity + 1, model_width), jnp.bfloat16)
        .at[flat_index.reshape(-1)]
        .set(jnp.repeat(routed, 2, axis=0))
    )
    buffer_rows = buffer_rows[:-1].reshape(experts, capacity, model_width)
    sent_rows = lax.all_to_all(buffer_rows, "fsdp", split_axis=0, concat_axis=0, tiled=True)
    grouped = by_expert(sent_rows)
    hidden = jax.nn.gelu(expert_hidden(grouped, w_in, b_in), approximate=False).astype(jnp.bfloat16)
    result_rows = jnp.einsum(
        "secf,efd->secd", hidden, w_out, preferred_element_type=jnp.float32
    ) + b_out[None, :, None, :].astype(jnp.float32)
    result_rows = result_rows.astype(jnp.bfloat16).reshape(sent_rows.shape)
    returned_rows = lax.all_to_all(result_rows, "fsdp", split_axis=0, concat_axis=0, tiled=True)
    expert_table = jnp.concatenate(
        [
            returned_rows.reshape(experts * capacity, model_width),
            jnp.zeros((1, model_width), jnp.bfloat16),
        ]
    )
    picked = expert_table[flat_index].astype(jnp.float32)
    output_rows = (middle + jnp.sum(chosen[:, :, None] * picked, axis=1)).astype(jnp.bfloat16)
    grad_rows = cotangent.astype(jnp.float32)
    d_chosen = jnp.sum(grad_rows[:, None, :] * picked, axis=-1)
    d_picked = (chosen[:, :, None] * grad_rows[:, None, :]).astype(jnp.bfloat16)
    d_table = (
        jnp.zeros((experts * capacity + 1, model_width), jnp.bfloat16)
        .at[flat_index.reshape(-1)]
        .set(d_picked.reshape(-1, model_width))
    )
    d_table = d_table[:-1].reshape(experts, capacity, model_width)
    sent_rows, d_sent = (
        lax.all_to_all(buffer_rows, "fsdp", split_axis=0, concat_axis=0, tiled=True),
        lax.all_to_all(d_table, "fsdp", split_axis=0, concat_axis=0, tiled=True),
    )
    grouped = by_expert(sent_rows)
    d_grouped = by_expert(d_sent)
    pre_act = expert_hidden(grouped, w_in, b_in)
    activation, gelu_back = jax.vjp(partial(jax.nn.gelu, approximate=False), pre_act)
    d_w_out = jnp.einsum(
        "secf,secd->efd",
        activation.astype(jnp.bfloat16),
        d_grouped,
        preferred_element_type=jnp.float32,
    )
    d_b_out = jnp.sum(d_grouped.astype(jnp.float32), axis=(0, 2))
    d_act = jnp.einsum("secd,efd->secf", d_grouped, w_out, preferred_element_type=jnp.float32)
    d_pre = gelu_back(d_act)[0].astype(jnp.bfloat16)
    d_w_in = jnp.einsum("secd,secf->edf", grouped, d_pre, preferred_element_type=jnp.float32)
    d_b_in = jnp.sum(d_pre.astype(jnp.float32), axis=(0, 2))
    d_rows = (
        jnp.einsum("secf,edf->secd", d_pre, w_in, preferred_element_type=jnp.float32)
        .astype(jnp.bfloat16)
        .reshape(sent_rows.shape)
    )
    d_buffer = lax.all_to_all(d_rows, "fsdp", split_axis=0, concat_axis=0, tiled=True)
    d_flat = jnp.concatenate(
        [
            d_buffer.reshape(experts * capacity, model_width),
            jnp.zeros((1, model_width), jnp.bfloat16),
        ]
    )
    d_routed = jnp.sum(d_flat[flat_index].astype(jnp.float32), axis=1)
    back_weights = (
        lax.all_gather(ln1_gain, "fsdp", axis=0, tiled=True),
        lax.all_gather(ln1_shift, "fsdp", axis=0, tiled=True),
        lax.all_gather(w_qkv, "fsdp", axis=0, tiled=True),
        lax.all_gather(b_qv, "fsdp", axis=0, tiled=True),
        lax.all_gather(w_o, "fsdp", axis=0, tiled=True),
        lax.all_gather(b_o, "fsdp", axis=0, tiled=True),
        lax.all_gather(ln2_gain, "fsdp", axis=0, tiled=True),
        lax.all_gather(ln2_shift, "fsdp", axis=0, tiled=True),
        lax.all_gather(w_router, "fsdp", axis=0, tiled=True),
    )
    gain_one_back = back_weights[0].astype(jnp.float32)
    qkv_back = back_weights[2]
    out_back = back_weights[4]
    gain_two_back = back_weights[6].astype(jnp.float32)
    router_back = back_weights[8]
    d_gates = jnp.sum(chosen_hot * d_chosen[:, :, None], axis=1)
    d_logits = (
        gate_probs * (d_gates - jnp.sum(gate_probs * d_gates, axis=-1, keepdims=True))
    ).astype(jnp.bfloat16)
    d_w_router = jnp.einsum("td,te->de", routed, d_logits, preferred_element_type=jnp.float32)
    d_routed = d_routed + jnp.einsum(
        "te,de->td", d_logits, router_back, preferred_element_type=jnp.float32
    )
    d_middle_norm, d_gain_two, d_shift_two = norm_back(d_routed, normed_two, inv_two, gain_two_back)
    d_middle = grad_rows + d_middle_norm
    d_attn = d_middle.astype(jnp.bfloat16)
    d_w_o = jnp.einsum("td,te->de", mixed, d_attn, preferred_element_type=jnp.float32)
    d_b_o = jnp.sum(d_attn.astype(jnp.float32), axis=0)
    d_mixed = jnp.einsum("te,de->td", d_attn, out_back, preferred_element_type=jnp.float32).astype(
        jnp.bfloat16
    )
    d_query, d_key, d_value = lax.map(
        partial(attend_back, head_scale=head_scale), seq_inputs + (log_total, per_seq(d_mixed))
    )
    d_query = d_query.reshape(count_tok, model_width)
    d_key = d_key.reshape(count_tok, model_width)
    d_value = d_value.reshape(count_tok, model_width)
    d_qkv = jnp.concatenate([d_query, d_key, d_value], axis=1)
    d_w_qkv = jnp.einsum("td,te->de", normed_low, d_qkv, preferred_element_type=jnp.float32)
    d_b_qv = jnp.concatenate(
        [jnp.sum(d_query.astype(jnp.float32), axis=0), jnp.sum(d_value.astype(jnp.float32), axis=0)]
    )
    d_normed = jnp.einsum("te,de->td", d_qkv, qkv_back, preferred_element_type=jnp.float32)
    d_input_norm, d_gain_one, d_shift_one = norm_back(d_normed, normed_one, inv_one, gain_one_back)
    d_tokens = d_middle + d_input_norm
    shares = (
        lax.psum_scatter(
            d_gain_one.astype(jnp.bfloat16), "fsdp", scatter_dimension=0, tiled=True
        ).astype(jnp.float32),
        lax.psum_scatter(
            d_shift_one.astype(jnp.bfloat16), "fsdp", scatter_dimension=0, tiled=True
        ).astype(jnp.float32),
        lax.psum_scatter(
            d_w_qkv.astype(jnp.bfloat16), "fsdp", scatter_dimension=0, tiled=True
        ).astype(jnp.float32),
        lax.psum_scatter(
            d_b_qv.astype(jnp.bfloat16), "fsdp", scatter_dimension=0, tiled=True
        ).astype(jnp.float32),
        lax.psum_scatter(
            d_w_o.astype(jnp.bfloat16), "fsdp", scatter_dimension=0, tiled=True
        ).astype(jnp.float32),
        lax.psum_scatter(
            d_b_o.astype(jnp.bfloat16), "fsdp", scatter_dimension=0, tiled=True
        ).astype(jnp.float32),
        lax.psum_scatter(
            d_gain_two.astype(jnp.bfloat16), "fsdp", scatter_dimension=0, tiled=True
        ).astype(jnp.float32),
        lax.psum_scatter(
            d_shift_two.astype(jnp.bfloat16), "fsdp", scatter_dimension=0, tiled=True
        ).astype(jnp.float32),
        lax.psum_scatter(
            d_w_router.astype(jnp.bfloat16), "fsdp", scatter_dimension=0, tiled=True
        ).astype(jnp.float32),
    )
    (
        share_g1,
        share_s1,
        share_qkv,
        share_bqv,
        share_wo,
        share_bo,
        share_g2,
        share_s2,
        share_router,
    ) = shares
    totals = (
        lax.psum(share_g1.astype(jnp.bfloat16), "dp").astype(jnp.float32),
        lax.psum(share_s1.astype(jnp.bfloat16), "dp").astype(jnp.float32),
        lax.psum(share_qkv.astype(jnp.bfloat16), "dp").astype(jnp.float32),
        lax.psum(share_bqv.astype(jnp.bfloat16), "dp").astype(jnp.float32),
        lax.psum(share_wo.astype(jnp.bfloat16), "dp").astype(jnp.float32),
        lax.psum(share_bo.astype(jnp.bfloat16), "dp").astype(jnp.float32),
        lax.psum(share_g2.astype(jnp.bfloat16), "dp").astype(jnp.float32),
        lax.psum(share_s2.astype(jnp.bfloat16), "dp").astype(jnp.float32),
        lax.psum(share_router.astype(jnp.bfloat16), "dp").astype(jnp.float32),
        lax.psum(d_w_in.astype(jnp.bfloat16), "dp").astype(jnp.float32),
        lax.psum(d_b_in.astype(jnp.bfloat16), "dp").astype(jnp.float32),
        lax.psum(d_w_out.astype(jnp.bfloat16), "dp").astype(jnp.float32),
        lax.psum(d_b_out.astype(jnp.bfloat16), "dp").astype(jnp.float32),
    )
    (
        total_g1,
        total_s1,
        total_qkv,
        total_bqv,
        total_wo,
        total_bo,
        total_g2,
        total_s2,
        total_router,
        total_win,
        total_bin,
        total_wout,
        total_bout,
    ) = totals
    return (
        output_rows,
        d_tokens,
        total_g1,
        total_s1,
        total_qkv,
        total_bqv,
        total_wo,
        total_bo,
        total_g2,
        total_s2,
        total_router,
        total_win,
        total_bin,
        total_wout,
        total_bout,
    )


def solution(mesh):
    return jax.shard_map(
        shards,
        mesh=mesh,
        in_specs=(
            P(("dp", "fsdp"), None),
            P(("dp", "fsdp"), None),
            P(("dp", "fsdp")),
            P(("dp", "fsdp")),
            P(("dp", "fsdp"), None),
            P(("dp", "fsdp"), None),
            P("fsdp"),
            P("fsdp"),
            P("fsdp", None),
            P("fsdp"),
            P("fsdp", None),
            P("fsdp"),
            P("fsdp"),
            P("fsdp"),
            P("fsdp", None),
            P("fsdp", None, None),
            P("fsdp", None),
            P("fsdp", None, None),
            P("fsdp", None),
        ),
        out_specs=(
            P(("dp", "fsdp"), None),
            P(("dp", "fsdp"), None),
            P("fsdp"),
            P("fsdp"),
            P("fsdp", None),
            P("fsdp"),
            P("fsdp", None),
            P("fsdp"),
            P("fsdp"),
            P("fsdp"),
            P("fsdp", None),
            P("fsdp", None, None),
            P("fsdp", None),
            P("fsdp", None, None),
            P("fsdp", None),
        ),
        check_vma=False,
    )
```

profile of v0, /device:TPU:1, one launch (start us, length us, event | category | flops | bytes accessed | tf_op | source)
XLA Modules:
  0.0 732.9 jit_solution(6091487176791436188)
XLA Ops:
  10.3 4.1 scatter_custom_fusion
  14.4 4.4 gather_fusion
  31.9 19.2 %all-reduce.15 = (bf16[512]{0:T(512)(128)(2,1)S(1)}, bf16[512]{0:T(512)(128)(2,1)S(1)}, bf16[512]{0:T(512)(128)(2,1)S(1)}, bf16[512]{0:T(512)(128)(2,1)S(1)}, bf16[512]{0:T(512)(128)(2,1)S(1)}) all-reduce(bf16[512]{0:T(512)(128)(2,1)S(1)} %dynamic-update-slice.1, ...), channel_id=1, replica_groups=mesh['dp'=4,'fsdp'=8] {'fsdp'}, use_global_device_ids=true, to_apply=%add.4 | all-reduce | flops 2560 | bytes 10240
  56.9 12.7 %all-gather = bf16[8,1,128]{2,1,0:T(2,128)(2,1)S(1)} all-gather(bf16[1,1,128]{2,1,0:T(2,128)(2,1)S(1)} %bitcast.266), channel_id=1, replica_groups=mesh['dp'=4,'fsdp'=8] {'fsdp'}, dimensions={0}, use_global_device_ids=true | all-gather | bytes 2304 | tf_op jit(solution)/shard_map/all_gather | solution.py:159
  70.3 27.4 %all_gather.36 = bf16[512,512]{1,0:T(8,128)(2,1)} all-gather(bf16[64,512]{1,0:T(8,128)(2,1)S(1)} %copy-done.37), channel_id=1, replica_groups=mesh['dp'=4,'fsdp'=8] {'fsdp'}, dimensions={0}, use_global_device_ids=true | all-gather | bytes 589824 | tf_op jit(solution)/shard_map/all_gather | solution.py:160
  108.6 9.2 %fusion = (f32[8,720]{1,0:T(8,128)S(1)}, f32[8,720,720]{1,2,0:T(8,128)}) fusion(pred[720,720]{0,1:T(8,128)(4,1)S(1)} %fusion.38, bf16[720,8,64]{0,2,1:T(8,128)(2,1)} %bitcast.245, bf16[720,8,64]{0,2,1:T(8,128)(2,1)S(1)} %bitcast.243), kind=kOutput, calls=%fused_computation.14 | convolution fusion | flops 543277440 | bytes 18604800 | tf_op jit(solution)/shard_map/while/body/eval_jaxpr/qhd,khd->hqk/dot_general | solution.py:45
  117.8 9.7 %exponential_reduce_fusion = f32[8,720]{1,0:T(8,128)S(1)} fusion(f32[8,720,720]{1,2,0:T(8,128)} %get-tuple-element.122, f32[8,720]{1,0:T(8,128)S(1)} %get-tuple-element.121, pred[720,720]{0,1:T(8,128)(4,1)S(1)} %fusion.38), kind=kLoop, calls=%fused_computation.12 | loop fusion | flops 16583040 | bytes 17153280 | tf_op jit(solution)/shard_map/while/body/eval_jaxpr/reduce_sum | solution.py:60
  127.6 10.8 %convolution_convert_fusion.2 = bf16[8,64,720]{2,1,0:T(8,128)(2,1)S(1)} fusion(bf16[720,8,64]{0,2,1:T(8,128)(2,1)} %bitcast.247, f32[8,720,720]{1,2,0:T(8,128)} %get-tuple-element.122, f32[8,720]{1,0:T(8,128)S(1)} %log_add_fusion, pred[720,720]{0,1:T(8,128)(4,1)S(1)} %fusion.38), kind=kOutput, calls=%fused_computation.110 | convolution fusion | flops 547799040 | bytes 18604800 | tf_op jit(solution)/shard_map/while/body/eval_jaxpr/hqk,khd->qhd/dot_general | solution.py:62
  142.8 4.8 reshape.451
  147.6 9.7 %scatter_custom_fusion.1 = bf16[1513,512]{1,0:T(8,128)(2,1)} fusion(s32[1440]{0:T(1024)S(1)} %fusion.80, bf16[1440,512]{1,0:T(8,128)(2,1)} %reshape.451, bf16[]{:T(256)} %constant.52.clone.1), kind=kCustom, calls=%fused_computation.120 | custom fusion | bytes 1549824 | tf_op jit(solution)/shard_map/scatter | solution.py:232
  159.9 3.0 reshape.387
  163.0 4.3 all-to-all-start
  167.3 45.5 %all-gather.1 = bf16[8,64,8]{1,2,0:T(8,128)(2,1)S(1)} all-gather(bf16[1,64,8]{1,2,0:T(8,128)(2,1)S(1)} %bitcast.264), channel_id=1, replica_groups=mesh['dp'=4,'fsdp'=8] {'fsdp'}, dimensions={0}, use_global_device_ids=true | all-gather | bytes 9216 | tf_op jit(solution)/shard_map/all_gather | solution.py:164
  212.9 3.5 mul.253
  216.4 5.0 mul.254
  222.8 13.7 %scatter_custom_fusion.2 = bf16[1513,512]{1,0:T(8,128)(2,1)} fusion(s32[1440]{0:T(1024)S(1)} %fusion.80, f32[1440,512]{1,0:T(8,128)} %mul.254, f32[1440]{0:T(1024)S(1)} %mul.251, bf16[]{:T(256)} %constant.52.clone.1), kind=kCustom, calls=%fused_computation.95 | custom fusion | flops 1474560 | bytes 4506626 | tf_op jit(solution)/shard_map/scatter | solution.py:257
  242.1 4.5 all-to-all-start.2
  246.6 5.5 fusion.43
  252.2 4.6 copy-done.60
  256.7 28.3 %fusion.56 = bf16[8,189,512]{2,1,0:T(8,128)(2,1)} fusion(f32[512]{0:T(512)S(1)} %bitcast.265, bf16[1,2048,512]{2,1,0:T(8,128)(2,1)S(1)} %copy-done, f32[8,189,2048]{2,1,0:T(8,128)S(1)} %fusion.43, f32[2048]{0:T(1024)S(1)} %bitcast.261), kind=kOutput, calls=%fused_computation.83 | convolution fusion | flops 3376816128 | bytes 16041984 | tf_op jit(solution)/shard_map/secf,efd->secd/dot_general | solution.py:238
  285.0 5.9 all-to-all-start.1
  290.9 34.4 %fusion.102 = (bf16[2048]{0:T(1024)(128)(2,1)}, bf16[8,1,189,2048]{3,2,0,1:T(8,128)(2,1)S(1)}) fusion(bf16[8,189,512]{2,1,0:T(8,128)(2,1)} %all-to-all-done.2, bf16[1,2048,512]{2,1,0:T(8,128)(2,1)S(1)} %copy-done, f32[2048]{0:T(1024)S(1)} %bitcast.262, f32[8,189,2048]{2,1,0:T(8,128)} %copy-done.60), kind=kOutput, calls=%fused_computation.181 | convolution fusion | flops 3400038400 | bytes 22237184 | tf_op jit(solution)/shard_map/secd,efd->secf/dot_general | solution.py:275
  328.0 4.6 fusion.51
  332.6 5.4 all-to-all-start.3
  339.6 3.0 reshape.392
  344.2 5.4 gather_fusion.3
  349.6 4.6 reshape.469
  354.1 8.5 %multiply_reduce_fusion.1 = (f32[720,2]{1,0:T(8,128)S(1)}, f32[720,512]{1,0:T(8,128)}) fusion(f32[720,2,512]{2,1,0:T(2,128)} %reshape.469, f32[720,512]{1,0:T(8,128)} %convert_element_type.291, f32[720,2]{1,0:T(8,128)S(1)} %copy-done.17), kind=kLoop, calls=%fused_computation.58 | loop fusion | flops 2579040 | bytes 5909760 | tf_op jit(solution)/shard_map/reduce_sum | solution.py:252
  362.9 7.5 %all-to-all-done.3 = bf16[8,189,512]{2,1,0:T(8,128)(2,1)} async-done(((bf16[8,189,512]{2,1,0:T(8,128)(2,1)}), bf16[8,189,512]{2,1,0:T(8,128)(2,1)}, u32[]{:S(2)}, u32[]{:S(2)}) %all-to-all-start.3) | async-done | bytes 1548320 | tf_op jit(solution)/shard_map/all_to_all | solution.py:284
  374.9 5.4 gather_fusion.4
  380.3 4.8 reshape.470
  385.1 5.4 reduce_sum.271
  390.5 3.4 multiply_reduce_fusion.3
  395.9 3.0 convolution_convert_fusion.4
  401.8 9.4 %fusion.100 = (bf16[8,64]{1,0:T(8,128)(2,1)S(1)}, bf16[8,64,720]{2,1,0:T(8,128)(2,1)}) fusion(bf16[720,8,64]{0,2,1:T(8,128)(2,1)S(1)} %bitcast.249, f32[8,720,720]{1,2,0:T(8,128)} %get-tuple-element.122, f32[8,720]{1,0:T(8,128)S(1)} %copy-done.28, pred[720,720]{0,1:T(8,128)(4,1)S(1)} %copy-done.6), kind=kOutput, calls=%fused_computation.179 | convolution fusion | flops 548167168 | bytes 18605824 | tf_op jit(solution)/shard_map/while/body/eval_jaxpr/hqk,qhd->khd/dot_general | solution.py:94
  411.3 12.5 %multiply_reduce_fusion = (f32[8,720]{1,0:T(8,128)S(1)}, f32[8,720,720]{1,2,0:T(8,128)}) fusion(f32[8,720,720]{1,2,0:T(8,128)} %get-tuple-element.122, f32[8,720]{1,0:T(8,128)S(1)} %copy-done.28, pred[720,720]{0,1:T(8,128)(4,1)S(1)} %copy-done.6, bf16[720,8,64]{0,2,1:T(8,128)(2,1)S(1)} %bitcast.250, bf16[720,8,64]{0,2,1:T(8,128)(2,1)S(1)} %bitcast.248), kind=kOutput, calls=%fused_computation.10 | convolution fusion | flops 551571840 | bytes 35216640 | tf_op jit(solution)/shard_map/while/body/eval_jaxpr/qhd,khd->hqk/dot_general | solution.py:73
  423.8 13.1 %multiply_convert_fusion = bf16[8,720,720]{1,2,0:T(8,128)(2,1)S(1)} fusion(f32[8,720,720]{1,2,0:T(8,128)} %get-tuple-element.129, f32[8,720,720]{1,2,0:T(8,128)} %get-tuple-element.122, f32[8,720]{1,0:T(8,128)S(1)} %get-tuple-element.128, f32[8,720]{1,0:T(8,128)S(1)} %copy-done.28, pred[720,720]{0,1:T(8,128)(4,1)S(1)} %copy-done.6), kind=kLoop, calls=%fused_computation.9 | loop fusion | flops 24883200 | bytes 42036480 | tf_op jit(solution)/shard_map/while/body/eval_jaxpr/convert_element_type | solution.py:79
  444.5 33.0 %fusion.36 = bf16[1,2048,512]{2,1,0:T(8,128)(2,1)} fusion(bf16[8,189,512]{2,1,0:T(8,128)(2,1)} %all-to-all-done.2, f32[8,189,2048]{2,1,0:T(8,128)} %copy-done.60, f32[2048]{0:T(1024)S(1)} %bitcast.263), kind=kOutput, calls=%fused_computation.62 | convolution fusion | flops 3376316416 | bytes 16039936 | tf_op jit(solution)/shard_map/secf,secd->efd/dot_general | solution.py:268
  478.8 8.1 %fusion.33 = bf16[1,512,2048]{2,1,0:T(8,128)(2,1)} fusion(bf16[8,189,512]{2,1,0:T(8,128)(2,1)} %all-to-all-done, bf16[8,1,189,2048]{3,2,0,1:T(8,128)(2,1)} %copy-done.61), kind=kOutput, calls=%fused_computation.61 | convolution fusion | flops 3171942400 | bytes 9838592 | tf_op jit(solution)/shard_map/secd,secf->edf/dot_general | solution.py:277
  489.1 68.4 %reduce-scatter.6.cloned.1.call-done = bf16[64,1536]{1,0:T(8,128)(2,1)} async-done(((bf16[512,1536]{1,0:T(8,128)(2,1)}), bf16[64,1536]{1,0:T(8,128)(2,1)}) %reduce-scatter.6.cloned.1.call-update) | async-done | bytes 196624 | tf_op jit(solution)/shard_map/reduce_scatter | solution.py:345
  560.7 5.1 fusion.65
  565.9 15.5 %all-reduce.14 = (bf16[512]{0:T(512)(128)(2,1)S(1)}, bf16[512]{0:T(512)(128)(2,1)S(1)}, bf16[1024]{0:T(1024)(128)(2,1)S(1)}, bf16[512]{0:T(512)(128)(2,1)S(1)}, ...) all-reduce(bf16[512]{0:T(512)(128)(2,1)S(1)} %get-tuple-element.76,, ...), channel_id=2, replica_groups=mesh['dp'=4,'fsdp'=8] {'fsdp'}, use_global_device_ids=true, to_apply=%region_26.27.clone | all-reduce | flops 3584 | bytes 14336
  581.8 3.5 fusion.64
  585.3 34.9 %reduce-scatter.10.cloned.1.call-done = bf16[64,8]{1,0:T(8,128)(2,1)} async-done(((bf16[512,8]{1,0:T(8,128)(2,1)}), bf16[64,8]{1,0:T(8,128)(2,1)}) %reduce-scatter.10.cloned.1.call-update) | async-done | bytes 1040
  620.9 11.7 %all-reduce.16 = (bf16[64]{0:T(256)(128)(2,1)S(1)}, bf16[64]{0:T(256)(128)(2,1)S(1)}, bf16[128]{0:T(256)(128)(2,1)S(1)}, bf16[64]{0:T(256)(128)(2,1)S(1)}, bf16[...) all-reduce(bf16[64]{0:T(256)(128)(2,1)S(1)} %dynamic-slice.13, ...), channel_id=1, replica_groups=mesh['dp'=4,'fsdp'=8] {'dp'}, use_global_device_ids=true, to_apply=%region_27.28 | all-reduce | flops 3520 | bytes 14080 | tf_op jit(solution)/shard_map/psum | solution.py:379
  637.5 76.8 %all-reduce.20.cloned.1.call-done = (bf16[64,1536]{1,0:T(8,128)(2,1)}, bf16[64,512]{1,0:T(8,128)(2,1)}, bf16[1,512,2048]{2,1,0:T(8,128)(2,1)}, bf16[1,2048,512]{2,1,0:T(8,128)(2,1)}) async-done(((bf16[64,1536]{1,0:T(8,128)(2,1)}, bf16[64,512]{1,0:T(8,128)(2,1)}, bf16[1,512,2048]{2,1,0:T(8,128)(2,1)}, bf16[1,2048,512]{2,1,0:T(8,128)(2,1)}), (bf16[64,1536]{1,0:T(8,128)(2,1)}, bf16[64,512]{1,0:T(8,128)(2,1)}, ...) | async-done | bytes 4456464 | tf_op jit(solution)/shard_map/psum | solution.py:381
  717.6 4.1 convert_element_type.329
  721.7 4.2 convert_element_type.333
  (263 shorter events, 84.1 us)
Async XLA Ops:
  7.2 249.5 %copy-start = (bf16[1,2048,512]{2,1,0:T(8,128)(2,1)S(1)}, bf16[1,2048,512]{2,1,0:T(8,128)(2,1)}, u32[]{:S(2)}) copy-start(bf16[1,2048,512]{2,1,0:T(8,128)(2,1)} %param.36) | copy-start | bytes 6291460
  7.2 63.0 %copy-start.2 = (s32[720]{0:T(1024)S(1)}, s32[720]{0:T(1024)}, u32[]{:S(2)}) copy-start(s32[720]{0:T(1024)} %param.22) | copy-start | bytes 8644
  7.2 49.7 %copy-start.57 = (bf16[128]{0:T(256)(128)(2,1)S(1)}, bf16[128]{0:T(256)(128)(2,1)}, u32[]{:S(2)}) copy-start(bf16[128]{0:T(256)(128)(2,1)} %param.28) | copy-start | bytes 772
  7.2 62.4 %copy-start.12 = (bf16[720,512]{1,0:T(8,128)(2,1)S(1)}, bf16[720,512]{1,0:T(8,128)(2,1)}, u32[]{:S(2)}) copy-start(bf16[720,512]{1,0:T(8,128)(2,1)} %param.19) | copy-start | bytes 2211844
  7.2 63.1 %copy-start.37 = (bf16[64,512]{1,0:T(8,128)(2,1)S(1)}, bf16[64,512]{1,0:T(8,128)(2,1)}, u32[]{:S(2)}) copy-start(bf16[64,512]{1,0:T(8,128)(2,1)} %param.29) | copy-start | bytes 196612
  7.2 90.4 %copy-start.46 = (s32[720]{0:T(1024)S(1)}, s32[720]{0:T(1024)}, u32[]{:S(2)}) copy-start(s32[720]{0:T(1024)} %param.21) | copy-start | bytes 8644
  7.3 90.9 %all-gather.4.cloned.1.call-start = ((), (), s32[]{:S(2)}) async-start(), calls=%async_computation.7 | async-start | bytes 1769472 | tf_op jit(solution)/shard_map/all_gather | solution.py:158
  51.1 52.3 %copy-start.54 = (f32[512]{0:T(512)}, f32[512]{0:T(512)S(1)}, u32[]{:S(2)}) copy-start(f32[512]{0:T(512)S(1)} %convert_element_type.269) | copy-start | bytes 6148
  51.1 52.3 %copy-start.49 = (f32[512]{0:T(512)}, f32[512]{0:T(512)S(1)}, u32[]{:S(2)}) copy-start(f32[512]{0:T(512)S(1)} %convert_element_type.268) | copy-start | bytes 6148
  51.2 88.4 %copy-start.44 = (f32[512]{0:T(512)}, f32[512]{0:T(512)S(1)}, u32[]{:S(2)}) copy-start(f32[512]{0:T(512)S(1)} %convert_element_type.279) | copy-start | bytes 6148
  69.8 33.6 %copy-start.42 = (f32[720]{0:T(1024)}, f32[720]{0:T(1024)S(1)}, u32[]{:S(2)}) copy-start(f32[720]{0:T(1024)S(1)} %broadcast_multiply_fusion.6) | copy-start | bytes 8644
  70.3 33.1 %copy-start.47 = (f32[720]{0:T(1024)}, f32[720]{0:T(1024)S(1)}, u32[]{:S(2)}) copy-start(f32[720]{0:T(1024)S(1)} %add_rsqrt_fusion.1) | copy-start | bytes 8644
  98.1 29.5 %copy-start.5 = (pred[720,720]{0,1:T(8,128)(4,1)}, pred[720,720]{0,1:T(8,128)(4,1)S(1)}, u32[]{:S(2)}) copy-start(pred[720,720]{0,1:T(8,128)(4,1)S(1)} %fusion.38) | copy-start | bytes 1555204
  106.0 21.5 %copy-start.9 = (bf16[720,512]{0,1:T(8,128)(2,1)}, bf16[720,512]{0,1:T(8,128)(2,1)S(1)}, u32[]{:S(2)}) copy-start(bf16[720,512]{0,1:T(8,128)(2,1)S(1)} %copy.102) | copy-start | bytes 2211844
  138.5 28.8 %copy-start.56 = (bf16[1,512]{1,0:T(2,128)(2,1)S(1)}, bf16[1,512]{1,0:T(2,128)(2,1)}, u32[]{:S(2)}) copy-start(bf16[1,512]{1,0:T(2,128)(2,1)} %param.37) | copy-start | bytes 3076
  138.5 28.8 %copy-start.51 = (bf16[1,2048]{1,0:T(2,128)(2,1)S(1)}, bf16[1,2048]{1,0:T(2,128)(2,1)}, u32[]{:S(2)}) copy-start(bf16[1,2048]{1,0:T(2,128)(2,1)} %param.35) | copy-start | bytes 12292
  138.5 28.8 %copy-start.53 = (bf16[64,8]{0,1:T(8,128)(2,1)S(1)}, bf16[64,8]{0,1:T(8,128)(2,1)}, u32[]{:S(2)}) copy-start(bf16[64,8]{0,1:T(8,128)(2,1)} %param.33) | copy-start | bytes 3076
  140.9 80.5 %copy-start.7 = (bf16[720,512]{1,0:T(8,128)(2,1)}, bf16[720,512]{1,0:T(8,128)(2,1)S(1)}, u32[]{:S(2)}) copy-start(bf16[720,512]{1,0:T(8,128)(2,1)S(1)} %add_convert_fusion.1) | copy-start | bytes 2211844
  142.8 79.6 %copy-start.33 = (s32[720,2]{0,1:T(2,128)S(1)}, s32[720,2]{0,1:T(2,128)}, u32[]{:S(2)}) copy-start(s32[720,2]{0,1:T(2,128)} %param.23) | copy-start | bytes 17284
  163.0 79.2 %all-to-all-start = ((bf16[8,189,512]{2,1,0:T(8,128)(2,1)}), bf16[8,189,512]{2,1,0:T(8,128)(2,1)}, u32[]{:S(2)}, u32[]{:S(2)}) async-start(bf16[8,189,512]{2,1,0:T(8,128)(2,1)} %reshape.387), calls=%async_computation | async-start | bytes 3145728 | tf_op jit(solution)/shard_map/all_to_all | solution.py:235
  212.9 39.2 %copy-start.35 = (bf16[512,8]{0,1:T(8,128)(2,1)}, bf16[512,8]{0,1:T(8,128)(2,1)S(1)}, u32[]{:S(2)}) copy-start(bf16[512,8]{0,1:T(8,128)(2,1)S(1)} %reshape.489) | copy-start | bytes 24580
  222.6 29.6 %copy-start.16 = (f32[720,2]{1,0:T(8,128)}, f32[720,2]{1,0:T(8,128)S(1)}, u32[]{:S(2)}) copy-start(f32[720,2]{1,0:T(8,128)S(1)} %copy.105) | copy-start | bytes 17284
  242.1 42.9 %all-to-all-start.2 = ((bf16[8,189,512]{2,1,0:T(8,128)(2,1)}), bf16[8,189,512]{2,1,0:T(8,128)(2,1)}, u32[]{:S(2)}, u32[]{:S(2)}) async-start(bf16[8,189,512]{2,1,0:T(8,128)(2,1)} %reshape.393), calls=%async_computation.2 | async-start | bytes 3145728 | tf_op jit(solution)/shard_map/all_to_all | solution.py:262
  285.0 47.6 %all-to-all-start.1 = ((bf16[8,189,512]{2,1,0:T(8,128)(2,1)}), bf16[8,189,512]{2,1,0:T(8,128)(2,1)}, u32[]{:S(2)}, u32[]{:S(2)}) async-start(bf16[8,189,512]{2,1,0:T(8,128)(2,1)} %fusion.56), calls=%async_computation.1 | async-start | bytes 3145728 | tf_op jit(solution)/shard_map/all_to_all | solution.py:242
  290.9 37.1 %copy-start.58 = (bf16[1,512,2048]{2,1,0:T(8,128)(2,1)S(1)}, bf16[1,512,2048]{2,1,0:T(8,128)(2,1)}, u32[]{:S(2)}) copy-start(bf16[1,512,2048]{2,1,0:T(8,128)(2,1)} %param.34) | copy-start | bytes 6291460
  332.6 37.8 %all-to-all-start.3 = ((bf16[8,189,512]{2,1,0:T(8,128)(2,1)}), bf16[8,189,512]{2,1,0:T(8,128)(2,1)}, u32[]{:S(2)}, u32[]{:S(2)}) async-start(bf16[8,189,512]{2,1,0:T(8,128)(2,1)} %fusion.51), calls=%async_computation.3 | async-start | bytes 3145728 | tf_op jit(solution)/shard_map/all_to_all | solution.py:284
  338.0 151.1 %reduce-scatter.8.cloned.1.call-start = ((), (), s32[]{:S(2)}) async-start(), calls=%async_computation.9 | async-start | bytes 589824 | tf_op jit(solution)/shard_map/reduce_scatter | solution.py:351
  339.4 14.7 %copy-start.17 = (f32[720,2]{1,0:T(8,128)S(1)}, f32[720,2]{1,0:T(8,128)}, u32[]{:S(2)}) copy-start(f32[720,2]{1,0:T(8,128)} %copy-done.16) | copy-start | bytes 17284
  344.1 18.6 %copy-start.34 = (s32[720,2]{0,1:T(2,128)S(1)}, s32[720,2]{0,1:T(2,128)}, u32[]{:S(2)}) copy-start(s32[720,2]{0,1:T(2,128)} %param.23) | copy-start | bytes 17284
  344.2 18.6 %copy-start.26 = (f32[720,8]{0,1:T(8,128)S(1)}, f32[720,8]{0,1:T(8,128)}, u32[]{:S(2)}) copy-start(f32[720,8]{0,1:T(8,128)} %copy-done.25) | copy-start | bytes 69124
  344.2 18.6 %copy-start.30 = (f32[720]{0:T(1024)S(1)}, f32[720]{0:T(1024)}, u32[]{:S(2)}) copy-start(f32[720]{0:T(1024)} %copy-done.29) | copy-start | bytes 8644
  344.2 18.6 %copy-start.39 = (f32[720]{0:T(1024)S(1)}, f32[720]{0:T(1024)}, u32[]{:S(2)}) copy-start(f32[720]{0:T(1024)} %copy-done.38) | copy-start | bytes 8644
  373.4 17.1 %copy-start.32 = (f32[720]{0:T(1024)S(1)}, f32[720]{0:T(1024)}, u32[]{:S(2)}) copy-start(f32[720]{0:T(1024)} %copy-done.31) | copy-start | bytes 8644
  373.4 17.2 %copy-start.36 = (bf16[512,8]{0,1:T(8,128)(2,1)S(1)}, bf16[512,8]{0,1:T(8,128)(2,1)}, u32[]{:S(2)}) copy-start(bf16[512,8]{0,1:T(8,128)(2,1)} %copy-done.35) | copy-start | bytes 24580
  373.4 17.2 %copy-start.41 = (f32[720]{0:T(1024)S(1)}, f32[720]{0:T(1024)}, u32[]{:S(2)}) copy-start(f32[720]{0:T(1024)} %copy-done.40) | copy-start | bytes 8644
  373.4 17.2 %copy-start.45 = (f32[512]{0:T(512)S(1)}, f32[512]{0:T(512)}, u32[]{:S(2)}) copy-start(f32[512]{0:T(512)} %copy-done.44) | copy-start | bytes 6148
  380.3 18.7 %copy-start.20 = (bf16[512,512]{1,0:T(8,128)(2,1)S(1)}, bf16[512,512]{1,0:T(8,128)(2,1)}, u32[]{:S(2)}) copy-start(bf16[512,512]{1,0:T(8,128)(2,1)} %all_gather.36) | copy-start | bytes 1572868
  385.1 16.7 %copy-start.6 = (pred[720,720]{0,1:T(8,128)(4,1)S(1)}, pred[720,720]{0,1:T(8,128)(4,1)}, u32[]{:S(2)}) copy-start(pred[720,720]{0,1:T(8,128)(4,1)} %copy-done.5) | copy-start | bytes 1555204
  385.1 16.7 %copy-start.28 = (f32[8,720]{1,0:T(8,128)S(1)}, f32[8,720]{1,0:T(8,128)}, u32[]{:S(2)}) copy-start(f32[8,720]{1,0:T(8,128)} %copy-done.27) | copy-start | bytes 69124
  395.9 15.4 %copy-start.3 = (f32[720,512]{1,0:T(8,128)}, f32[720,512]{1,0:T(8,128)S(1)}, u32[]{:S(2)}) copy-start(f32[720,512]{1,0:T(8,128)S(1)} %get-tuple-element.109) | copy-start | bytes 4423684
  423.8 133.8 %reduce-scatter.6.cloned.1.call-start = ((), (), s32[]{:S(2)}) async-start(), calls=%async_computation.8 | async-start | bytes 1769472 | tf_op jit(solution)/shard_map/reduce_scatter | solution.py:345
  423.8 15.8 %copy-start.10 = (bf16[720,512]{0,1:T(8,128)(2,1)S(1)}, bf16[720,512]{0,1:T(8,128)(2,1)}, u32[]{:S(2)}) copy-start(bf16[720,512]{0,1:T(8,128)(2,1)} %copy-done.9) | copy-start | bytes 2211844
  441.4 36.0 %copy-start.22 = (bf16[8,64,720]{2,1,0:T(8,128)(2,1)}, bf16[8,64,720]{2,1,0:T(8,128)(2,1)S(1)}, u32[]{:S(2)}) copy-start(bf16[8,64,720]{2,1,0:T(8,128)(2,1)S(1)} %get-tuple-element.134) | copy-start | bytes 2211844
  444.4 33.0 %copy-start.8 = (bf16[720,512]{1,0:T(8,128)(2,1)S(1)}, bf16[720,512]{1,0:T(8,128)(2,1)}, u32[]{:S(2)}) copy-start(bf16[720,512]{1,0:T(8,128)(2,1)} %copy-done.7) | copy-start | bytes 2211844
  444.4 175.7 %reduce-scatter.10.cloned.1.call-start = ((), (), s32[]{:S(2)}) async-start(), calls=%async_computation.10 | async-start | bytes 147456
  477.5 83.1 %copy-start.52 = (bf16[2048]{0:T(1024)(128)(2,1)S(1)}, bf16[2048]{0:T(1024)(128)(2,1)}, u32[]{:S(2)}) copy-start(bf16[2048]{0:T(1024)(128)(2,1)} %get-tuple-element.135) | copy-start | bytes 12292
  478.5 235.8 %all-reduce.20.cloned.1.call-start = ((), (), s32[]{:S(2)}) async-start(), calls=%async_computation.11 | async-start | bytes 8912896 | tf_op jit(solution)/shard_map/psum | solution.py:381
  560.7 165.2 %copy-start.1 = (bf16[1,2048,512]{2,1,0:T(8,128)(2,1)S(1)}, bf16[1,2048,512]{2,1,0:T(8,128)(2,1)}, u32[]{:S(2)}) copy-start(bf16[1,2048,512]{2,1,0:T(8,128)(2,1)} %param.36) | copy-start | bytes 6291460
  (23 other events, 120.8 us)
Sparse Core Ops, SparseCore 0:
  10.3 46.0 all-gather.3
  423.9 65.1 reduce-scatter.7
  492.9 64.5 reduce-scatter.5
  561.3 58.8 reduce-scatter.9
  623.2 91.1 all-reduce.19
where the time goes:
time: 742 us; the launch traced here: 733 us
  waiting for transfers between devices  191 us (26%)
  matrix products  180 us (24%)
  blocking collectives  132 us (18%)
  local copies, waits for them, and re-layouts  108 us (15%)
  other arithmetic  84.5 us (11%)
  starting transfers between devices  20.5 us (3%)
  between operations  17.3 us (2%)
    psum x1, waiting for transfers between devices, shards(): lax.psum(share_qkv.astype(jnp.bfloat16), 'dp').astype(jnp.float32)  76.8 us
    reduce_scatter x1, waiting for transfers between devices, shards(): lax.psum_scatter(d_w_qkv.astype(jnp.bfloat16), 'fsdp', scatter_dimension=...  68.4 us
    all_gather x1, blocking collectives, shards(): lax.all_gather(w_router, 'fsdp', axis=0, tiled=True)  45.5 us
    unnamed x6, waiting for transfers between devices  35.6 us
    unnamed x2, blocking collectives  34.7 us
    dot_general x1, matrix products, shards(): jnp.einsum('secd,efd->secf', d_grouped, w_out, preferred_element_type=jnp...  34.4 us
    dot_general x1, matrix products, shards(): jnp.einsum('secf,secd->efd', activation.astype(jnp.bfloat16), d_grouped,...  33 us
    dot_general x1, matrix products, shards(): jnp.einsum('secf,efd->secd', hidden, w_out, preferred_element_type=jnp.fl...  28.3 us
  transfers between devices with their start and end apart: 9, of which 5 were waited for; matrix products, arithmetic and copies ran while one was open for 32% of the time, Pallas kernels for 0%

commit v1 on v0

v1 whole, which is shorter than its diff:
```python
import functools

import jax
import jax.numpy as jnp
from jax import lax
from jax.experimental import pallas as pl
from jax.experimental.pallas import tpu as pltpu
from jax.sharding import PartitionSpec as P

MESH = pl.DeviceIdType.MESH
BF16 = jnp.bfloat16
F32 = jnp.float32
SLOTS = 720
WIDTH = 512
PAIRS = 4
EPS = 1e-06
WINDOWS = ((0, 384), (96, 624), (336, 720))
QBLK = 240
KWIN = 528
ROWBLK = 240


def nt(left, right):
    return lax.dot_general(left, right, (((1,), (1,)), ((), ())), preferred_element_type=F32)


def tn(left, right):
    return lax.dot_general(left, right, (((0,), (0,)), ((), ())), preferred_element_type=F32)


def nn(left, right):
    return jnp.dot(left, right, preferred_element_type=F32)


def normalize(value):
    centred = value - jnp.mean(value, axis=-1, keepdims=True)
    inv_std = lax.rsqrt(jnp.mean(centred * centred, axis=-1, keepdims=True) + EPS)
    return centred * inv_std, inv_std


def aligned(index, size):
    return pl.ds(pl.multiple_of(index * size, size), size)


class Place:
    def __init__(self, n_f, n_d):
        self.n_f, self.n_d, self.n_x = n_f, n_d, n_d // 2
        self.me = lax.axis_index("fsdp")
        self.d = lax.axis_index("dp")
        self.x = lax.div(self.d, 2)
        self.core = lax.rem(self.d, 2)

    def ahead(self, k):
        return lax.rem(self.me + k, self.n_f)

    def fsdp_peer(self, k):
        return (self.d, self.ahead(k))

    def x_index(self, i):
        return lax.rem(self.x + i, self.n_x)

    def x_peer(self, i):
        return (self.x_index(i) * 2 + self.core, self.me)

    def partner(self):
        return (self.x * 2 + 1 - self.core, self.me)

    def enter(self):
        bar = pltpu.get_barrier_semaphore()

        def greet(k, _):
            pl.semaphore_signal(bar, inc=1, device_id=self.fsdp_peer(k), device_id_type=MESH)
            return 0

        lax.fori_loop(1, self.n_f, greet, 0)
        for i in range(1, self.n_x):
            pl.semaphore_signal(bar, inc=1, device_id=self.x_peer(i), device_id_type=MESH)
        pl.semaphore_signal(bar, inc=1, device_id=self.partner(), device_id_type=MESH)
        pl.semaphore_wait(bar, self.n_f - 1 + self.n_x - 1 + 1)


def remote(src, dst, send_sem, recv_sem, device):
    return pltpu.make_async_remote_copy(
        src_ref=src,
        dst_ref=dst,
        send_sem=send_sem,
        recv_sem=recv_sem,
        device_id=device,
        device_id_type=MESH,
    )


def loop(low, high, body):
    def step(k, carry):
        body(k)
        return carry

    lax.fori_loop(low, high, step, 0)


def front_kernel(
    n_f,
    n_d,
    experts,
    cap,
    cap_rows,
    tok,
    cot,
    cols,
    rows,
    wsh,
    vsh,
    x_out,
    g_out,
    p_out,
    qkv_out,
    mix_out,
    mid_out,
    w_out,
    v_out,
    place_out,
    wfull,
    vall,
    vecs,
    bias,
    scores,
    probs,
    qkv,
    normed,
    mixed,
    middle,
    routed,
    place,
    send_x,
    send_g,
    s_w,
    r_w,
    s_v,
    r_v,
    s_dx,
    r_dx,
    s_dc,
    r_dc,
    s_g,
    r_g,
    s_x,
    r_x,
    s_own,
    s_out,
):
    at = Place(n_f, n_d)
    shard = WIDTH // n_f
    colw = wsh.shape[1] // n_d

    def cols_of(d):
        return aligned(d, colw)

    def w_piece(owner, d):
        return wfull.at[aligned(owner, shard), cols_of(d)]

    at.enter()

    def send_w(k):
        return remote(
            wsh.at[:, cols_of(at.d)], w_piece(at.me, at.d), s_w.at[k], r_w.at[k], at.fsdp_peer(k)
        )

    def send_v(k):
        return remote(vsh, vall.at[at.me], s_v.at[k], r_v.at[k], at.fsdp_peer(k))

    def share_x(i, k):
        piece = w_piece(at.ahead(n_f - k), at.d)
        return remote(piece, piece, s_dx.at[i - 1, k], r_dx.at[i - 1, k], at.x_peer(i))

    def share_core(i, k):
        piece = w_piece(at.ahead(n_f - k), at.x_index(at.n_x - i) * 2 + at.core)
        return remote(piece, piece, s_dc.at[i, k], r_dc.at[i, k], at.partner())

    loop(1, n_f, lambda k: send_v(k).start())
    loop(1, n_f, lambda k: send_w(k).start())
    wfull[aligned(at.me, shard), :] = wsh[...]
    vall[at.me] = vsh[...]

    lane_e = lax.broadcasted_iota(jnp.int32, (SLOTS, experts), 1)
    sub_e = lax.broadcasted_iota(jnp.int32, (experts, SLOTS), 0)
    live_c, live_r = cols[:, 1:2] > 0, rows[1:2, :] > 0
    pri_c, pri_r = cols[:, 4:5], rows[4:5, :]
    first_c = [jnp.where((cols[:, 2 + k : 3 + k] == lane_e) & live_c, 1.0, 0.0) for k in range(2)]
    first_r = [jnp.where((rows[2 + k : 3 + k, :] == sub_e) & live_r, 1.0, 0.0) for k in range(2)]
    before_c = jnp.where(pri_r < pri_c, 1.0, 0.0).astype(BF16)
    before_r = jnp.where(pri_c < pri_r, 1.0, 0.0).astype(BF16)
    rank_c = [nn(before_c, hot.astype(BF16)) for hot in first_c]
    rank_r = [nn(hot.astype(BF16), before_r) for hot in first_r]
    rank_c[1] = rank_c[1] + jnp.sum(first_c[0], axis=0, keepdims=True)
    rank_r[1] = rank_r[1] + jnp.sum(first_r[0], axis=1, keepdims=True)
    spot_c, spot_r = [], []
    for k in range(2):
        slot = jnp.sum(first_c[k] * rank_c[k], axis=1, keepdims=True)
        spot = cols[:, 2 + k : 3 + k].astype(F32) * cap_rows + slot
        spot_c.append(jnp.where(live_c & (slot < cap), spot, -1.0))
        slot = jnp.sum(first_r[k] * rank_r[k], axis=0, keepdims=True)
        spot = rows[2 + k : 3 + k, :].astype(F32) * cap_rows + slot
        spot_r.append(jnp.where(live_r & (slot < cap), spot, -1.0))
        place[:, k : k + 1] = spot_c[k]
    slot_iota = lax.broadcasted_iota(jnp.int32, (cap_rows, SLOTS), 0)

    def pick(expert):
        mine = (slot_iota + expert * cap_rows).astype(F32)
        return jnp.where((mine == spot_r[0]) | (mine == spot_r[1]), 1.0, 0.0).astype(BF16)

    for b, (low, high) in enumerate(WINDOWS):
        queries = slice(b * QBLK, (b + 1) * QBLK)
        shape = (high - low, QBLK)
        same = cols[low:high, 0:1] == rows[0:1, queries]
        itself = (lax.broadcasted_iota(jnp.int32, shape, 0) + low) == (
            lax.broadcasted_iota(jnp.int32, shape, 1) + b * QBLK
        )
        allowed = same & ((cols[low:high, 1:2] > 0) | itself)
        bias[b, : high - low, :] = jnp.where(allowed, 0.0, -1e30)

    loop(1, n_f, lambda k: send_v(k).wait_recv())
    total = vall[0].astype(F32)
    for owner in range(1, n_f):
        total = total + vall[owner].astype(F32)
    vecs[...] = total

    def first_norm(i):
        block = aligned(i, ROWBLK)
        value, _ = normalize(tok[block, :].astype(F32))
        normed[block, :] = (value * vecs[0:1, :] + vecs[1:2, :]).astype(BF16)

    loop(0, SLOTS // ROWBLK, first_norm)

    def pass_on(k):
        send_w(k).wait_recv()
        for i in range(1, at.n_x):
            share_x(i, k).start()
        share_core(0, k).start()

    loop(1, n_f, pass_on)

    def send_rows(buffer, out, send, recv, k):
        expert = at.ahead(k)
        return remote(
            buffer.at[aligned(expert, cap_rows), :],
            out.at[n_f - k],
            send.at[k],
            recv.at[n_f - k],
            at.fsdp_peer(k),
        )

    def own_rows(buffer, out, sem):
        return pltpu.make_async_copy(buffer.at[aligned(at.me, cap_rows), :], out.at[0], sem)

    def dispatch_g(k):
        expert = at.ahead(k)
        send_g[aligned(expert, cap_rows), :] = nn(pick(expert), cot[...]).astype(BF16)
        send_rows(send_g, g_out, s_g, r_g, k).start()

    loop(1, n_f, dispatch_g)
    send_g[aligned(at.me, cap_rows), :] = nn(pick(at.me), cot[...]).astype(BF16)
    own_rows(send_g, g_out, s_own.at[0]).start()

    for i in range(1, at.n_x):

        def cross(k, i=i):
            piece = w_piece(at.ahead(n_f - k), at.x_index(at.n_x - i) * 2 + at.core)
            remote(piece, piece, s_dx.at[i - 1, k], r_dx.at[i - 1, k], at.x_peer(i)).wait_recv()
            share_core(i, k).start()

        loop(1, n_f, cross)
    for i in range(at.n_x):

        def arrive(k, i=i):
            piece = w_piece(at.ahead(n_f - k), at.x_index(at.n_x - i) * 2 + 1 - at.core)
            remote(piece, piece, s_dc.at[i, k], r_dc.at[i, k], at.partner()).wait_recv()

        loop(1, n_f, arrive)
    copies = [
        pltpu.make_async_copy(wfull, w_out, s_out.at[0]),
        pltpu.make_async_copy(vecs, v_out, s_out.at[1]),
        pltpu.make_async_copy(place, place_out, s_out.at[2]),
    ]
    for copy in copies:
        copy.start()

    bias_row = [vecs[2:3, :], jnp.zeros((1, WIDTH), F32), vecs[3:4, :]]
    for part in range(3):
        for half in range(2):
            low = part * WIDTH + half * 256
            out = nn(normed[...], wfull[:, low : low + 256])
            out = out + bias_row[part][:, half * 256 : half * 256 + 256]
            if part == 0:
                out = out * 0.125
            for j in range(2):
                qkv[part * PAIRS + half * 2 + j] = out[:, j * 128 : j * 128 + 128].astype(BF16)
    copies.append(pltpu.make_async_copy(qkv, qkv_out, s_out.at[3]))
    copies[-1].start()

    lane = lax.broadcasted_iota(jnp.int32, (1, 128), 1)
    halves = (lane < 64, lane >= 64)

    def attend(pair):
        for b, (low, high) in enumerate(WINDOWS):
            query = qkv[pair, b * QBLK : (b + 1) * QBLK, :]
            keys = qkv[PAIRS + pair, low:high, :]
            for h in range(2):
                one = jnp.where(halves[h], query, jnp.zeros_like(query))
                scores[b, h, : high - low, :] = nt(keys, one) + bias[b, : high - low, :]
        for b, (low, high) in enumerate(WINDOWS):
            for h in range(2):
                value = scores[b, h, : high - low, :]
                power = jnp.exp(value - jnp.max(value, axis=0, keepdims=True))
                share = 1.0 / jnp.sum(power, axis=0, keepdims=True)
                probs[2 * pair + h, b, : high - low, :] = (power * share).astype(BF16)
        for b, (low, high) in enumerate(WINDOWS):
            values = qkv[2 * PAIRS + pair, low:high, :]
            both = [tn(probs[2 * pair + h, b, : high - low, :], values) for h in range(2)]
            mixed[b * QBLK : (b + 1) * QBLK, aligned(pair, 128)] = jnp.where(
                halves[0], both[0], both[1]
            ).astype(BF16)

    loop(0, PAIRS, attend)
    copies.append(pltpu.make_async_copy(probs, p_out, s_out.at[4]))
    copies[-1].start()
    copies.append(pltpu.make_async_copy(mixed, mix_out, s_out.at[5]))
    copies[-1].start()

    def second_norm(i):
        block = aligned(i, ROWBLK)
        total = nn(mixed[block, :], wfull[:, 3 * WIDTH : 4 * WIDTH])
        total = tok[block, :].astype(F32) + total + vecs[4:5, :]
        middle[block, :] = total
        value, _ = normalize(total)
        routed[block, :] = (value * vecs[5:6, :] + vecs[6:7, :]).astype(BF16)

    loop(0, SLOTS // ROWBLK, second_norm)
    copies.append(pltpu.make_async_copy(middle, mid_out, s_out.at[6]))
    copies[-1].start()

    def dispatch_x(k):
        expert = at.ahead(k)
        send_x[aligned(expert, cap_rows), :] = nn(pick(expert), routed[...]).astype(BF16)
        send_rows(send_x, x_out, s_x, r_x, k).start()

    loop(1, n_f, dispatch_x)
    send_x[aligned(at.me, cap_rows), :] = nn(pick(at.me), routed[...]).astype(BF16)
    own_rows(send_x, x_out, s_own.at[1]).start()

    for copy in copies:
        copy.wait()
    own_rows(send_g, g_out, s_own.at[0]).wait()
    own_rows(send_x, x_out, s_own.at[1]).wait()

    def sent(k):
        send_v(k).wait_send()
        send_w(k).wait_send()
        for i in range(1, at.n_x):
            share_x(i, k).wait_send()
        for i in range(at.n_x):
            share_core(i, k).wait_send()

    loop(1, n_f, sent)
    loop(1, n_f, lambda k: send_rows(send_g, g_out, s_g, r_g, k).wait())
    loop(1, n_f, lambda k: send_rows(send_x, x_out, s_x, r_x, k).wait())


def front(n_f, n_d, experts, cap, cap_rows, tok, cot, cols, rows, wsh, vsh):
    vmem = pl.BlockSpec(memory_space=pltpu.VMEM)
    hbm = pl.BlockSpec(memory_space=pl.ANY)
    n_x = n_d // 2
    vec_rows = vsh.shape[0]
    sds = jax.ShapeDtypeStruct
    dma = pltpu.SemaphoreType.DMA
    return pl.pallas_call(
        functools.partial(front_kernel, n_f, n_d, experts, cap, cap_rows),
        out_shape=(
            sds((n_f, cap_rows, WIDTH), BF16),
            sds((n_f, cap_rows, WIDTH), BF16),
            sds((2 * PAIRS, 3, KWIN, QBLK), BF16),
            sds((3 * PAIRS, SLOTS, 128), BF16),
            sds((SLOTS, WIDTH), BF16),
            sds((SLOTS, WIDTH), F32),
            sds((WIDTH, 4 * WIDTH), BF16),
            sds((vec_rows, WIDTH), F32),
            sds((SLOTS, 2), F32),
        ),
        in_specs=[vmem] * 6,
        out_specs=[hbm] * 9,
        scratch_shapes=[
            pltpu.VMEM((WIDTH, 4 * WIDTH), BF16),
            pltpu.VMEM((n_f, vec_rows, WIDTH), BF16),
            pltpu.VMEM((vec_rows, WIDTH), F32),
            pltpu.VMEM((3, KWIN, QBLK), F32),
            pltpu.VMEM((3, 2, KWIN, QBLK), F32),
            pltpu.VMEM((2 * PAIRS, 3, KWIN, QBLK), BF16),
            pltpu.VMEM((3 * PAIRS, SLOTS, 128), BF16),
            pltpu.VMEM((SLOTS, WIDTH), BF16),
            pltpu.VMEM((SLOTS, WIDTH), BF16),
            pltpu.VMEM((SLOTS, WIDTH), F32),
            pltpu.VMEM((SLOTS, WIDTH), BF16),
            pltpu.VMEM((SLOTS, 2), F32),
            pltpu.VMEM((n_f * cap_rows, WIDTH), BF16),
            pltpu.VMEM((n_f * cap_rows, WIDTH), BF16),
            dma((n_f,)),
            dma((n_f,)),
            dma((n_f,)),
            dma((n_f,)),
            dma((max(n_x - 1, 1), n_f)),
            dma((max(n_x - 1, 1), n_f)),
            dma((n_x, n_f)),
            dma((n_x, n_f)),
            dma((n_f,)),
            dma((n_f,)),
            dma((n_f,)),
            dma((n_f,)),
            dma((2,)),
            dma((7,)),
        ],
        compiler_params=pltpu.CompilerParams(
            collective_id=0, has_side_effects=True, vmem_limit_bytes=48 << 20
        ),
        name="front",
    )(tok, cot, cols, rows, wsh, vsh)


def spread(vector, n_f, me):
    size = vector.shape[-1]
    whole = jnp.tile(vector, (1,) * (vector.ndim - 1) + (n_f,))
    return jnp.where(jnp.arange(size * n_f) // size == me, whole, jnp.zeros_like(whole))


def norm_back(grad_in, normed, inv_std, gain_vec):
    scaled = grad_in * gain_vec
    corrected = (
        scaled
        - jnp.mean(scaled, axis=-1, keepdims=True)
        - normed * jnp.mean(scaled * normed, axis=-1, keepdims=True)
    )
    return (inv_std * corrected, jnp.sum(grad_in * normed, axis=0), jnp.sum(grad_in, axis=0))


def shards(
    tokens,
    cotangent,
    segment_ids,
    pad_mask,
    expert_ids,
    priority,
    ln1_gain,
    ln1_shift,
    w_qkv,
    b_qv,
    w_o,
    b_o,
    ln2_gain,
    ln2_shift,
    w_router,
    w_in,
    b_in,
    w_out,
    b_out,
    n_f,
    n_d,
):
    me = lax.axis_index("fsdp")
    count_tok = tokens.shape[0]
    experts = w_router.shape[1]
    cap = (21 * count_tok + 10 * experts - 1) // (10 * experts)
    cap_rows = -(-cap // 16) * 16
    zero_row = jnp.zeros_like(segment_ids)
    rows = jnp.stack(
        [segment_ids, pad_mask, expert_ids[:, 0], expert_ids[:, 1], priority[0]] + [zero_row] * 3
    )
    cols = rows.T
    wsh = jnp.concatenate([w_qkv, w_o], axis=1)
    whole = functools.partial(spread, n_f=n_f, me=me)
    vec_rows = -(-(8 + experts) // 16) * 16
    vsh = jnp.concatenate(
        [
            whole(ln1_gain)[None],
            whole(ln1_shift)[None],
            whole(b_qv).reshape(2, WIDTH),
            whole(b_o)[None],
            whole(ln2_gain)[None],
            whole(ln2_shift)[None],
            jnp.zeros((1, WIDTH), BF16),
            whole(w_router.T),
            jnp.zeros((vec_rows - 8 - experts, WIDTH), BF16),
        ]
    )
    x_in, g_in, probs, qkv, mixed, middle, wfull, vecs, place = front(
        n_f, n_d, experts, cap, cap_rows, tokens, cotangent, cols, rows, wsh, vsh
    )
    router = vecs[8 : 8 + experts].astype(BF16)
    x = x_in.reshape(-1, WIDTH)
    g = g_in.reshape(-1, WIDTH).astype(F32)
    gates = jax.nn.softmax(nt(x, router), axis=-1)
    hot = (jnp.arange(experts) == me).astype(F32)
    chosen = jnp.sum(gates * hot, axis=-1, keepdims=True)
    pre = nn(x, w_in[0]) + b_in[0].astype(F32)
    act, gelu_back = jax.vjp(functools.partial(jax.nn.gelu, approximate=False), pre)
    act = act.astype(BF16)
    result = nn(act, w_out[0]) + b_out[0].astype(F32)
    d_result = (chosen * g).astype(BF16)
    d_chosen = jnp.sum(g * result, axis=-1, keepdims=True)
    d_logits = (d_chosen * chosen * (hot - gates)).astype(BF16)
    d_pre = gelu_back(nt(d_result, w_out[0]))[0].astype(BF16)
    d_rows = nt(d_pre, w_in[0]) + nn(d_logits, router)
    d_w_in = tn(x, d_pre)
    d_w_out = tn(act, d_result)
    d_b_in = jnp.sum(d_pre.astype(F32), axis=0)
    d_b_out = jnp.sum(d_result.astype(F32), axis=0)
    d_router_t = tn(d_logits, x)

    def back(value):
        value = value.astype(BF16).reshape(n_f, cap_rows, WIDTH)
        value = jnp.roll(value, me, axis=0)
        return lax.all_to_all(value, "fsdp", split_axis=0, concat_axis=0, tiled=True).reshape(
            -1, WIDTH
        )

    table_d = back(d_rows)
    table_o = back(chosen * result)
    lanes = jnp.arange(n_f * cap_rows).astype(F32)[None]
    picks = ((lanes == place[:, 0:1]) | (lanes == place[:, 1:2])).astype(BF16)
    output = (middle + nn(picks, table_o)).astype(BF16)
    d_routed = nn(picks, table_d)
    norm_two, inv_two = normalize(middle)
    grads = cotangent.astype(F32)
    d_mid, d_g2, d_s2 = norm_back(d_routed, norm_two, inv_two, vecs[5:6])
    d_middle = grads + d_mid
    d_attn = d_middle.astype(BF16)
    d_w_o = tn(mixed, d_attn)
    d_b_o = jnp.sum(d_attn.astype(F32), axis=0)
    d_mixed = nt(d_attn, wfull[:, 3 * WIDTH :]).astype(BF16)
    d_parts = [[], [], []]
    for pair in range(PAIRS):
        for h in range(2):
            dq, dk, dv = [], jnp.zeros((SLOTS, 64), F32), jnp.zeros((SLOTS, 64), F32)
            take = slice(h * 64, h * 64 + 64)
            for b, (low, high) in enumerate(WINDOWS):
                qs = slice(b * QBLK, (b + 1) * QBLK)
                p = probs[2 * pair + h, b, : high - low, :]
                do = d_mixed[qs, pair * 128 + h * 64 : pair * 128 + h * 64 + 64]
                dp = nt(qkv[8 + pair, low:high, take], do)
                t = p.astype(F32) * dp
                ds = (t - p.astype(F32) * jnp.sum(t, axis=0, keepdims=True)).astype(BF16)
                dq.append(tn(ds, qkv[4 + pair, low:high, take]) * 0.125)
                dk = dk.at[low:high].add(nn(ds, qkv[pair, qs, take]))
                dv = dv.at[low:high].add(nn(p, do))
            d_parts[0].append(jnp.concatenate(dq, axis=0))
            d_parts[1].append(dk)
            d_parts[2].append(dv)
    d_qkv = jnp.concatenate(d_parts[0] + d_parts[1] + d_parts[2], axis=1).astype(BF16)
    norm_one, inv_one = normalize(tokens.astype(F32))
    normed = (norm_one * vecs[0:1] + vecs[1:2]).astype(BF16)
    d_w_qkv = tn(normed, d_qkv)
    sums = jnp.sum(d_qkv.astype(F32), axis=0)
    d_b_qv = jnp.concatenate([sums[:WIDTH], sums[2 * WIDTH :]])
    d_normed = nt(d_qkv, wfull[:, : 3 * WIDTH])
    d_in, d_g1, d_s1 = norm_back(d_normed, norm_one, inv_one, vecs[0:1])
    d_tokens = d_middle + d_in

    def spread_sum(value):
        value = lax.psum_scatter(value.astype(BF16), "fsdp", scatter_dimension=0, tiled=True)
        return lax.psum(value, "dp").astype(F32)

    def batch_sum(value):
        return lax.psum(value.astype(BF16), "dp").astype(F32)[None]

    return (
        output,
        d_tokens,
        spread_sum(d_g1),
        spread_sum(d_s1),
        spread_sum(d_w_qkv),
        spread_sum(d_b_qv),
        spread_sum(d_w_o),
        spread_sum(d_b_o),
        spread_sum(d_g2),
        spread_sum(d_s2),
        spread_sum(d_router_t.T),
        batch_sum(d_w_in),
        batch_sum(d_b_in),
        batch_sum(d_w_out),
        batch_sum(d_b_out),
    )


def solution(mesh):
    both, one = P(("dp", "fsdp")), P("fsdp")
    n_f, n_d = mesh.shape["fsdp"], mesh.shape["dp"]
    return jax.shard_map(
        functools.partial(shards, n_f=n_f, n_d=n_d),
        mesh=mesh,
        in_specs=(both,) * 6 + (one,) * 13,
        out_specs=(both,) * 2 + (one,) * 13,
        check_vma=False,
    )
```

time: 742 us -> 694 us (0.935)
  blocking collectives: 132 us -> 32.8 us
  Pallas kernels: 0 us -> 76.3 us
  other arithmetic: 84.5 us -> 49.4 us
  local copies, waits for them, and re-layouts: 108 us -> 88.8 us
  matrix products: 180 us -> 197 us
  starting transfers between devices: 20.5 us -> 30.6 us
    all_gather x3 -> x0, blocking collectives: 85.5 us -> none  [the longest x1 45.5 us: shards(): lax.all_gather(w_router, 'fsdp', axis=0, tiled=True)]
    pallas_call x0 -> x1, Pallas kernels: none -> 76.3 us  [front(): pl.pallas_call(functools.partial(front_kernel, n_f, n_d, experts, cap, ca...]
    scatter-add x0 -> x48, local copies, waits for them, and re-layouts: none -> 70.5 us  [the longest x24 35.3 us: shards(): dv = dv.at[low:high].add(nn(p, do))]
    psum x1, waiting for transfers between devices: 76.8 us -> 40.8 us  [spread_sum(): return lax.psum(value, 'dp').astype(F32)]
    unnamed x6 -> x5, waiting for transfers between devices: 35.6 us -> 61 us
    all_to_all x4 -> x2, waiting for transfers between devices: 7.5 us -> 31.5 us  [back(): lax.all_to_all(value, 'fsdp', split_axis=0, concat_axis=0, tiled=True)]
    convert_element_type x25 -> x16, other arithmetic: 32.4 us -> 11.2 us  [the longest x9 6.87 us: spread_sum(): return lax.psum(value, 'dp').astype(F32)]
    reduce_sum x13 -> x9, other arithmetic: 28.3 us -> 8.37 us  [the longest x1 2.53 us: shards(): d_b_out = jnp.sum(d_result.astype(F32), axis=0)]
  transfers between devices with their start and end apart: 9 -> 6, of which waited for: 5 -> 4; matrix products, arithmetic and copies ran while one was open for 32% -> 24% of each run, Pallas kernels for 0% -> 0%
where the time goes in v1:
time: 694 us; the launch traced here: 682 us
  matrix products  197 us (28%)
  waiting for transfers between devices  190 us (27%)
  local copies, waits for them, and re-layouts  88.8 us (13%)
  Pallas kernels  76.3 us (11%)
  other arithmetic  49.4 us (7%)
  blocking collectives  32.8 us (5%)
  starting transfers between devices  30.6 us (4%)
  between operations  16.4 us (2%)
    dot_general x53, matrix products, nn(): return jnp.dot(left, right, preferred_element_type=F32)  107 us
    pallas_call x1, Pallas kernels, front(): pl.pallas_call(functools.partial(front_kernel, n_f, n_d, experts, cap, ca...  76.3 us
    unnamed x5, waiting for transfers between devices  61 us
    reduce_scatter x2, waiting for transfers between devices, spread_sum(): lax.psum_scatter(value.astype(BF16), 'fsdp', scatter_dimension=0, tiled=T...  56.7 us
    dot_general x29, matrix products, tn(): lax.dot_general(left, right, (((0,), (0,)), ((), ())), preferred_element_...  49.2 us
    psum x1, waiting for transfers between devices, spread_sum(): return lax.psum(value, 'dp').astype(F32)  40.8 us
    dot_general x29, matrix products, nt(): lax.dot_general(left, right, (((1,), (1,)), ((), ())), preferred_element_...  40.8 us
    scatter-add x24, local copies, waits for them, and re-layouts, shards(): dv = dv.at[low:high].add(nn(p, do))  35.3 us
  transfers between devices with their start and end apart: 6, of which 4 were waited for; matrix products, arithmetic and copies ran while one was open for 24% of the time, Pallas kernels for 0%

profile of v1, /device:TPU:1, one launch (start us, length us, event | category | flops | bytes accessed | tf_op | source)
XLA Modules:
  0.0 681.7 jit_solution(763146642048849855)
XLA Ops:
  20.4 76.3 %front.1 = (bf16[8,192,512]{2,1,0:T(8,128)(2,1)}, bf16[8,192,512]{2,1,0:T(8,128)(2,1)}, bf16[8,3,528,240]{3,2,1,0:T(8,128)(2,1)}, bf16[12,720,128]{2,1,0:T(8,128...) custom-call(bf16[720,512]{1,0:T(8,128)(2,1)S(1)} %copy-done.4, ...), custom_call_target="tpu_custom_call" | custom-call | tf_op jit(solution)/shard_map/front/pallas_call | solution.py:375
  98.7 1.9 fusion.393
  100.9 2.5 fusion.388
  103.4 32.0 %multiply_convert_fusion = (bf16[1536,2048]{1,0:T(8,128)(2,1)S(1)}, f32[1536,2048]{1,0:T(8,128)}, f32[1536,2048]{1,0:T(8,128)}) fusion(f32[2048]{0:T(1024)S(1)} %bitcast.510, bf16[1536,512]{1,0:T(8,128)(2,1)S(1)} %bitcast.501, bf16[1,512,2048]{2,1,0:T(8,128)(2,1)S(1)} %copy-done), kind=kOutput, calls=%fused_computation.3 | convolution fusion | flops 3428843520 | bytes 35135488 | tf_op jit(solution)/shard_map/dot_general | solution.py:32
  135.5 5.4 fusion.9
  140.9 15.6 %fusion.418 = (bf16[2048]{0:T(1024)(128)(2,1)}, bf16[1536,2048]{1,0:T(8,128)(2,1)}) fusion(f32[1536,2048]{1,0:T(8,128)} %get-tuple-element.644, bf16[1536,512]{1,0:T(8,128)(2,1)S(1)} %bitcast.503, bf16[1,2048,512]{2,1,0:T(8,128)(2,1)S(1)} %copy-done.50, f32[1536,2048]{1,0:T(8,128)} %get-tuple-element.679, f32[2048]{0:T(1024)S(1)} %bitcast.511), kind=kOutput, calls=%fused_computation.622 | convolution fusion | flops 3271555072 | bytes 35139584 | tf_op jit(solution)/shard_map/dot_general | solution.py:24
  156.4 7.9 %fusion.22 = f32[1536,512]{1,0:T(8,128)} fusion(bf16[1536,2048]{1,0:T(8,128)(2,1)} %get-tuple-element.733, bf16[1,512,2048]{2,1,0:T(8,128)(2,1)S(1)} %copy-done), kind=kOutput, calls=%fused_computation.47 | convolution fusion | flops 3221225472 | bytes 11534336 | tf_op jit(solution)/shard_map/dot_general | solution.py:24
  164.4 2.6 fusion.11
  168.7 25.3 %all-to-all-start.1 = ((bf16[8,192,512]{2,1,0:T(8,128)(2,1)}), bf16[8,192,512]{2,1,0:T(8,128)(2,1)}, u32[]{:S(2)}, u32[]{:S(2)}) async-start(bf16[8,192,512]{2,1,0:T(8,128)(2,1)} %fusion.32), calls=%async_computation.1 | async-start | bytes 3145728 | tf_op jit(solution)/shard_map/all_to_all | solution.py:519
  198.8 31.5 %all-to-all-done.1 = bf16[8,192,512]{2,1,0:T(8,128)(2,1)} async-done(((bf16[8,192,512]{2,1,0:T(8,128)(2,1)}), bf16[8,192,512]{2,1,0:T(8,128)(2,1)}, u32[]{:S(2)}, u32[]{:S(2)}) %all-to-all-start.1) | async-done | bytes 1572896 | tf_op jit(solution)/shard_map/all_to_all | solution.py:519
  230.4 4.4 multiply_reduce_fusion
  236.1 2.2 convolution_convert_fusion.3
  247.9 1.9 convolution_add_fusion.2
  253.0 1.9 convolution_add_fusion.4
  305.2 1.9 scatter-add.236
  307.1 2.0 convolution_add_fusion.18
  316.5 1.9 scatter-add.226
  318.4 2.0 convolution_add_fusion.20
  322.2 1.9 scatter-add.221
  327.8 1.9 scatter-add.216
  329.7 2.0 convolution_add_fusion.22
  333.5 1.9 scatter-add.211
  341.0 2.0 convolution_add_fusion.24
  344.7 1.9 scatter-add.201
  364.8 1.9 scatter-add.191
  370.4 1.9 scatter-add.186
  372.3 2.0 convolution_add_fusion.28
  376.1 1.9 scatter-add.196
  378.0 2.0 convolution_add_fusion.26
  387.3 1.9 scatter-add.166
  389.2 2.0 convolution_add_fusion.32
  393.0 2.0 scatter-add.171
  421.2 2.9 convolution_convert_fusion.2
  424.1 3.1 fusion.33
  427.3 4.5 all-to-all-start
  434.8 8.2 %fusion.12 = bf16[1,512,2048]{2,1,0:T(8,128)(2,1)} fusion(bf16[1536,512]{1,0:T(8,128)(2,1)} %bitcast.500, bf16[1536,2048]{1,0:T(8,128)(2,1)} %get-tuple-element.733), kind=kOutput, calls=%fused_computation.37 | convolution fusion | flops 3222274048 | bytes 9961472 | tf_op jit(solution)/shard_map/dot_general | solution.py:28
  443.0 7.7 %fusion.13 = bf16[1,2048,512]{2,1,0:T(8,128)(2,1)} fusion(bf16[1536,2048]{1,0:T(8,128)(2,1)} %copy-done.52, bf16[1536,512]{1,0:T(8,128)(2,1)S(1)} %copy-done.53), kind=kOutput, calls=%fused_computation.38 | convolution fusion | flops 3222274048 | bytes 9961472 | tf_op jit(solution)/shard_map/dot_general | solution.py:28
  450.7 56.7 %reduce-scatter.6.cloned.1.call-done = bf16[64,1536]{1,0:T(8,128)(2,1)} async-done(((bf16[512,1536]{1,0:T(8,128)(2,1)}), bf16[64,1536]{1,0:T(8,128)(2,1)}) %reduce-scatter.6.cloned.1.call-update) | async-done | bytes 196624 | tf_op jit(solution)/shard_map/reduce_scatter | solution.py:566
  509.3 61.0 %reduce-scatter.10.cloned.1.call-done = bf16[64,8]{1,0:T(8,128)(2,1)} async-done(((bf16[512,8]{1,0:T(8,128)(2,1)}), bf16[64,8]{1,0:T(8,128)(2,1)}) %reduce-scatter.10.cloned.1.call-update) | async-done | bytes 1040
  571.1 2.1 reduce.100
  573.2 5.0 fusion.40
  578.2 16.3 %all-reduce.22 = (bf16[512]{0:T(512)(128)(2,1)S(1)}, bf16[512]{0:T(512)(128)(2,1)S(1)}, bf16[1024]{0:T(1024)(128)(2,1)S(1)}, bf16[512]{0:T(512)(128)(2,1)S(1)}, ...) all-reduce(bf16[512]{0:T(512)(128)(2,1)S(1)} %get-tuple-element.612, ...), channel_id=2, replica_groups=mesh['dp'=4,'fsdp'=8] {'fsdp'}, use_global_device_ids=true, to_apply=%region_37.39.clone | all-reduce | flops 3584 | bytes 14336
  594.9 16.6 %all-reduce.23 = (bf16[64]{0:T(256)(128)(2,1)S(1)}, bf16[64]{0:T(256)(128)(2,1)S(1)}, bf16[128]{0:T(256)(128)(2,1)S(1)}, bf16[64]{0:T(256)(128)(2,1)S(1)}, bf16[...) all-reduce(bf16[64]{0:T(256)(128)(2,1)S(1)} %dynamic-slice.369, ...), channel_id=1, replica_groups=mesh['dp'=4,'fsdp'=8] {'dp'}, use_global_device_ids=true, to_apply=%region_38.40 | all-reduce | flops 3520 | bytes 14080 | tf_op jit(solution)/shard_map/psum | solution.py:567
  616.4 3.5 fusion.39
  619.9 4.1 add_convert_fusion.1
  623.9 40.8 %all-reduce.27.cloned.1.call-done = (bf16[64,1536]{1,0:T(8,128)(2,1)}, bf16[64,512]{1,0:T(8,128)(2,1)}, bf16[1,512,2048]{2,1,0:T(8,128)(2,1)}, bf16[1,2048,512]{2,1,0:T(8,128)(2,1)}) async-done(((bf16[64,1536]{1,0:T(8,128)(2,1)}, bf16[64,512]{1,0:T(8,128)(2,1)}, bf16[1,512,2048]{2,1,0:T(8,128)(2,1)}, bf16[1,2048,512]{2,1,0:T(8,128)(2,1)}), (bf16[64,1536]{1,0:T(8,128)(2,1)}, bf16[64,512]{1,0:T(8,128)(2,1)}, ...) | async-done | bytes 4456464 | tf_op jit(solution)/shard_map/psum | solution.py:567
  667.9 4.3 broadcast_in_dim.32
  672.2 2.6 broadcast_in_dim.36
  (355 shorter events, 179.8 us)
Async XLA Ops:
  7.2 96.2 %copy-start = (bf16[1,512,2048]{2,1,0:T(8,128)(2,1)S(1)}, bf16[1,512,2048]{2,1,0:T(8,128)(2,1)}, u32[]{:S(2)}) copy-start(bf16[1,512,2048]{2,1,0:T(8,128)(2,1)} %param.132) | copy-start | bytes 6291460
  7.2 157.1 %copy-start.38 = (f32[8]{0:T(128)}, f32[8]{0:T(128)S(1)}, u32[]{:S(2)}) copy-start(f32[8]{0:T(128)S(1)} %compare_convert_fusion) | copy-start | bytes 100
  103.4 32.1 %copy-start.16 = (bf16[8,192,512]{2,1,0:T(8,128)(2,1)S(1)}, bf16[8,192,512]{2,1,0:T(8,128)(2,1)}, u32[]{:S(2)}) copy-start(bf16[8,192,512]{2,1,0:T(8,128)(2,1)} %get-tuple-element.605) | copy-start | bytes 4718596
  103.4 32.1 %copy-start.50 = (bf16[1,2048,512]{2,1,0:T(8,128)(2,1)S(1)}, bf16[1,2048,512]{2,1,0:T(8,128)(2,1)}, u32[]{:S(2)}) copy-start(bf16[1,2048,512]{2,1,0:T(8,128)(2,1)} %param.134) | copy-start | bytes 6291460
  135.4 5.4 copy-start.52
  140.9 23.5 %copy-start.30 = (f32[1536]{0:T(1024)}, f32[1536]{0:T(1024)S(1)}, u32[]{:S(2)}) copy-start(f32[1536]{0:T(1024)S(1)} %mul.523) | copy-start | bytes 18436
  168.7 27.7 %copy-start.5 = (bf16[720,512]{1,0:T(8,128)(2,1)S(1)}, bf16[720,512]{1,0:T(8,128)(2,1)}, u32[]{:S(2)}) copy-start(bf16[720,512]{1,0:T(8,128)(2,1)} %tok.1) | copy-start | bytes 2211844
  168.7 61.7 %all-to-all-start.1 = ((bf16[8,192,512]{2,1,0:T(8,128)(2,1)}), bf16[8,192,512]{2,1,0:T(8,128)(2,1)}, u32[]{:S(2)}, u32[]{:S(2)}) async-start(bf16[8,192,512]{2,1,0:T(8,128)(2,1)} %fusion.32), calls=%async_computation.1 | async-start | bytes 3145728 | tf_op jit(solution)/shard_map/all_to_all | solution.py:519
  193.9 256.7 %reduce-scatter.8.cloned.1.call-start = ((), (), s32[]{:S(2)}) async-start(), calls=%async_computation.6 | async-start | bytes 589824 | tf_op jit(solution)/shard_map/reduce_scatter | solution.py:566
  196.0 38.8 %copy-start.36 = (f32[1536]{0:T(1024)}, f32[1536]{0:T(1024)S(1)}, u32[]{:S(2)}) copy-start(f32[1536]{0:T(1024)S(1)} %iota_convert_fusion) | copy-start | bytes 18436
  196.4 38.4 %copy-start.40 = (f32[720]{0:T(1024)}, f32[720]{0:T(1024)S(1)}, u32[]{:S(2)}) copy-start(f32[720]{0:T(1024)S(1)} %get-tuple-element.618) | copy-start | bytes 8644
  196.4 38.4 %copy-start.42 = (f32[720]{0:T(1024)}, f32[720]{0:T(1024)S(1)}, u32[]{:S(2)}) copy-start(f32[720]{0:T(1024)S(1)} %get-tuple-element.619) | copy-start | bytes 8644
  196.6 38.2 %copy-start.32 = (f32[720]{0:T(1024)}, f32[720]{0:T(1024)S(1)}, u32[]{:S(2)}) copy-start(f32[720]{0:T(1024)S(1)} %broadcast_multiply_fusion.2) | copy-start | bytes 8644
  234.8 20.8 %slice-start = ((s8[6488064]{0:T(1024)(128)(4,1)}), s8[2293760]{0:T(1024)(128)(4,1)S(1)}, s32[]{:S(2)}) async-start(s8[6488064]{0:T(1024)(128)(4,1)} %bitcast.496), calls=%async_computation.9 | async-start | bytes 4587520
  236.1 67.6 %copy-start.10 = (f32[720,512]{1,0:T(8,128)}, f32[720,512]{1,0:T(8,128)S(1)}, u32[]{:S(2)}) copy-start(f32[720,512]{1,0:T(8,128)S(1)} %get-tuple-element.642) | copy-start | bytes 4423684
  236.1 19.5 %slice-start.1 = ((s8[6488064]{0:T(1024)(128)(4,1)}), s8[4194304]{0:T(1024)(128)(4,1)S(1)}, s32[]{:S(2)}) async-start(s8[6488064]{0:T(1024)(128)(4,1)} %bitcast.496), calls=%async_computation.10 | async-start | bytes 8388608
  238.3 49.5 %copy-start.12 = (bf16[720,512]{1,0:T(8,128)(2,1)}, bf16[720,512]{1,0:T(8,128)(2,1)S(1)}, u32[]{:S(2)}) copy-start(bf16[720,512]{1,0:T(8,128)(2,1)S(1)} %convolution_convert_fusion.3) | copy-start | bytes 2211844
  254.9 8.7 %copy-start.11 = (bf16[12,720,128]{2,1,0:T(8,128)(2,1)S(1)}, bf16[12,720,128]{2,1,0:T(8,128)(2,1)}, u32[]{:S(2)}) copy-start(bf16[12,720,128]{2,1,0:T(8,128)(2,1)} %get-tuple-element.607) | copy-start | bytes 6635524
  295.4 8.3 %copy-start.9 = (bf16[720,512]{1,0:T(8,128)(2,1)S(1)}, bf16[720,512]{1,0:T(8,128)(2,1)}, u32[]{:S(2)}) copy-start(bf16[720,512]{1,0:T(8,128)(2,1)} %copy-done.8) | copy-start | bytes 2211844
  305.2 202.2 %reduce-scatter.6.cloned.1.call-start = ((), (), s32[]{:S(2)}) async-start(), calls=%async_computation.5 | async-start | bytes 1769472 | tf_op jit(solution)/shard_map/reduce_scatter | solution.py:566
  405.4 14.2 %copy-start.17 = (f32[720,64]{0,1:T(8,128)S(1)}, f32[720,64]{0,1:T(8,128)}, u32[]{:S(2)}) copy-start(f32[720,64]{0,1:T(8,128)} %scatter-add.204) | copy-start | bytes 552964
  405.4 14.2 %copy-start.18 = (f32[720,64]{0,1:T(8,128)S(1)}, f32[720,64]{0,1:T(8,128)}, u32[]{:S(2)}) copy-start(f32[720,64]{0,1:T(8,128)} %scatter-add.209) | copy-start | bytes 552964
  407.2 12.4 %copy-start.19 = (f32[720,64]{0,1:T(8,128)S(1)}, f32[720,64]{0,1:T(8,128)}, u32[]{:S(2)}) copy-start(f32[720,64]{0,1:T(8,128)} %scatter-add.214) | copy-start | bytes 552964
  409.1 10.3 %copy-start.29 = (f32[720,64]{0,1:T(8,128)S(1)}, f32[720,64]{0,1:T(8,128)}, u32[]{:S(2)}) copy-start(f32[720,64]{0,1:T(8,128)} %scatter-add.179) | copy-start | bytes 552964
  409.1 10.4 %copy-start.28 = (f32[720,64]{0,1:T(8,128)S(1)}, f32[720,64]{0,1:T(8,128)}, u32[]{:S(2)}) copy-start(f32[720,64]{0,1:T(8,128)} %scatter-add.184) | copy-start | bytes 552964
  409.1 10.4 %copy-start.26 = (f32[720,64]{0,1:T(8,128)S(1)}, f32[720,64]{0,1:T(8,128)}, u32[]{:S(2)}) copy-start(f32[720,64]{0,1:T(8,128)} %scatter-add.189) | copy-start | bytes 552964
  409.1 10.4 %copy-start.25 = (f32[720,64]{0,1:T(8,128)S(1)}, f32[720,64]{0,1:T(8,128)}, u32[]{:S(2)}) copy-start(f32[720,64]{0,1:T(8,128)} %scatter-add.194) | copy-start | bytes 552964
  409.1 10.4 %copy-start.27 = (f32[720,64]{0,1:T(8,128)S(1)}, f32[720,64]{0,1:T(8,128)}, u32[]{:S(2)}) copy-start(f32[720,64]{0,1:T(8,128)} %scatter-add.199) | copy-start | bytes 552964
  409.1 10.5 %copy-start.20 = (f32[720,64]{0,1:T(8,128)S(1)}, f32[720,64]{0,1:T(8,128)}, u32[]{:S(2)}) copy-start(f32[720,64]{0,1:T(8,128)} %scatter-add.219) | copy-start | bytes 552964
  411.0 8.7 %copy-start.21 = (f32[720,64]{0,1:T(8,128)S(1)}, f32[720,64]{0,1:T(8,128)}, u32[]{:S(2)}) copy-start(f32[720,64]{0,1:T(8,128)} %scatter-add.224) | copy-start | bytes 552964
  411.9 7.8 %copy-start.22 = (f32[720,64]{0,1:T(8,128)S(1)}, f32[720,64]{0,1:T(8,128)}, u32[]{:S(2)}) copy-start(f32[720,64]{0,1:T(8,128)} %scatter-add.229) | copy-start | bytes 552964
  413.8 6.0 copy-start.23
  414.7 5.1 copy-start.24
  416.5 4.7 copy-start.33
  416.5 4.7 copy-start.34
  416.5 4.7 copy-start.35
  416.6 4.7 copy-start.47
  427.3 4.6 copy-start.39
  427.3 192.6 %all-to-all-start = ((bf16[8,192,512]{2,1,0:T(8,128)(2,1)}), bf16[8,192,512]{2,1,0:T(8,128)(2,1)}, u32[]{:S(2)}, u32[]{:S(2)}) async-start(bf16[8,192,512]{2,1,0:T(8,128)(2,1)} %fusion.33), calls=%async_computation | async-start | bytes 3145728 | tf_op jit(solution)/shard_map/all_to_all | solution.py:519
  431.8 138.5 %reduce-scatter.10.cloned.1.call-start = ((), (), s32[]{:S(2)}) async-start(), calls=%async_computation.7 | async-start | bytes 147456
  434.5 230.2 %all-reduce.27.cloned.1.call-start = ((), (), s32[]{:S(2)}) async-start(), calls=%async_computation.8 | async-start | bytes 8912896 | tf_op jit(solution)/shard_map/psum | solution.py:567
  434.7 8.2 %copy-start.53 = (bf16[1536,512]{1,0:T(8,128)(2,1)S(1)}, bf16[1536,512]{1,0:T(8,128)(2,1)}, u32[]{:S(2)}) copy-start(bf16[1536,512]{1,0:T(8,128)(2,1)} %get-tuple-element.671) | copy-start | bytes 4718596
  450.6 56.8 %copy-start.51 = (u32[32]{0:T(128)S(1)}, u32[32]{0:T(128)}, u32[]{:S(2)}) copy-start(u32[32]{0:T(128)} %constant.1183) | copy-start | bytes 388
  450.6 58.7 %copy-start.44 = (bf16[512]{0:T(512)(128)(2,1)S(1)}, bf16[512]{0:T(512)(128)(2,1)}, u32[]{:S(2)}) copy-start(bf16[512]{0:T(512)(128)(2,1)} %get-tuple-element.639) | copy-start | bytes 3076
  450.6 58.7 %copy-start.45 = (bf16[2048]{0:T(1024)(128)(2,1)S(1)}, bf16[2048]{0:T(1024)(128)(2,1)}, u32[]{:S(2)}) copy-start(bf16[2048]{0:T(1024)(128)(2,1)} %get-tuple-element.732) | copy-start | bytes 12292
  573.2 5.0 copy-start.46
  573.2 5.0 copy-start.48
  573.2 5.0 copy-start.49
  (14 other events, 37.8 us)
Sparse Core Ops, SparseCore 0:
  305.3 60.0 reduce-scatter.7
  424.3 83.0 reduce-scatter.5
  511.3 58.9 reduce-scatter.9
  573.3 91.3 all-reduce.26

commit v2 on v1

v2 whole, which is shorter than its diff:
```python
import functools

import jax
import jax.numpy as jnp
from jax import lax
from jax.experimental import pallas as pl
from jax.experimental.pallas import tpu as pltpu
from jax.sharding import PartitionSpec as P

MESH = pl.DeviceIdType.MESH
BF16 = jnp.bfloat16
F32 = jnp.float32
SLOTS = 720
WIDTH = 512
PAIRS = 4
EPS = 1e-06
WINDOWS = ((0, 384, 0), (96, 624, 384), (336, 720, 912))
KEYS = 1296
QBLK = 240
ROWBLK = 240
TILE = 128
FTILE = 512
CHUNKS = 4


def nt(left, right):
    return lax.dot_general(left, right, (((1,), (1,)), ((), ())), preferred_element_type=F32)


def tn(left, right):
    return lax.dot_general(left, right, (((0,), (0,)), ((), ())), preferred_element_type=F32)


def nn(left, right):
    return jnp.dot(left, right, preferred_element_type=F32)


def normalize(value):
    centred = value - jnp.mean(value, axis=-1, keepdims=True)
    inv_std = lax.rsqrt(jnp.mean(centred * centred, axis=-1, keepdims=True) + EPS)
    return centred * inv_std, inv_std


def aligned(index, size):
    return pl.ds(pl.multiple_of(index * size, size), size)


class Place:
    def __init__(self, n_f, n_d):
        self.n_f, self.n_d, self.n_x = n_f, n_d, n_d // 2
        self.me = lax.axis_index("fsdp")
        self.d = lax.axis_index("dp")
        self.x = lax.div(self.d, 2)
        self.core = lax.rem(self.d, 2)

    def ahead(self, k):
        return lax.rem(self.me + k, self.n_f)

    def fsdp_peer(self, k):
        return (self.d, self.ahead(k))

    def x_index(self, i):
        return lax.rem(self.x + i, self.n_x)

    def x_peer(self, i):
        return (self.x_index(i) * 2 + self.core, self.me)

    def partner(self):
        return (self.x * 2 + 1 - self.core, self.me)

    def dp_peer(self, i):
        return (lax.rem(self.d + i, self.n_d), self.me)

    def enter(self):
        bar = pltpu.get_barrier_semaphore()

        def greet(k, _):
            pl.semaphore_signal(bar, inc=1, device_id=self.fsdp_peer(k), device_id_type=MESH)
            return 0

        lax.fori_loop(1, self.n_f, greet, 0)
        for i in range(1, self.n_d):
            pl.semaphore_signal(bar, inc=1, device_id=self.dp_peer(i), device_id_type=MESH)
        pl.semaphore_wait(bar, self.n_f - 1 + self.n_d - 1)


def remote(src, dst, send_sem, recv_sem, device):
    return pltpu.make_async_remote_copy(
        src_ref=src,
        dst_ref=dst,
        send_sem=send_sem,
        recv_sem=recv_sem,
        device_id=device,
        device_id_type=MESH,
    )


def loop(low, high, body):
    def step(k, carry):
        body(k)
        return carry

    lax.fori_loop(low, high, step, 0)


def block_kernel(
    n_f,
    n_d,
    experts,
    cap,
    cap_rows,
    tok,
    cot,
    cols,
    rows,
    wsh,
    vsh,
    w_in_hbm,
    w_out_hbm,
    b_in,
    b_out,
    o_out,
    o_tokens,
    o_expert,
    o_dense,
    o_vec,
    o_qv,
    o_bias,
    wfull,
    vecs,
    bias,
    scores,
    probs,
    qkv,
    normed,
    mixed,
    middle,
    routed,
    place,
    send_x,
    send_g,
    x_in,
    g_in,
    w_in,
    w_out,
    hidden,
    d_pre,
    ret_d,
    ret_o,
    table_d,
    ew,
    ew_core,
    ew_x,
    dense_core,
    dense_x,
    dense_f,
    final,
    pack,
    pack_dp,
    vec_f,
    qv_f,
    d_middle,
    s_w,
    r_w,
    s_v,
    r_v,
    s_dx,
    r_dx,
    s_dc,
    r_dc,
    s_g,
    r_g,
    s_x,
    r_x,
    s_d,
    r_d,
    s_o,
    r_o,
    s_ec,
    r_ec,
    s_ex,
    r_ex,
    s_ea,
    r_ea,
    s_eb,
    r_eb,
    s_gc,
    r_gc,
    s_gx,
    r_gx,
    s_gf,
    r_gf,
    s_gd,
    r_gd,
    s_p,
    r_p,
    s_vf,
    r_vf,
    s_qf,
    r_qf,
    s_own,
    ready,
):
    at = Place(n_f, n_d)
    n_x = at.n_x
    shard = WIDTH // n_f
    colw = wsh.shape[1] // n_d
    other = 1 - at.core

    def cols_of(d):
        return aligned(d, colw)

    def w_piece(owner, d):
        return wfull.at[aligned(owner, shard), cols_of(d)]

    def x_back(i):
        return at.x_index(n_x - i)

    load_in = pltpu.make_async_copy(w_in_hbm, w_in, s_own.at[0])
    load_out = pltpu.make_async_copy(w_out_hbm, w_out, s_own.at[1])
    load_in.start()
    load_out.start()
    at.enter()

    def send_w(k):
        return remote(
            wsh.at[:, cols_of(at.d)], w_piece(at.me, at.d), s_w.at[k], r_w.at[k], at.fsdp_peer(k)
        )

    vec_rows = vsh.shape[0]

    def vec_piece(owner):
        return hidden.at[aligned(owner, vec_rows), 0:WIDTH]

    def send_v(k):
        return remote(vsh, vec_piece(at.me), s_v.at[k], r_v.at[k], at.fsdp_peer(k))

    def share_x(i, k):
        piece = w_piece(at.ahead(n_f - k), at.d)
        return remote(piece, piece, s_dx.at[i - 1, k], r_dx.at[i - 1, k], at.x_peer(i))

    def share_core(i, k):
        piece = w_piece(at.ahead(n_f - k), x_back(i) * 2 + at.core)
        return remote(piece, piece, s_dc.at[i, k], r_dc.at[i, k], at.partner())

    loop(1, n_f, lambda k: send_v(k).start())
    loop(1, n_f, lambda k: send_w(k).start())
    wfull[aligned(at.me, shard), :] = wsh[...]
    vec_piece(at.me)[...] = vsh[...]

    expert_iota = lax.broadcasted_iota(jnp.int32, (experts, SLOTS), 0)
    live = rows[1:2, :] > 0
    before = jnp.where(cols[:, 4:5] < rows[4:5, :], 1.0, 0.0).astype(BF16)
    chose = [
        jnp.where((rows[2 + k : 3 + k, :] == expert_iota) & live, 1.0, 0.0) for k in range(2)
    ]
    rank = [nn(one.astype(BF16), before) for one in chose]
    rank[1] = rank[1] + jnp.sum(chose[0], axis=1, keepdims=True)
    spot_r = []
    for k in range(2):
        slot = jnp.sum(chose[k] * rank[k], axis=0, keepdims=True)
        spot = rows[2 + k : 3 + k, :].astype(F32) * cap_rows + slot
        spot_r.append(jnp.where(live & (slot < cap), spot, -1.0))
    place[...] = jnp.transpose(jnp.concatenate(spot_r + [jnp.zeros((6, SLOTS), F32)], axis=0))
    slot_iota = lax.broadcasted_iota(jnp.int32, (cap_rows, SLOTS), 0)

    def pick(expert):
        mine = (slot_iota + expert * cap_rows).astype(F32)
        return jnp.where((mine == spot_r[0]) | (mine == spot_r[1]), 1.0, 0.0).astype(BF16)

    for b, (low, high, row) in enumerate(WINDOWS):
        queries = slice(b * QBLK, (b + 1) * QBLK)
        shape = (high - low, QBLK)
        same = cols[low:high, 0:1] == rows[0:1, queries]
        itself = (lax.broadcasted_iota(jnp.int32, shape, 0) + low) == (
            lax.broadcasted_iota(jnp.int32, shape, 1) + b * QBLK
        )
        allowed = same & ((cols[low:high, 1:2] > 0) | itself)
        bias[row : row + high - low, 0:QBLK] = jnp.where(allowed, 0.0, -1e30)

    loop(1, n_f, lambda k: send_v(k).wait_recv())
    vecs[...] = vec_piece(0)[...].astype(F32)

    def add_vectors(owner):
        vecs[...] += vec_piece(owner)[...].astype(F32)

    loop(1, n_f, add_vectors)

    def first_norm(i):
        block = aligned(i, ROWBLK)
        value, _ = normalize(tok[block, :].astype(F32))
        normed[block, :] = (value * vecs[0:1, :] + vecs[1:2, :]).astype(BF16)

    loop(0, SLOTS // ROWBLK, first_norm)

    def pass_on(k):
        send_w(k).wait_recv()
        for i in range(1, n_x):
            share_x(i, k).start()
        share_core(0, k).start()

    loop(1, n_f, pass_on)

    def order(step):
        return 1 + lax.rem(2 * n_f - 4 - step, n_f - 1)

    def send_rows(buffer, into, send, recv, k):
        return remote(
            buffer.at[aligned(at.ahead(k), cap_rows), :],
            into.at[aligned(n_f - k, cap_rows), :],
            send.at[k],
            recv.at[n_f - k],
            at.fsdp_peer(k),
        )

    def dispatch(source, buffer, into, send, recv):
        def one(step):
            k = order(step)
            expert = at.ahead(k)
            buffer[aligned(expert, cap_rows), :] = nn(pick(expert), source[...]).astype(BF16)
            send_rows(buffer, into, send, recv, k).start()

        loop(0, n_f - 1, one)
        into[0:cap_rows, :] = nn(pick(at.me), source[...]).astype(BF16)

    dispatch(cot, send_g, g_in, s_g, r_g)

    for i in range(1, n_x):

        def cross(k, i=i):
            piece = w_piece(at.ahead(n_f - k), x_back(i) * 2 + at.core)
            remote(piece, piece, s_dx.at[i - 1, k], r_dx.at[i - 1, k], at.x_peer(i)).wait_recv()
            share_core(i, k).start()

        loop(1, n_f, cross)
    for i in range(n_x):

        def arrive(k, i=i):
            piece = w_piece(at.ahead(n_f - k), x_back(i) * 2 + other)
            remote(piece, piece, s_dc.at[i, k], r_dc.at[i, k], at.partner()).wait_recv()

        loop(1, n_f, arrive)

    def project(pair):
        out = nn(normed[...], wfull[:, pl.ds(pl.multiple_of(pair * 384, 128), 384)])
        lanes = aligned(pair, TILE)
        qkv[pair] = ((out[:, 0:128] + vecs[2:3, lanes]) * 0.125).astype(BF16)
        qkv[PAIRS + pair] = out[:, 128:256].astype(BF16)
        qkv[2 * PAIRS + pair] = (out[:, 256:384] + vecs[3:4, lanes]).astype(BF16)

    loop(0, PAIRS, project)

    lane = lax.broadcasted_iota(jnp.int32, (1, TILE), 1)
    halves = (lane < 64, lane >= 64)

    def attend(pair):
        for b, (low, high, row) in enumerate(WINDOWS):
            window = slice(row, row + high - low)
            query = qkv[pair, b * QBLK : (b + 1) * QBLK, :]
            keys = qkv[PAIRS + pair, low:high, :]
            for h in range(2):
                one = jnp.where(halves[h], query, jnp.zeros_like(query))
                scores[h, window, :] = nt(keys, one) + bias[window, 0:QBLK]
        for b, (low, high, row) in enumerate(WINDOWS):
            window = slice(row, row + high - low)
            for h in range(2):
                value = scores[h, window, :]
                power = jnp.exp(value - jnp.max(value, axis=0, keepdims=True))
                share = 1.0 / jnp.sum(power, axis=0, keepdims=True)
                probs[2 * pair + h, window, :] = (power * share).astype(BF16)
        for b, (low, high, row) in enumerate(WINDOWS):
            window = slice(row, row + high - low)
            values = qkv[2 * PAIRS + pair, low:high, :]
            both = [tn(probs[2 * pair + h, window, :], values) for h in range(2)]
            mixed[b * QBLK : (b + 1) * QBLK, aligned(pair, TILE)] = jnp.where(
                halves[0], both[0], both[1]
            ).astype(BF16)

    loop(0, PAIRS, attend)

    def second_norm(i):
        block = aligned(i, ROWBLK)
        total = nn(mixed[block, :], wfull[:, 3 * WIDTH : 4 * WIDTH])
        total = tok[block, :].astype(F32) + total + vecs[4:5, :]
        middle[block, :] = total
        value, _ = normalize(total)
        routed[block, :] = (value * vecs[5:6, :] + vecs[6:7, :]).astype(BF16)

    loop(0, SLOTS // ROWBLK, second_norm)
    dispatch(routed, send_x, x_in, s_x, r_x)

    load_in.wait()
    load_out.wait()
    pack[...] = jnp.zeros_like(pack)
    router = vecs[8 : 8 + experts, :].astype(BF16)
    chunk_rows = n_f * cap_rows // CHUNKS
    sources = n_f // CHUNKS
    f_tiles = w_in.shape[1] // FTILE
    bias_at = 8 + experts
    hot = jnp.where(lax.broadcasted_iota(jnp.int32, (1, experts), 1) == at.me, 1.0, 0.0)

    def give_back(buffer, into, send, recv, r):
        return remote(
            buffer.at[aligned(r, cap_rows), :],
            into.at[aligned(at.me, cap_rows), :],
            send.at[r],
            recv.at[r],
            at.fsdp_peer(r),
        )

    acc_o, acc_d = d_middle.at[0:chunk_rows, :], d_middle.at[chunk_rows : 2 * chunk_rows, :]

    def expert_chunk(step):
        pos = lax.rem(step + 1, CHUNKS)
        block = aligned(pos, chunk_rows)
        first = pos * sources

        def arrive(r):
            @pl.when(r > 0)
            def _():
                send_rows(send_g, g_in, s_g, r_g, n_f - r).wait_recv()
                send_rows(send_x, x_in, s_x, r_x, n_f - r).wait_recv()

        loop(first, first + sources, arrive)
        x_rows = x_in[block, :]
        logits = nt(x_rows, router)
        gates = jnp.exp(logits - jnp.max(logits, axis=-1, keepdims=True))
        gates = gates / jnp.sum(gates, axis=-1, keepdims=True)
        chosen = jnp.sum(gates * hot, axis=-1, keepdims=True)
        g_rows = (chosen * g_in[block, :].astype(F32)).astype(BF16)
        g_in[block, :] = g_rows
        pack[bias_at + 4 : bias_at + 5, :] += jnp.sum(g_rows.astype(F32), axis=0, keepdims=True)
        acc_o[...] = jnp.broadcast_to(b_out[...].astype(F32), acc_o.shape)
        acc_d[...] = jnp.zeros_like(acc_d)
        def tile(f):
            lanes = aligned(f, FTILE)
            pre = nn(x_in[block, :], w_in[:, lanes]) + b_in[:, lanes].astype(F32)
            d_act = nt(g_in[block, :], w_out[lanes, :])
            cdf = 0.5 + 0.5 * lax.erf(pre * 0.7071067811865476)
            act = (pre * cdf).astype(BF16)
            slope = cdf + pre * jnp.exp(-0.5 * pre * pre) * 0.3989422804014327
            d_row = (d_act * slope).astype(BF16)
            hidden[block, lanes] = act
            d_pre[block, lanes] = d_row
            pack[pl.ds(bias_at + f, 1), :] += jnp.sum(
                d_row.astype(F32), axis=0, keepdims=True
            )
            acc_o[...] += nn(act, w_out[lanes, :])
            acc_d[...] += nt(d_row, w_in[:, lanes])

        loop(0, f_tiles, tile)
        result = acc_o[...]
        weight = jnp.sum(g_in[block, :].astype(F32) * result, axis=-1, keepdims=True)
        d_logits = (weight * (hot - gates)).astype(BF16)
        pack[8:bias_at, :] += tn(d_logits, x_in[block, :])
        ret_d[block, :] = (acc_d[...] + nn(d_logits, router)).astype(BF16)
        ret_o[block, :] = (chosen * result).astype(BF16)

        def back(r):
            @pl.when(r > 0)
            def _():
                give_back(ret_d, table_d, s_d, r_d, r).start()

        loop(first, first + sources, back)

    loop(0, CHUNKS, expert_chunk)
    mine = aligned(at.me, cap_rows)
    table_d[mine, :] = ret_d[0:cap_rows, :]

    part = FTILE // n_x
    per_core = f_tiles // 2

    def e_tile(core, j):
        return (core * per_core + j // 2) * 2 + j % 2

    def to_partner(j):
        return remote(ew.at[e_tile(other, j)], ew_core.at[j], s_ec.at[j], r_ec.at[j], at.partner())

    def to_x(i, j):
        src = ew.at[e_tile(at.core, j), aligned(at.x_index(i), part), :]
        return remote(src, ew_x.at[i - 1, j], s_ex.at[i - 1, j], r_ex.at[i - 1, j], at.x_peer(i))

    def e_part(core, j, x):
        return e_tile(core, j), aligned(x, part)

    def all_x(i, j):
        tile, mine = e_part(at.core, j, at.x)
        src, dst = ew.at[tile, mine, :], o_expert.at[tile, mine, :]
        return remote(src, dst, s_ea.at[i - 1, j], r_ea.at[i - 1, j], at.x_peer(i))

    def from_x(i, j):
        tile, theirs = e_part(at.core, j, x_back(i))
        dst = o_expert.at[tile, theirs, :]
        return remote(dst, dst, s_ea.at[i - 1, j], r_ea.at[i - 1, j], at.x_peer(i))

    def to_core(i, j, core):
        tile, piece = e_part(core, j, x_back(i))
        dst = o_expert.at[tile, piece, :]
        src = ew.at[tile, piece, :] if i == 0 else dst
        return remote(src, dst, s_eb.at[i, j], r_eb.at[i, j], at.partner())

    def to_self(j):
        tile, mine = e_part(at.core, j, at.x)
        return pltpu.make_async_copy(
            ew.at[tile, mine, :], o_expert.at[tile, mine, :], s_own.at[2 + j]
        )

    n_mine = 2 * per_core

    def grad_tiles(core, f):
        tile = core * per_core + f
        lanes = aligned(tile, FTILE)
        ew[2 * tile] = tn(x_in[...], d_pre[:, lanes]).astype(BF16)
        ew[2 * tile + 1] = tn(hidden[:, lanes], g_in[...]).astype(BF16)

    def theirs(f):
        grad_tiles(other, f)
        to_partner(2 * f).start()
        to_partner(2 * f + 1).start()

    loop(0, per_core, theirs)
    loop(0, per_core, lambda f: grad_tiles(at.core, f))

    def sum_cores(j):
        to_partner(j).wait_recv()
        tile = e_tile(at.core, j)
        ew[tile] = (ew[tile].astype(F32) + ew_core[j].astype(F32)).astype(BF16)
        for i in range(1, n_x):
            to_x(i, j).start()

    loop(0, n_mine, sum_cores)

    table_o = send_x

    def left(k):
        send_rows(send_x, x_in, s_x, r_x, k).wait_send()

    loop(1, n_f, left)
    table_o[mine, :] = ret_o[0:cap_rows, :]

    def tell(k):
        pl.semaphore_signal(ready, inc=1, device_id=at.fsdp_peer(k), device_id_type=MESH)

    loop(1, n_f, tell)
    loop(1, n_f, lambda r: give_back(ret_d, table_d, s_d, r_d, r).wait_send())
    pl.semaphore_wait(ready, n_f - 1)
    loop(1, n_f, lambda r: give_back(ret_o, table_o, s_o, r_o, r).start())

    def returned(buffer, into, send, recv, r):
        home = at.ahead(n_f - r)
        return remote(
            buffer.at[aligned(r, cap_rows), :],
            into.at[aligned(home, cap_rows), :],
            send.at[r],
            recv.at[r],
            at.fsdp_peer(r),
        )

    loop(1, n_f, lambda r: returned(ret_d, table_d, s_d, r_d, r).wait_recv())

    loop(1, n_f, lambda k: send_rows(send_g, g_in, s_g, r_g, k).wait_send())
    d_mixed = send_g

    table_iota = lax.broadcasted_iota(jnp.int32, (ROWBLK, n_f * cap_rows), 1).astype(F32)

    def gather_rows(block):
        hit = (table_iota == place[block, 0:1]) | (table_iota == place[block, 1:2])
        return jnp.where(hit, 1.0, 0.0).astype(BF16)

    def norm_back(grad, value, inv_std, gain):
        scaled = grad * gain
        return inv_std * (
            scaled
            - jnp.mean(scaled, axis=-1, keepdims=True)
            - value * jnp.mean(scaled * value, axis=-1, keepdims=True)
        )

    def second_back(i):
        block = aligned(i, ROWBLK)
        grad = nn(gather_rows(block), table_d[...])
        value, inv_std = normalize(middle[block, :])
        pack[5:6, :] += jnp.sum(grad * value, axis=0, keepdims=True)
        pack[6:7, :] += jnp.sum(grad, axis=0, keepdims=True)
        total = cot[block, :].astype(F32) + norm_back(grad, value, inv_std, vecs[5:6, :])
        d_middle[block, :] = total
        low = total.astype(BF16)
        routed[block, :] = low
        pack[4:5, :] += jnp.sum(low.astype(F32), axis=0, keepdims=True)
        d_mixed[block, :] = nt(low, wfull[:, 3 * WIDTH : 4 * WIDTH]).astype(BF16)

    loop(0, SLOTS // ROWBLK, second_back)

    def e_spread(j):
        for i in range(1, n_x):
            to_x(i, j).wait_recv()
        tile = e_tile(at.core, j)
        own = aligned(at.x, part)
        total = ew[tile, own, :].astype(F32)
        for i in range(1, n_x):
            total = total + ew_x[i - 1, j].astype(F32)
        ew[tile, own, :] = total.astype(BF16)
        for i in range(1, n_x):
            all_x(i, j).start()
        to_core(0, j, at.core).start()
        to_self(j).start()

    def e_forward(j):
        for i in range(1, n_x):
            from_x(i, j).wait_recv()
            to_core(i, j, at.core).start()

    d_wo = tn(mixed[...], routed[...])
    for pair in range(PAIRS):
        hidden[WIDTH * 2 : WIDTH * 3, (4 * pair + 3) * TILE : (4 * pair + 4) * TILE] = d_wo[:, pair * TILE : (pair + 1) * TILE].astype(BF16)

    units = 16 // n_d
    pairs_in_unit = PAIRS // units

    def own_rows(owner):
        return pl.ds(pl.multiple_of(WIDTH * 2 + owner * shard, shard), shard)

    def dense(tile):
        return hidden.at[WIDTH * 2 : WIDTH * 3, aligned(tile, TILE)]

    def g_core(u, x):
        src = dense(u * n_d + x * 2 + other)
        return remote(src, dense_core.at[u, x], s_gc.at[u, x], r_gc.at[u, x], at.partner())

    def g_x(u, i):
        src = dense(u * n_d + at.x_index(i) * 2 + at.core)
        return remote(
            src, dense_x.at[u, i - 1], s_gx.at[u, i - 1], r_gx.at[u, i - 1], at.x_peer(i)
        )

    def g_f(u, k):
        src = hidden.at[own_rows(at.ahead(k)), aligned(u * n_d + at.d, TILE)]
        return remote(src, dense_f.at[u, k], s_gf.at[u, k], r_gf.at[u, k], at.fsdp_peer(k))

    def g_d(u, i):
        src = final.at[u * n_d + at.d]
        return remote(src, src, s_gd.at[u, i], r_gd.at[u, i], at.dp_peer(i))

    def g_d_from(u, i):
        dst = final.at[u * n_d + lax.rem(at.d + n_d - i, n_d)]
        return remote(dst, dst, s_gd.at[u, i], r_gd.at[u, i], at.dp_peer(i))

    def first_hop(u):
        for x in range(n_x):
            g_core(u, x).start()

    def second_hop(u):
        for x in range(n_x):
            g_core(u, x).wait_recv()
            tile = dense(u * n_d + x * 2 + at.core)
            tile[...] = (tile[...].astype(F32) + dense_core[u, x].astype(F32)).astype(BF16)
        for i in range(1, n_x):
            g_x(u, i).start()

    def third_hop(u):
        tile = dense(u * n_d + at.d)
        total = tile[...].astype(F32)
        for i in range(1, n_x):
            g_x(u, i).wait_recv()
            total = total + dense_x[u, i - 1].astype(F32)
        tile[...] = total.astype(BF16)
        loop(1, n_f, lambda k: g_f(u, k).start())

    def fourth_hop(u):
        tile = u * n_d + at.d
        dense_f[u, 0] = hidden[own_rows(at.me), aligned(tile, TILE)]
        loop(1, n_f, lambda k: g_f(u, k).wait_recv())
        total = dense_f[u, 0].astype(F32)
        for k in range(1, n_f):
            total = total + dense_f[u, k].astype(F32)
        final[tile] = total.astype(BF16)
        for i in range(1, n_d):
            g_d(u, i).start()

    hops = (first_hop, second_hop, third_hop, fourth_hop)

    def attend_back(pair):
        for b, (low, high, row) in enumerate(WINDOWS):
            window = slice(row, row + high - low)
            grad = d_mixed[b * QBLK : (b + 1) * QBLK, aligned(pair, TILE)]
            values = qkv[2 * PAIRS + pair, low:high, :]
            for h in range(2):
                one = jnp.where(halves[h], grad, jnp.zeros_like(grad))
                scores[h, window, :] = nt(values, one)
        for b, (low, high, row) in enumerate(WINDOWS):
            window = slice(row, row + high - low)
            for h in range(2):
                share = probs[2 * pair + h, window, :].astype(F32)
                moved = share * scores[h, window, :]
                moved = moved - share * jnp.sum(moved, axis=0, keepdims=True)
                d_pre[window, h * 256 : h * 256 + QBLK] = moved.astype(BF16)
        for array in (acc_k, acc_v):
            array[...] = jnp.zeros_like(array)
        for b, (low, high, row) in enumerate(WINDOWS):
            window = slice(row, row + high - low)
            block = slice(b * QBLK, (b + 1) * QBLK)
            keys = qkv[PAIRS + pair, low:high, :]
            query = qkv[pair, block, :]
            grad = d_mixed[block, aligned(pair, TILE)]
            both = [
                [
                    tn(d_pre[window, h * 256 : h * 256 + QBLK], keys),
                    nn(d_pre[window, h * 256 : h * 256 + QBLK], query),
                    nn(probs[2 * pair + h, window, :], grad),
                ]
                for h in range(2)
            ]
            d_q, d_k, d_v = [jnp.where(halves[0], one, two) for one, two in zip(*both)]
            hidden[block, pl.ds(pl.multiple_of(pair * 384, 128), 128)] = (d_q * 0.125).astype(BF16)
            acc_k[low:high, :] += d_k
            acc_v[low:high, :] += d_v
        hidden[0:SLOTS, pl.ds(pl.multiple_of(pair * 384 + 128, 128), 128)] = acc_k[...].astype(BF16)
        hidden[0:SLOTS, pl.ds(pl.multiple_of(pair * 384 + 256, 128), 128)] = acc_v[...].astype(BF16)
        d_qkv = hidden[0:SLOTS, pl.ds(pl.multiple_of(pair * 384, 128), 384)]
        sums = jnp.sum(d_qkv.astype(F32), axis=0, keepdims=True)
        pack[2:3, aligned(pair, TILE)] = sums[:, 0:128]
        pack[3:4, aligned(pair, TILE)] = sums[:, 256:384]
        d_w = tn(normed[...], d_qkv)
        for c in range(3):
            dense(4 * pair + c)[...] = d_w[:, c * TILE : (c + 1) * TILE].astype(BF16)

        @pl.when(lax.rem(pair, pairs_in_unit) == pairs_in_unit - 1)
        def _():
            unit = lax.div(pair, pairs_in_unit)
            for age, hop in enumerate(hops):

                @pl.when(unit >= age)
                def _(age=age, hop=hop):
                    hop(unit - age)

        e_spread(pair)

    acc_k, acc_v = bias.at[0:SLOTS, 0:TILE], bias.at[0:SLOTS, TILE : 2 * TILE]
    loop(0, PAIRS, attend_back)

    def later(step):
        for age, hop in enumerate(hops):
            if 0 <= step - age < units:
                hop(step - age)

    later(units)

    def first_back(i):
        block = aligned(i, ROWBLK)
        grad = nt(hidden[block, 0 : 3 * WIDTH], wfull[:, 0 : 3 * WIDTH])
        value, inv_std = normalize(tok[block, :].astype(F32))
        pack[0:1, :] += jnp.sum(grad * value, axis=0, keepdims=True)
        pack[1:2, :] += jnp.sum(grad, axis=0, keepdims=True)
        d_middle[block, :] += norm_back(grad, value, inv_std, vecs[0:1, :])

    loop(0, SLOTS // ROWBLK, first_back)
    save_tokens = pltpu.make_async_copy(d_middle.at[0:SLOTS, :], o_tokens, s_own.at[2 + n_mine])
    save_tokens.start()

    def p_dp(i):
        return remote(pack, pack_dp.at[i], s_p.at[i], r_p.at[i], at.dp_peer(i))

    for i in range(1, n_d):
        p_dp(i).start()
    later(units + 1)
    loop(0, n_mine, e_forward)

    def vec_lane(owner):
        return aligned(lax.div(owner * shard, TILE), TILE)

    def qv_lane(owner):
        return aligned(lax.div(lax.rem(owner * 2 * shard, WIDTH), TILE), TILE)

    def p_vec(k):
        src = pack_dp.at[0, 0:bias_at, vec_lane(at.ahead(k))]
        return remote(src, vec_f.at[k], s_vf.at[k], r_vf.at[k], at.fsdp_peer(k))

    def p_qv(k):
        src = pack_dp.at[0, 0:8, qv_lane(at.ahead(k))]
        return remote(src, qv_f.at[k], s_qf.at[k], r_qf.at[k], at.fsdp_peer(k))

    pack_dp[0] = pack[...]
    for i in range(1, n_d):
        p_dp(i).wait_recv()
        pack_dp[0] += pack_dp[i]
    loop(1, n_f, lambda k: [p_vec(k).start(), p_qv(k).start()])
    save_bias = pltpu.make_async_copy(
        pack_dp.at[0, bias_at : bias_at + 8, :], o_bias, s_own.at[3 + n_mine]
    )
    save_bias.start()
    later(units + 2)

    loop(1, n_f, lambda r: returned(ret_o, table_o, s_o, r_o, r).wait_recv())

    def combine(i):
        block = aligned(i, ROWBLK)
        total = middle[block, :] + nn(gather_rows(block), table_o[...])
        routed[block, :] = total.astype(BF16)

    loop(0, SLOTS // ROWBLK, combine)
    save_out = pltpu.make_async_copy(routed, o_out, s_own.at[4 + n_mine])
    save_out.start()

    loop(1, n_f, lambda k: [p_vec(k).wait_recv(), p_qv(k).wait_recv()])
    vec_f[0] = pack_dp[0, 0:bias_at, vec_lane(at.me)]
    qv_f[0] = pack_dp[0, 0:8, qv_lane(at.me)]

    def add_lanes(k):
        vec_f[0] += vec_f[k]
        qv_f[0] += qv_f[k]

    loop(1, n_f, add_lanes)
    save_vec = pltpu.make_async_copy(vec_f.at[0], o_vec, s_own.at[5 + n_mine])
    save_qv = pltpu.make_async_copy(qv_f.at[0], o_qv, s_own.at[6 + n_mine])
    save_vec.start()
    save_qv.start()
    loop(0, units, lambda u: [g_d_from(u, i).wait_recv() for i in range(1, n_d)])
    save_dense = pltpu.make_async_copy(final, o_dense, s_own.at[7 + n_mine])
    save_dense.start()

    def ended_f(k):
        send_v(k).wait_send()
        send_w(k).wait_send()
        for i in range(1, n_x):
            share_x(i, k).wait_send()
        for i in range(n_x):
            share_core(i, k).wait_send()
        give_back(ret_o, table_o, s_o, r_o, k).wait_send()
        p_vec(k).wait_send()
        p_qv(k).wait_send()

    loop(1, n_f, ended_f)

    def ended_e(j):
        to_partner(j).wait_send()
        for i in range(1, n_x):
            to_x(i, j).wait_send()
            all_x(i, j).wait_send()
        for i in range(n_x):
            to_core(i, j, at.core).wait_send()
            to_core(i, j, other).wait_recv()
        to_self(j).wait()

    loop(0, n_mine, ended_e)

    def ended_u(u):
        for x in range(n_x):
            g_core(u, x).wait_send()
        for i in range(1, n_x):
            g_x(u, i).wait_send()
        loop(1, n_f, lambda k: g_f(u, k).wait_send())
        for i in range(1, n_d):
            g_d(u, i).wait_send()

    loop(0, units, ended_u)
    for i in range(1, n_d):
        p_dp(i).wait_send()
    for copy in (save_tokens, save_bias, save_out, save_vec, save_qv, save_dense):
        copy.wait()


def block(n_f, n_d, experts, cap, cap_rows, tok, cot, cols, rows, wsh, vsh, w_in, w_out, b_in, b_out):
    vmem = pl.BlockSpec(memory_space=pltpu.VMEM)
    hbm = pl.BlockSpec(memory_space=pl.ANY)
    n_x = n_d // 2
    more_x = max(n_x - 1, 1)
    vec_rows = vsh.shape[0]
    shard = WIDTH // n_f
    table = n_f * cap_rows
    hid = w_in.shape[1]
    units = 16 // n_d
    n_mine = hid // FTILE
    pack_rows = 8 + experts + 8
    sds = jax.ShapeDtypeStruct
    vm = pltpu.VMEM
    dma = pltpu.SemaphoreType.DMA
    chunk_rows = table // CHUNKS
    pairs_of = lambda *shape: [dma(shape), dma(shape)]
    return pl.pallas_call(
        functools.partial(block_kernel, n_f, n_d, experts, cap, cap_rows),
        out_shape=(
            sds((SLOTS, WIDTH), BF16),
            sds((SLOTS, WIDTH), F32),
            sds((2 * n_mine, FTILE, WIDTH), BF16),
            sds((16, shard, TILE), BF16),
            sds((8 + experts, TILE), F32),
            sds((8, TILE), F32),
            sds((8, WIDTH), F32),
        ),
        in_specs=[vmem] * 6 + [hbm] * 2 + [vmem] * 2,
        out_specs=[hbm] * 7,
        scratch_shapes=[
            vm((WIDTH, 4 * WIDTH), BF16),
            vm((vec_rows, WIDTH), F32),
            vm((KEYS, 2 * TILE), F32),
            vm((2, KEYS, QBLK), F32),
            vm((2 * PAIRS, KEYS, QBLK), BF16),
            vm((3 * PAIRS, SLOTS, TILE), BF16),
            vm((SLOTS, WIDTH), BF16),
            vm((SLOTS, WIDTH), BF16),
            vm((SLOTS, WIDTH), F32),
            vm((SLOTS, WIDTH), BF16),
            vm((SLOTS, 8), F32),
        ]
        + [vm((table, WIDTH), BF16)] * 4
        + [
            vm((WIDTH, hid), BF16),
            vm((hid, WIDTH), BF16),
            vm((table, hid), BF16),
            vm((table, hid), BF16),
        ]
        + [vm((table, WIDTH), BF16)] * 3
        + [
            vm((2 * n_mine, FTILE, WIDTH), BF16),
            vm((n_mine, FTILE, WIDTH), BF16),
            vm((more_x, n_mine, FTILE // n_x, WIDTH), BF16),
            vm((units, n_x, WIDTH, TILE), BF16),
            vm((units, more_x, WIDTH, TILE), BF16),
            vm((units, n_f, shard, TILE), BF16),
            vm((16, shard, TILE), BF16),
            vm((pack_rows, WIDTH), F32),
            vm((n_d, pack_rows, WIDTH), F32),
            vm((n_f, 8 + experts, TILE), F32),
            vm((n_f, 8, TILE), F32),
            vm((max(2 * chunk_rows, SLOTS), WIDTH), F32),
        ]
        + pairs_of(n_f)
        + pairs_of(n_f)
        + pairs_of(more_x, n_f)
        + pairs_of(n_x, n_f)
        + pairs_of(n_f)
        + pairs_of(n_f)
        + pairs_of(n_f)
        + pairs_of(n_f)
        + pairs_of(n_mine)
        + pairs_of(more_x, n_mine)
        + pairs_of(more_x, n_mine)
        + pairs_of(n_x, n_mine)
        + pairs_of(units, n_x)
        + pairs_of(units, more_x)
        + pairs_of(units, n_f)
        + pairs_of(units, n_d)
        + pairs_of(n_d)
        + pairs_of(n_f)
        + pairs_of(n_f)
        + [dma((8 + n_mine,)), pltpu.SemaphoreType.REGULAR],
        compiler_params=pltpu.CompilerParams(
            collective_id=0, has_side_effects=True, vmem_limit_bytes=63 << 20
        ),
        name="block",
    )(tok, cot, cols, rows, wsh, vsh, w_in, w_out, b_in, b_out)


def spread(vector, n_f, me):
    size = vector.shape[-1]
    whole = jnp.tile(vector, (1,) * (vector.ndim - 1) + (n_f,))
    return jnp.where(jnp.arange(size * n_f) // size == me, whole, jnp.zeros_like(whole))


def shards(
    tokens,
    cotangent,
    segment_ids,
    pad_mask,
    expert_ids,
    priority,
    ln1_gain,
    ln1_shift,
    w_qkv,
    b_qv,
    w_o,
    b_o,
    ln2_gain,
    ln2_shift,
    w_router,
    w_in,
    b_in,
    w_out,
    b_out,
    n_f,
    n_d,
):
    me = lax.axis_index("fsdp")
    count_tok = tokens.shape[0]
    experts = w_router.shape[1]
    cap = (21 * count_tok + 10 * experts - 1) // (10 * experts)
    cap_rows = -(-cap // 16) * 16
    shard = w_qkv.shape[0]
    zero_row = jnp.zeros_like(segment_ids)
    rows = jnp.stack(
        [segment_ids, pad_mask, expert_ids[:, 0], expert_ids[:, 1], priority[0]] + [zero_row] * 3
    )
    cols = rows.T
    by_pair = w_qkv.reshape(shard, 3, PAIRS, TILE).transpose(0, 2, 1, 3).reshape(shard, -1)
    wsh = jnp.concatenate([by_pair, w_o], axis=1)
    whole = functools.partial(spread, n_f=n_f, me=me)
    vec_rows = -(-(8 + experts) // 16) * 16
    vsh = jnp.concatenate(
        [
            whole(ln1_gain)[None],
            whole(ln1_shift)[None],
            whole(b_qv).reshape(2, WIDTH),
            whole(b_o)[None],
            whole(ln2_gain)[None],
            whole(ln2_shift)[None],
            jnp.zeros((1, WIDTH), BF16),
            whole(w_router.T),
            jnp.zeros((vec_rows - 8 - experts, WIDTH), BF16),
        ]
    )
    output, d_tokens, expert_sums, dense, vec, qv, biases = block(
        n_f,
        n_d,
        experts,
        cap,
        cap_rows,
        tokens,
        cotangent,
        cols,
        rows,
        wsh,
        vsh,
        w_in[0],
        w_out[0],
        b_in,
        b_out,
    )
    n_hid = w_in.shape[2]
    d_w_in = expert_sums[0::2].transpose(1, 0, 2).reshape(1, WIDTH, n_hid).astype(F32)
    d_w_out = expert_sums[1::2].reshape(1, n_hid, WIDTH).astype(F32)
    dense = dense.reshape(PAIRS, 4, shard, TILE).astype(F32)
    d_w_qkv = dense[:, :3].transpose(2, 1, 0, 3).reshape(shard, 3 * WIDTH)
    d_w_o = dense[:, 3].transpose(1, 0, 2).reshape(shard, WIDTH)
    vec = lax.dynamic_slice_in_dim(vec, (me * shard) % TILE, shard, axis=1)
    qv = lax.dynamic_slice(qv, (2 + me * 2 * shard // WIDTH, (me * 2 * shard) % TILE), (1, 2 * shard))
    return (
        output,
        d_tokens,
        vec[0],
        vec[1],
        d_w_qkv,
        qv[0],
        d_w_o,
        vec[4],
        vec[5],
        vec[6],
        vec[8:].T,
        d_w_in,
        biases[:4].reshape(1, n_hid),
        d_w_out,
        biases[4:5],
    )


def solution(mesh):
    both, one = P(("dp", "fsdp")), P("fsdp")
    n_f, n_d = mesh.shape["fsdp"], mesh.shape["dp"]
    return jax.shard_map(
        functools.partial(shards, n_f=n_f, n_d=n_d),
        mesh=mesh,
        in_specs=(both,) * 6 + (one,) * 13,
        out_specs=(both,) * 2 + (one,) * 13,
        check_vma=False,
    )
```

time: 694 us -> 250 us (0.36); the launches traced: 682 us -> 250 us
  matrix products: 197 us -> 0 us
  waiting for transfers between devices: 190 us -> 0 us
  Pallas kernels: 76.3 us -> 209 us
  local copies, waits for them, and re-layouts: 88.8 us -> 30.4 us
  other arithmetic: 49.4 us -> 9.22 us
  blocking collectives: 32.8 us -> 0 us
  starting transfers between devices: 30.6 us -> 0 us
  between operations: 16.4 us -> 0.79 us
    dot_general x111 -> x0, matrix products: 197 us -> none  [the longest x53 107 us: nn(): return jnp.dot(left, right, preferred_element_type=F32)]
    pallas_call x1, Pallas kernels: 76.3 us -> 209 us  [block(): pl.pallas_call(functools.partial(block_kernel, n_f, n_d, experts, cap, ca...]
    scatter-add x48 -> x0, local copies, waits for them, and re-layouts: 70.5 us -> none  [the longest x24 35.3 us: shards(): dv = dv.at[low:high].add(nn(p, do))]
    unnamed x5 -> x0, waiting for transfers between devices: 61 us -> none
    reduce_scatter x2 -> x0, waiting for transfers between devices: 56.7 us -> none  [spread_sum(): lax.psum_scatter(value.astype(BF16), 'fsdp', scatter_dimension=0, tiled=T...]
    psum x1 -> x0, waiting for transfers between devices: 40.8 us -> none  [spread_sum(): return lax.psum(value, 'dp').astype(F32)]
    all_to_all x2 -> x0, waiting for transfers between devices: 31.5 us -> none  [back(): lax.all_to_all(value, 'fsdp', split_axis=0, concat_axis=0, tiled=True)]
    all_to_all x2 -> x0, starting transfers between devices: 29.8 us -> none  [back(): lax.all_to_all(value, 'fsdp', split_axis=0, concat_axis=0, tiled=True)]
  transfers between devices with their start and end apart: 6 -> 0, of which waited for: 4 -> 0; matrix products, arithmetic and copies ran while one was open for 24% -> 0% of each run, Pallas kernels for 0% -> 0%
where the time goes in v2:
time: 250 us
  Pallas kernels  209 us (84%)
  local copies, waits for them, and re-layouts  30.4 us (12%)
  other arithmetic  9.22 us (4%)
    pallas_call x1, Pallas kernels, block(): pl.pallas_call(functools.partial(block_kernel, n_f, n_d, experts, cap, ca...  209 us
    unnamed x17, local copies, waits for them, and re-layouts  7.95 us
    convert_element_type x1, local copies, waits for them, and re-layouts, shards(): expert_sums[0::2].transpose(1, 0, 2).reshape(1, WIDTH, n_hid).astype(F32)  5.25 us

profile of v2, /device:TPU:1, one launch (start us, length us, event | category | flops | bytes accessed | tf_op | source)
XLA Modules:
  0.0 249.7 jit_solution(7755908157800230337)
XLA Ops:
  0.6 0.0 copy-start
  0.7 0.7 tile.74
  1.3 0.1 tile.75
  1.4 0.7 tile.76
  2.1 0.1 tile.77
  2.2 0.7 tile.32
  2.8 0.1 tile.33
  2.9 0.7 tile.72
  3.6 0.1 tile.73
  3.7 0.7 tile.78
  4.4 0.1 tile.79
  4.5 0.7 tile.30
  5.2 0.1 tile.31
  5.2 0.0 copy-done
  5.3 1.2 concatenate.7.vsh
  6.5 0.8 slice_bitcast_fusion.3
  7.3 0.7 stack.12
  8.0 0.7 stack.13
  8.7 0.7 stack.15.rows
  9.4 0.0 copy-start.4
  9.4 0.9 copy.39.cols
  10.3 1.0 reshape.189
  11.3 0.1 copy.48
  11.4 0.2 reshape.190
  11.6 1.6 pad_maximum_fusion.wsh
  13.2 0.0 copy-done.4
  13.2 209.3 %block.1 = (bf16[720,512]{1,0:T(8,128)(2,1)}, f32[720,512]{1,0:T(8,128)}, bf16[8,512,512]{2,1,0:T(8,128)(2,1)}, bf16[16,64,128]{2,1,0:T(8,128)(2,1)}, f32[16,128...) custom-call(bf16[720,512]{1,0:T(8,128)(2,1)} %tok.1, bf16[720,512]{1,0:T(8,128)(2,1)} %cot.1, s32[720,8]{1,0:T(8,128)} %copy.39.cols, ...), custom_call_target="tpu_custom_call" | custom-call | tf_op jit(solution)/shard_map/block/pallas_call | solution.py:878
  222.5 1.5 dynamic-slice_bitcast_fusion.1
  224.0 1.3 dynamic-slice_bitcast_fusion
  225.3 1.2 dynamic-slice_bitcast_fusion.6
  226.5 4.9 %fusion.5 = (bf16[4,512,512]{2,1,0:T(8,128)(2,1)S(1)}, f32[512,4,512]{2,0,1:T(8,128)}) fusion(bf16[8,512,512]{2,1,0:T(8,128)(2,1)} %get-tuple-element.27), kind=kLoop, calls=%fused_computation.42 | loop fusion | flops 1048576 | bytes 10485760 | tf_op jit(solution)/shard_map/slice | solution.py:1029
  231.4 5.3 %copy.42 = f32[512,4,512]{0,2,1:T(8,128)} copy(f32[512,4,512]{2,0,1:T(8,128)} %get-tuple-element.45) | data formatting | bytes 8388608 | tf_op jit(solution)/shard_map/convert_element_type | solution.py:1028
  236.7 5.3 %copy.43 = f32[1,512,2048]{2,1,0:T(8,128)} copy(f32[1,512,2048]{1,2,0:T(8,128)} %bitcast.50) | data formatting | bytes 8388608
  242.0 0.0 copy-start.3
  242.0 0.0 copy-start.5
  242.0 0.0 copy-start.2
  242.0 2.6 %bitcast_convert_fusion = f32[1,2048,512]{2,1,0:T(8,128)} fusion(bf16[1,2048,512]{2,1,0:T(8,128)(2,1)S(1)} %bitcast.51), kind=kLoop, calls=%fused_computation.1 | loop fusion | flops 1048576 | bytes 6291456 | tf_op jit(solution)/shard_map/convert_element_type | solution.py:1029
  244.6 0.0 copy-done.3
  244.7 0.3 copy.40
  245.0 0.9 reshape.191
  245.9 0.7 copy_bitcast_fusion.1
  246.5 0.0 copy-done.5
  246.6 0.6 copy.45
  247.2 0.6 slice.55
  247.7 0.0 copy-done.2
  247.7 0.9 copy.51
  248.6 0.0 copy-done.1
  248.6 1.1 copy.52
  (14 shorter events, 0.2 us)
Async XLA Ops:
  0.6 4.6 %copy-start = (bf16[128]{0:T(256)(128)(2,1)S(1)}, bf16[128]{0:T(256)(128)(2,1)}, u32[]{:S(2)}) copy-start(bf16[128]{0:T(256)(128)(2,1)} %param.28) | copy-start | bytes 772
  9.4 3.7 %copy-start.4 = (s32[8,720]{1,0:T(8,128)}, s32[8,720]{1,0:T(8,128)S(1)}, u32[]{:S(2)}) copy-start(s32[8,720]{1,0:T(8,128)S(1)} %stack.15.rows) | copy-start | bytes 69124
  242.0 2.6 %copy-start.3 = (bf16[16,64,128]{2,1,0:T(8,128)(2,1)S(1)}, bf16[16,64,128]{2,1,0:T(8,128)(2,1)}, u32[]{:S(2)}) copy-start(bf16[16,64,128]{2,1,0:T(8,128)(2,1)} %get-tuple-element.25) | copy-start | bytes 786436
  242.0 4.5 %copy-start.5 = (f32[8,512]{1,0:T(8,128)S(1)}, f32[8,512]{1,0:T(8,128)}, u32[]{:S(2)}) copy-start(f32[8,512]{1,0:T(8,128)} %get-tuple-element.28) | copy-start | bytes 49156
  242.0 5.7 %copy-start.2 = (bf16[720,512]{1,0:T(8,128)(2,1)S(1)}, bf16[720,512]{1,0:T(8,128)(2,1)}, u32[]{:S(2)}) copy-start(bf16[720,512]{1,0:T(8,128)(2,1)} %get-tuple-element.72) | copy-start | bytes 2211844
  244.6 4.0 %copy-start.1 = (f32[720,512]{1,0:T(8,128)S(1)}, f32[720,512]{1,0:T(8,128)}, u32[]{:S(2)}) copy-start(f32[720,512]{1,0:T(8,128)} %get-tuple-element.73) | copy-start | bytes 4423684

commit v3 on v2

--- a/solution.py
+++ b/solution.py
@@ -111,10 +111,19 @@
     cap_rows,
     tok,
     cot,
-    cols,
-    rows,
-    wsh,
-    vsh,
+    segment,
+    pad,
+    chosen_ids,
+    priority,
+    w_qkv,
+    w_o,
+    gain_one,
+    shift_one,
+    b_qv,
+    b_o,
+    gain_two,
+    shift_two,
+    w_router,
     w_in_hbm,
     w_out_hbm,
     b_in,
@@ -127,6 +136,7 @@
     o_qv,
     o_bias,
     wfull,
+    vsh,
     vecs,
     bias,
     scores,
@@ -204,7 +214,7 @@
     at = Place(n_f, n_d)
     n_x = at.n_x
     shard = WIDTH // n_f
-    colw = wsh.shape[1] // n_d
+    colw = 4 * WIDTH // n_d
     other = 1 - at.core
 
     def cols_of(d):
@@ -223,9 +233,8 @@
     at.enter()
 
     def send_w(k):
-        return remote(
-            wsh.at[:, cols_of(at.d)], w_piece(at.me, at.d), s_w.at[k], r_w.at[k], at.fsdp_peer(k)
-        )
+        piece = w_piece(at.me, at.d)
+        return remote(piece, piece, s_w.at[k], r_w.at[k], at.fsdp_peer(k))
 
     vec_rows = vsh.shape[0]
 
@@ -243,23 +252,52 @@
         piece = w_piece(at.ahead(n_f - k), x_back(i) * 2 + at.core)
         return remote(piece, piece, s_dc.at[i, k], r_dc.at[i, k], at.partner())
 
+    own = aligned(at.me, shard)
+    for pair in range(PAIRS):
+        for c in range(3):
+            low = (3 * pair + c) * TILE
+            src = c * WIDTH + pair * TILE
+            wfull[own, low : low + TILE] = w_qkv[:, src : src + TILE]
+    wfull[own, 3 * WIDTH : 4 * WIDTH] = w_o[...]
+    loop(1, n_f, lambda k: send_w(k).start())
+
+    def placing(size, low):
+        shape = (size, WIDTH)
+        target = lax.broadcasted_iota(jnp.int32, shape, 1) + low
+        source = lax.broadcasted_iota(jnp.int32, shape, 0) + at.me * size
+        return jnp.where(target == source, 1.0, 0.0).astype(BF16)
+
+    blank = jnp.zeros((1, shard), F32)
+    stack = [
+        blank if ref is None else ref[...].astype(F32)
+        for ref in (gain_one, shift_one, None, None, b_o, gain_two, shift_two, None)
+    ]
+    spread = nn(jnp.concatenate(stack, axis=0).astype(BF16), placing(shard, 0))
+    row_iota = lax.broadcasted_iota(jnp.int32, (8, WIDTH), 0)
+    for r in range(2):
+        line = nn(b_qv[...], placing(2 * shard, r * WIDTH))
+        spread = spread + jnp.where(row_iota == 2 + r, line, 0.0)
+    router_rows = tn(w_router[...], placing(shard, 0))
+    rest = jnp.zeros((vec_rows - 8 - experts, WIDTH), F32)
+    parts = [spread, router_rows] + ([rest] if vec_rows > 8 + experts else [])
+    vsh[...] = jnp.concatenate(parts, axis=0).astype(BF16)
+    vec_piece(at.me)[...] = vsh[...]
     loop(1, n_f, lambda k: send_v(k).start())
-    loop(1, n_f, lambda k: send_w(k).start())
-    wfull[aligned(at.me, shard), :] = wsh[...]
-    vec_piece(at.me)[...] = vsh[...]
-
+
+    seg_r, pad_r, pri_r = (ref[...].astype(F32) for ref in (segment, pad, priority))
+    lines = jnp.concatenate([seg_r, pad_r, pri_r, jnp.zeros((5, SLOTS), F32)], axis=0)
+    columns = jnp.transpose(lines)
+    seg_c, pad_c, pri_c = (columns[:, j : j + 1] for j in range(3))
     expert_iota = lax.broadcasted_iota(jnp.int32, (experts, SLOTS), 0)
-    live = rows[1:2, :] > 0
-    before = jnp.where(cols[:, 4:5] < rows[4:5, :], 1.0, 0.0).astype(BF16)
-    chose = [
-        jnp.where((rows[2 + k : 3 + k, :] == expert_iota) & live, 1.0, 0.0) for k in range(2)
-    ]
+    live = pad_r > 0
+    before = jnp.where(pri_c < pri_r, 1.0, 0.0).astype(BF16)
+    chose = [jnp.where((chosen_ids[k : k + 1, :] == expert_iota) & live, 1.0, 0.0) for k in range(2)]
     rank = [nn(one.astype(BF16), before) for one in chose]
     rank[1] = rank[1] + jnp.sum(chose[0], axis=1, keepdims=True)
     spot_r = []
     for k in range(2):
         slot = jnp.sum(chose[k] * rank[k], axis=0, keepdims=True)
-        spot = rows[2 + k : 3 + k, :].astype(F32) * cap_rows + slot
+        spot = chosen_ids[k : k + 1, :].astype(F32) * cap_rows + slot
         spot_r.append(jnp.where(live & (slot < cap), spot, -1.0))
     place[...] = jnp.transpose(jnp.concatenate(spot_r + [jnp.zeros((6, SLOTS), F32)], axis=0))
     slot_iota = lax.broadcasted_iota(jnp.int32, (cap_rows, SLOTS), 0)
@@ -271,11 +309,11 @@
     for b, (low, high, row) in enumerate(WINDOWS):
         queries = slice(b * QBLK, (b + 1) * QBLK)
         shape = (high - low, QBLK)
-        same = cols[low:high, 0:1] == rows[0:1, queries]
+        same = seg_c[low:high, :] == seg_r[:, queries]
         itself = (lax.broadcasted_iota(jnp.int32, shape, 0) + low) == (
             lax.broadcasted_iota(jnp.int32, shape, 1) + b * QBLK
         )
-        allowed = same & ((cols[low:high, 1:2] > 0) | itself)
+        allowed = same & ((pad_c[low:high, :] > 0) | itself)
         bias[row : row + high - low, 0:QBLK] = jnp.where(allowed, 0.0, -1e30)
 
     loop(1, n_f, lambda k: send_v(k).wait_recv())
@@ -858,12 +896,12 @@
         copy.wait()
 
 
-def block(n_f, n_d, experts, cap, cap_rows, tok, cot, cols, rows, wsh, vsh, w_in, w_out, b_in, b_out):
+def block(n_f, n_d, experts, cap, cap_rows, small, w_in, w_out, b_in, b_out):
     vmem = pl.BlockSpec(memory_space=pltpu.VMEM)
     hbm = pl.BlockSpec(memory_space=pl.ANY)
     n_x = n_d // 2
     more_x = max(n_x - 1, 1)
-    vec_rows = vsh.shape[0]
+    vec_rows = -(-(8 + experts) // 16) * 16
     shard = WIDTH // n_f
     table = n_f * cap_rows
     hid = w_in.shape[1]
@@ -886,10 +924,11 @@
             sds((8, TILE), F32),
             sds((8, WIDTH), F32),
         ),
-        in_specs=[vmem] * 6 + [hbm] * 2 + [vmem] * 2,
+        in_specs=[vmem] * len(small) + [hbm] * 2 + [vmem] * 2,
         out_specs=[hbm] * 7,
         scratch_shapes=[
             vm((WIDTH, 4 * WIDTH), BF16),
+            vm((vec_rows, WIDTH), BF16),
             vm((vec_rows, WIDTH), F32),
             vm((KEYS, 2 * TILE), F32),
             vm((2, KEYS, QBLK), F32),
@@ -947,13 +986,120 @@
             collective_id=0, has_side_effects=True, vmem_limit_bytes=63 << 20
         ),
         name="block",
-    )(tok, cot, cols, rows, wsh, vsh, w_in, w_out, b_in, b_out)
-
-
-def spread(vector, n_f, me):
-    size = vector.shape[-1]
-    whole = jnp.tile(vector, (1,) * (vector.ndim - 1) + (n_f,))
-    return jnp.where(jnp.arange(size * n_f) // size == me, whole, jnp.zeros_like(whole))
+    )(*small, w_in, w_out, b_in, b_out)
+
+
+def finish_kernel(
+    n_f,
+    experts,
+    in_out,
+    in_tokens,
+    in_expert,
+    dense,
+    vec,
+    qv,
+    biases,
+    o_out,
+    o_tokens,
+    o_g1,
+    o_s1,
+    o_qkv,
+    o_bqv,
+    o_wo,
+    o_bo,
+    o_g2,
+    o_s2,
+    o_router,
+    o_w_in,
+    o_b_in,
+    o_w_out,
+    o_b_out,
+    low,
+    wide,
+    s_load,
+    s_save,
+):
+    me = lax.axis_index("fsdp")
+    shard = WIDTH // n_f
+    tiles = in_expert.shape[0]
+    loads = [pltpu.make_async_copy(in_expert.at[t], low.at[t], s_load.at[t]) for t in range(tiles)]
+    for load in loads:
+        load.start()
+    saves = [
+        pltpu.make_async_copy(in_out, o_out, s_save.at[tiles]),
+        pltpu.make_async_copy(in_tokens, o_tokens, s_save.at[tiles + 1]),
+    ]
+    for save in saves:
+        save.start()
+
+    def my_lanes(value, size):
+        place = lax.rem(me * size, TILE)
+        total = jnp.zeros((value.shape[0], size), F32)
+        for low_lane in range(0, TILE, size):
+            total = total + jnp.where(place == low_lane, value[:, low_lane : low_lane + size], 0.0)
+        return total
+
+    own = my_lanes(vec[...], shard)
+    for row, ref in ((0, o_g1), (1, o_s1), (4, o_bo), (5, o_g2), (6, o_s2)):
+        ref[...] = own[row : row + 1, :]
+    o_router[...] = jnp.transpose(own[8 : 8 + experts, :])
+    lines = my_lanes(qv[...], 2 * shard)
+    o_bqv[...] = jnp.where(me * 2 * shard < WIDTH, lines[2:3, :], lines[3:4, :])
+    for pair in range(PAIRS):
+        for c in range(3):
+            at = c * WIDTH + pair * TILE
+            o_qkv[:, at : at + TILE] = dense[4 * pair + c].astype(F32)
+        o_wo[:, pair * TILE : (pair + 1) * TILE] = dense[4 * pair + 3].astype(F32)
+    for f in range(tiles // 2):
+        o_b_in[:, f * FTILE : (f + 1) * FTILE] = biases[f : f + 1, :]
+    o_b_out[...] = biases[4:5, :]
+    for t in range(tiles):
+        loads[t].wait()
+        wide[t] = low[t].astype(F32)
+        piece = pl.ds(t // 2 * FTILE, FTILE)
+        dst = o_w_out.at[0, piece, :] if t % 2 else o_w_in.at[0, :, piece]
+        saves.append(pltpu.make_async_copy(wide.at[t], dst, s_save.at[t]))
+        saves[-1].start()
+    for save in saves:
+        save.wait()
+
+
+def finish(n_f, experts, hid, parts):
+    vmem = pl.BlockSpec(memory_space=pltpu.VMEM)
+    hbm = pl.BlockSpec(memory_space=pl.ANY)
+    shard = WIDTH // n_f
+    tiles = parts[2].shape[0]
+    line = lambda *shape: jax.ShapeDtypeStruct(shape, F32)
+    return pl.pallas_call(
+        functools.partial(finish_kernel, n_f, experts),
+        out_shape=(
+            jax.ShapeDtypeStruct((SLOTS, WIDTH), BF16),
+            line(SLOTS, WIDTH),
+            line(1, shard),
+            line(1, shard),
+            line(shard, 3 * WIDTH),
+            line(1, 2 * shard),
+            line(shard, WIDTH),
+            line(1, shard),
+            line(1, shard),
+            line(1, shard),
+            line(shard, experts),
+            line(1, WIDTH, hid),
+            line(1, hid),
+            line(1, hid, WIDTH),
+            line(1, WIDTH),
+        ),
+        in_specs=[hbm] * 3 + [vmem] * 4,
+        out_specs=[hbm] * 2 + [vmem] * 9 + [hbm, vmem, hbm, vmem],
+        scratch_shapes=[
+            pltpu.VMEM((tiles, FTILE, WIDTH), BF16),
+            pltpu.VMEM((tiles, FTILE, WIDTH), F32),
+            pltpu.SemaphoreType.DMA((tiles,)),
+            pltpu.SemaphoreType.DMA((tiles + 2,)),
+        ],
+        compiler_params=pltpu.CompilerParams(vmem_limit_bytes=62 << 20),
+        name="finish",
+    )(*parts)
 
 
 def shards(
@@ -979,76 +1125,31 @@
     n_f,
     n_d,
 ):
-    me = lax.axis_index("fsdp")
-    count_tok = tokens.shape[0]
     experts = w_router.shape[1]
-    cap = (21 * count_tok + 10 * experts - 1) // (10 * experts)
+    cap = (21 * tokens.shape[0] + 10 * experts - 1) // (10 * experts)
     cap_rows = -(-cap // 16) * 16
-    shard = w_qkv.shape[0]
-    zero_row = jnp.zeros_like(segment_ids)
-    rows = jnp.stack(
-        [segment_ids, pad_mask, expert_ids[:, 0], expert_ids[:, 1], priority[0]] + [zero_row] * 3
-    )
-    cols = rows.T
-    by_pair = w_qkv.reshape(shard, 3, PAIRS, TILE).transpose(0, 2, 1, 3).reshape(shard, -1)
-    wsh = jnp.concatenate([by_pair, w_o], axis=1)
-    whole = functools.partial(spread, n_f=n_f, me=me)
-    vec_rows = -(-(8 + experts) // 16) * 16
-    vsh = jnp.concatenate(
-        [
-            whole(ln1_gain)[None],
-            whole(ln1_shift)[None],
-            whole(b_qv).reshape(2, WIDTH),
-            whole(b_o)[None],
-            whole(ln2_gain)[None],
-            whole(ln2_shift)[None],
-            jnp.zeros((1, WIDTH), BF16),
-            whole(w_router.T),
-            jnp.zeros((vec_rows - 8 - experts, WIDTH), BF16),
-        ]
-    )
-    output, d_tokens, expert_sums, dense, vec, qv, biases = block(
-        n_f,
-        n_d,
-        experts,
-        cap,
-        cap_rows,
+    line = lambda vector: vector.reshape(1, -1)
+    small = (
         tokens,
         cotangent,
-        cols,
-        rows,
-        wsh,
-        vsh,
-        w_in[0],
-        w_out[0],
-        b_in,
-        b_out,
+        line(segment_ids),
+        line(pad_mask),
+        expert_ids.T,
+        priority,
+        w_qkv,
+        w_o,
+        line(ln1_gain),
+        line(ln1_shift),
+        line(b_qv),
+        line(b_o),
+        line(ln2_gain),
+        line(ln2_shift),
+        w_router,
     )
-    n_hid = w_in.shape[2]
-    d_w_in = expert_sums[0::2].transpose(1, 0, 2).reshape(1, WIDTH, n_hid).astype(F32)
-    d_w_out = expert_sums[1::2].reshape(1, n_hid, WIDTH).astype(F32)
-    dense = dense.reshape(PAIRS, 4, shard, TILE).astype(F32)
-    d_w_qkv = dense[:, :3].transpose(2, 1, 0, 3).reshape(shard, 3 * WIDTH)
-    d_w_o = dense[:, 3].transpose(1, 0, 2).reshape(shard, WIDTH)
-    vec = lax.dynamic_slice_in_dim(vec, (me * shard) % TILE, shard, axis=1)
-    qv = lax.dynamic_slice(qv, (2 + me * 2 * shard // WIDTH, (me * 2 * shard) % TILE), (1, 2 * shard))
-    return (
-        output,
-        d_tokens,
-        vec[0],
-        vec[1],
-        d_w_qkv,
-        qv[0],
-        d_w_o,
-        vec[4],
-        vec[5],
-        vec[6],
-        vec[8:].T,
-        d_w_in,
-        biases[:4].reshape(1, n_hid),
-        d_w_out,
-        biases[4:5],
-    )
+    parts = block(n_f, n_d, experts, cap, cap_rows, small, w_in[0], w_out[0], b_in, b_out)
+    done = finish(n_f, experts, w_in.shape[2], parts)
+    flat = (2, 3, 5, 7, 8, 9)
+    return tuple(value.reshape(-1) if i in flat else value for i, value in enumerate(done))
 
 
 def solution(mesh):

time: 250 us -> 275 us (1.10)
  Pallas kernels: 209 us -> 268 us
  local copies, waits for them, and re-layouts: 30.4 us -> 5.32 us
  other arithmetic: 9.22 us -> 0 us
    pallas_call x0 -> x1, Pallas kernels: none -> 70.1 us  [finish(): pl.pallas_call(functools.partial(finish_kernel, n_f, experts), out_shape=...]
    pallas_call x1, Pallas kernels: 209 us -> 198 us  [block(): pl.pallas_call(functools.partial(block_kernel, n_f, n_d, experts, cap, ca...]
    another operation x20 -> x0, local copies, waits for them, and re-layouts: 7.39 us -> none  [the longest x13 4.5 us: spread(): whole = jnp.tile(vector, (1,) * (vector.ndim - 1) + (n_f,))]
    convert_element_type x1 -> x0, local copies, waits for them, and re-layouts: 5.25 us -> none  [shards(): expert_sums[0::2].transpose(1, 0, 2).reshape(1, WIDTH, n_hid).astype(F32)]
    unnamed x17 -> x2, local copies, waits for them, and re-layouts: 7.95 us -> 2.79 us
    slice x1 -> x0, other arithmetic: 4.93 us -> none  [shards(): d_w_out = expert_sums[1::2].reshape(1, n_hid, WIDTH).astype(F32)]
where the time goes in v3:
time: 275 us; the launch traced here: 274 us
  Pallas kernels  268 us (97%)
  local copies, waits for them, and re-layouts  5.32 us (2%)
    pallas_call x1, Pallas kernels, block(): pl.pallas_call(functools.partial(block_kernel, n_f, n_d, experts, cap, ca...  198 us
    pallas_call x1, Pallas kernels, finish(): pl.pallas_call(functools.partial(finish_kernel, n_f, experts), out_shape=...  70.1 us

profile of v3, /device:TPU:1, one launch (start us, length us, event | category | flops | bytes accessed | tf_op | source)
XLA Modules:
  0.0 273.8 jit_solution(7964603998707847483)
XLA Ops:
  0.6 1.3 reshape.72.segment
  1.9 1.3 reshape.73.pad
  3.2 1.4 copy.34.w_router
  4.6 197.7 %block.1 = (bf16[720,512]{1,0:T(8,128)(2,1)}, f32[720,512]{1,0:T(8,128)}, bf16[8,512,512]{2,1,0:T(8,128)(2,1)}, bf16[16,64,128]{2,1,0:T(8,128)(2,1)}, f32[16,128...) custom-call(bf16[720,512]{1,0:T(8,128)(2,1)} %tok.1, bf16[720,512]{1,0:T(8,128)(2,1)} %cot.1, ...), custom_call_target="tpu_custom_call" | custom-call | tf_op jit(solution)/shard_map/block/pallas_call | solution.py:916
  202.3 70.1 %finish.1 = (bf16[720,512]{1,0:T(8,128)(2,1)}, f32[720,512]{1,0:T(8,128)}, f32[1,64]{1,0:T(1,128)}, f32[1,64]{1,0:T(1,128)}, f32[64,1536]{1,0:T(8,128)}, /*index...) custom-call(bf16[720,512]{1,0:T(8,128)(2,1)} %get-tuple-element.37.i, ...), custom_call_target="tpu_custom_call" | custom-call | tf_op jit(solution)/shard_map/finish/pallas_call | solution.py:1073
  272.4 1.4 copy.35

commit v4 on v3

--- a/solution.py
+++ b/solution.py
@@ -21,6 +21,7 @@
 TILE = 128
 FTILE = 512
 CHUNKS = 4
+LOTS = 7
 
 
 def nt(left, right):
@@ -209,6 +210,7 @@
     s_qf,
     r_qf,
     s_own,
+    s_self,
     ready,
 ):
     at = Place(n_f, n_d)
@@ -232,9 +234,27 @@
     load_out.start()
     at.enter()
 
-    def send_w(k):
+    n_y = 1 << ((n_f.bit_length() - 1) // 2)
+    n_z = n_f // n_y
+    my_z, my_y = lax.div(at.me, n_y), lax.rem(at.me, n_y)
+
+    def member(z, y):
+        return lax.rem(my_z + z, n_z) * n_y + lax.rem(my_y + y, n_y)
+
+    def owner(k):
+        return member(n_z - lax.rem(k, n_z), n_y - lax.div(k, n_z))
+
+    def along_z(k):
         piece = w_piece(at.me, at.d)
-        return remote(piece, piece, s_w.at[k], r_w.at[k], at.fsdp_peer(k))
+        return remote(piece, piece, s_w.at[k], r_w.at[k], (at.d, member(k, 0)))
+
+    def along_y(j, i):
+        piece, k = w_piece(member(n_z - i, 0), at.d), j * n_z + i
+        return remote(piece, piece, s_w.at[k], r_w.at[k], (at.d, member(0, j)))
+
+    def got_w(k):
+        piece = w_piece(owner(k), at.d)
+        return remote(piece, piece, s_w.at[k], r_w.at[k], (at.d, at.me))
 
     vec_rows = vsh.shape[0]
 
@@ -245,11 +265,11 @@
         return remote(vsh, vec_piece(at.me), s_v.at[k], r_v.at[k], at.fsdp_peer(k))
 
     def share_x(i, k):
-        piece = w_piece(at.ahead(n_f - k), at.d)
+        piece = w_piece(owner(k), at.d)
         return remote(piece, piece, s_dx.at[i - 1, k], r_dx.at[i - 1, k], at.x_peer(i))
 
     def share_core(i, k):
-        piece = w_piece(at.ahead(n_f - k), x_back(i) * 2 + at.core)
+        piece = w_piece(owner(k), x_back(i) * 2 + at.core)
         return remote(piece, piece, s_dc.at[i, k], r_dc.at[i, k], at.partner())
 
     own = aligned(at.me, shard)
@@ -259,7 +279,8 @@
             src = c * WIDTH + pair * TILE
             wfull[own, low : low + TILE] = w_qkv[:, src : src + TILE]
     wfull[own, 3 * WIDTH : 4 * WIDTH] = w_o[...]
-    loop(1, n_f, lambda k: send_w(k).start())
+    loop(1, n_z, lambda k: along_z(k).start())
+    loop(1, n_y, lambda j: along_y(j, 0).start())
 
     def placing(size, low):
         shape = (size, WIDTH)
@@ -277,7 +298,7 @@
     for r in range(2):
         line = nn(b_qv[...], placing(2 * shard, r * WIDTH))
         spread = spread + jnp.where(row_iota == 2 + r, line, 0.0)
-    router_rows = tn(w_router[...], placing(shard, 0))
+    router_rows = nn(w_router[...], placing(shard, 0))
     rest = jnp.zeros((vec_rows - 8 - experts, WIDTH), F32)
     parts = [spread, router_rows] + ([rest] if vec_rows > 8 + experts else [])
     vsh[...] = jnp.concatenate(parts, axis=0).astype(BF16)
@@ -316,31 +337,11 @@
         allowed = same & ((pad_c[low:high, :] > 0) | itself)
         bias[row : row + high - low, 0:QBLK] = jnp.where(allowed, 0.0, -1e30)
 
-    loop(1, n_f, lambda k: send_v(k).wait_recv())
-    vecs[...] = vec_piece(0)[...].astype(F32)
-
-    def add_vectors(owner):
-        vecs[...] += vec_piece(owner)[...].astype(F32)
-
-    loop(1, n_f, add_vectors)
-
-    def first_norm(i):
-        block = aligned(i, ROWBLK)
-        value, _ = normalize(tok[block, :].astype(F32))
-        normed[block, :] = (value * vecs[0:1, :] + vecs[1:2, :]).astype(BF16)
-
-    loop(0, SLOTS // ROWBLK, first_norm)
-
-    def pass_on(k):
-        send_w(k).wait_recv()
-        for i in range(1, n_x):
-            share_x(i, k).start()
-        share_core(0, k).start()
-
-    loop(1, n_f, pass_on)
-
-    def order(step):
-        return 1 + lax.rem(2 * n_f - 4 - step, n_f - 1)
+    chunk_rows = n_f * cap_rows // CHUNKS
+    sources = n_f // CHUNKS
+
+    def position(step):
+        return lax.rem(2 * step, 3) + 3 * lax.div(step, 3)
 
     def send_rows(buffer, into, send, recv, k):
         return remote(
@@ -352,21 +353,61 @@
         )
 
     def dispatch(source, buffer, into, send, recv):
-        def one(step):
-            k = order(step)
-            expert = at.ahead(k)
-            buffer[aligned(expert, cap_rows), :] = nn(pick(expert), source[...]).astype(BF16)
-            send_rows(buffer, into, send, recv, k).start()
-
-        loop(0, n_f - 1, one)
         into[0:cap_rows, :] = nn(pick(at.me), source[...]).astype(BF16)
 
+        def stage(step):
+            first = position(step) * sources
+
+            def one(r):
+                @pl.when(r > 0)
+                def _():
+                    k = n_f - r
+                    expert = at.ahead(k)
+                    rows = nn(pick(expert), source[...]).astype(BF16)
+                    buffer[aligned(expert, cap_rows), :] = rows
+                    send_rows(buffer, into, send, recv, k).start()
+
+            loop(first, first + sources, one)
+
+        loop(0, CHUNKS, stage)
+
+    def pass_on(k):
+        for i in range(1, n_x):
+            share_x(i, k).start()
+        share_core(0, k).start()
+
+    def from_z(k):
+        got_w(k).wait_recv()
+        loop(1, n_y, lambda j: along_y(j, k).start())
+        pass_on(k)
+
+    def from_y(k):
+        got_w(k).wait_recv()
+        pass_on(k)
+
+    loop(1, n_z, from_z)
     dispatch(cot, send_g, g_in, s_g, r_g)
+    loop(n_z, n_f, from_y)
+
+    loop(1, n_f, lambda k: send_v(k).wait_recv())
+    vecs[...] = vec_piece(0)[...].astype(F32)
+
+    def add_vectors(owner):
+        vecs[...] += vec_piece(owner)[...].astype(F32)
+
+    loop(1, n_f, add_vectors)
+
+    def first_norm(i):
+        block = aligned(i, ROWBLK)
+        value, _ = normalize(tok[block, :].astype(F32))
+        normed[block, :] = (value * vecs[0:1, :] + vecs[1:2, :]).astype(BF16)
+
+    loop(0, SLOTS // ROWBLK, first_norm)
 
     for i in range(1, n_x):
 
         def cross(k, i=i):
-            piece = w_piece(at.ahead(n_f - k), x_back(i) * 2 + at.core)
+            piece = w_piece(owner(k), x_back(i) * 2 + at.core)
             remote(piece, piece, s_dx.at[i - 1, k], r_dx.at[i - 1, k], at.x_peer(i)).wait_recv()
             share_core(i, k).start()
 
@@ -374,7 +415,7 @@
     for i in range(n_x):
 
         def arrive(k, i=i):
-            piece = w_piece(at.ahead(n_f - k), x_back(i) * 2 + other)
+            piece = w_piece(owner(k), x_back(i) * 2 + other)
             remote(piece, piece, s_dc.at[i, k], r_dc.at[i, k], at.partner()).wait_recv()
 
         loop(1, n_f, arrive)
@@ -431,8 +472,6 @@
     load_out.wait()
     pack[...] = jnp.zeros_like(pack)
     router = vecs[8 : 8 + experts, :].astype(BF16)
-    chunk_rows = n_f * cap_rows // CHUNKS
-    sources = n_f // CHUNKS
     f_tiles = w_in.shape[1] // FTILE
     bias_at = 8 + experts
     hot = jnp.where(lax.broadcasted_iota(jnp.int32, (1, experts), 1) == at.me, 1.0, 0.0)
@@ -449,7 +488,7 @@
     acc_o, acc_d = d_middle.at[0:chunk_rows, :], d_middle.at[chunk_rows : 2 * chunk_rows, :]
 
     def expert_chunk(step):
-        pos = lax.rem(step + 1, CHUNKS)
+        pos = position(step)
         block = aligned(pos, chunk_rows)
         first = pos * sources
 
@@ -522,26 +561,25 @@
         return e_tile(core, j), aligned(x, part)
 
     def all_x(i, j):
-        tile, mine = e_part(at.core, j, at.x)
-        src, dst = ew.at[tile, mine, :], o_expert.at[tile, mine, :]
+        src = ew.at[e_tile(at.core, j), aligned(at.x, part), :]
+        dst = ew_core.at[j, aligned(at.x, part), :]
         return remote(src, dst, s_ea.at[i - 1, j], r_ea.at[i - 1, j], at.x_peer(i))
 
     def from_x(i, j):
-        tile, theirs = e_part(at.core, j, x_back(i))
-        dst = o_expert.at[tile, theirs, :]
+        dst = ew_core.at[j, aligned(x_back(i), part), :]
         return remote(dst, dst, s_ea.at[i - 1, j], r_ea.at[i - 1, j], at.x_peer(i))
 
+    def e_result(i, j):
+        piece = aligned(x_back(i), part)
+        return ew.at[e_tile(at.core, j), piece, :] if i == 0 else ew_core.at[j, piece, :]
+
     def to_core(i, j, core):
-        tile, piece = e_part(core, j, x_back(i))
-        dst = o_expert.at[tile, piece, :]
-        src = ew.at[tile, piece, :] if i == 0 else dst
-        return remote(src, dst, s_eb.at[i, j], r_eb.at[i, j], at.partner())
-
-    def to_self(j):
-        tile, mine = e_part(at.core, j, at.x)
-        return pltpu.make_async_copy(
-            ew.at[tile, mine, :], o_expert.at[tile, mine, :], s_own.at[2 + j]
-        )
+        dst = o_expert.at[e_tile(core, j), aligned(x_back(i), part), :]
+        return remote(e_result(i, j), dst, s_eb.at[i, j], r_eb.at[i, j], at.partner())
+
+    def to_self(i, j):
+        dst = o_expert.at[e_tile(at.core, j), aligned(x_back(i), part), :]
+        return pltpu.make_async_copy(e_result(i, j), dst, s_self.at[i, j])
 
     n_mine = 2 * per_core
 
@@ -555,9 +593,6 @@
         grad_tiles(other, f)
         to_partner(2 * f).start()
         to_partner(2 * f + 1).start()
-
-    loop(0, per_core, theirs)
-    loop(0, per_core, lambda f: grad_tiles(at.core, f))
 
     def sum_cores(j):
         to_partner(j).wait_recv()
@@ -566,7 +601,13 @@
         for i in range(1, n_x):
             to_x(i, j).start()
 
-    loop(0, n_mine, sum_cores)
+    def tile_row(f):
+        theirs(f)
+        grad_tiles(at.core, f)
+        sum_cores(2 * f)
+        sum_cores(2 * f + 1)
+
+    loop(0, per_core, tile_row)
 
     table_o = send_x
 
@@ -580,9 +621,16 @@
         pl.semaphore_signal(ready, inc=1, device_id=at.fsdp_peer(k), device_id_type=MESH)
 
     loop(1, n_f, tell)
-    loop(1, n_f, lambda r: give_back(ret_d, table_d, s_d, r_d, r).wait_send())
     pl.semaphore_wait(ready, n_f - 1)
-    loop(1, n_f, lambda r: give_back(ret_o, table_o, s_o, r_o, r).start())
+
+    def send_lot(lot):
+        def one(step):
+            r = 1 + lax.rem(n_f // 2 - 1 + step, n_f - 1)
+            give_back(ret_o, table_o, s_o, r_o, r).start()
+
+        loop(lax.div((n_f - 1) * lot, LOTS), lax.div((n_f - 1) * (lot + 1), LOTS), one)
+
+    loop(0, 2, send_lot)
 
     def returned(buffer, into, send, recv, r):
         home = at.ahead(n_f - r)
@@ -594,6 +642,27 @@
             at.fsdp_peer(r),
         )
 
+    def e_spread(j):
+        for i in range(1, n_x):
+            to_x(i, j).wait_recv()
+        tile = e_tile(at.core, j)
+        own = aligned(at.x, part)
+        total = ew[tile, own, :].astype(F32)
+        for i in range(1, n_x):
+            total = total + ew_x[i - 1, j].astype(F32)
+        ew[tile, own, :] = total.astype(BF16)
+        for i in range(1, n_x):
+            all_x(i, j).start()
+        to_core(0, j, at.core).start()
+        to_self(0, j).start()
+
+    def e_forward(j):
+        for i in range(1, n_x):
+            from_x(i, j).wait_recv()
+            to_core(i, j, at.core).start()
+            to_self(i, j).start()
+
+    loop(0, n_mine // 2, e_spread)
     loop(1, n_f, lambda r: returned(ret_d, table_d, s_d, r_d, r).wait_recv())
 
     loop(1, n_f, lambda k: send_rows(send_g, g_in, s_g, r_g, k).wait_send())
@@ -627,25 +696,6 @@
         d_mixed[block, :] = nt(low, wfull[:, 3 * WIDTH : 4 * WIDTH]).astype(BF16)
 
     loop(0, SLOTS // ROWBLK, second_back)
-
-    def e_spread(j):
-        for i in range(1, n_x):
-            to_x(i, j).wait_recv()
-        tile = e_tile(at.core, j)
-        own = aligned(at.x, part)
-        total = ew[tile, own, :].astype(F32)
-        for i in range(1, n_x):
-            total = total + ew_x[i - 1, j].astype(F32)
-        ew[tile, own, :] = total.astype(BF16)
-        for i in range(1, n_x):
-            all_x(i, j).start()
-        to_core(0, j, at.core).start()
-        to_self(j).start()
-
-    def e_forward(j):
-        for i in range(1, n_x):
-            from_x(i, j).wait_recv()
-            to_core(i, j, at.core).start()
 
     d_wo = tn(mixed[...], routed[...])
     for pair in range(PAIRS):
@@ -770,7 +820,12 @@
                 def _(age=age, hop=hop):
                     hop(unit - age)
 
-        e_spread(pair)
+        send_lot(pair + 2)
+
+        @pl.when(pair == 1)
+        def _():
+            loop(n_mine // 2, n_mine - 1, e_spread)
+
 
     acc_k, acc_v = bias.at[0:SLOTS, 0:TILE], bias.at[0:SLOTS, TILE : 2 * TILE]
     loop(0, PAIRS, attend_back)
@@ -781,6 +836,7 @@
                 hop(step - age)
 
     later(units)
+    send_lot(PAIRS + 2)
 
     def first_back(i):
         block = aligned(i, ROWBLK)
@@ -800,7 +856,8 @@
     for i in range(1, n_d):
         p_dp(i).start()
     later(units + 1)
-    loop(0, n_mine, e_forward)
+    e_spread(n_mine - 1)
+    loop(0, n_mine - 1, e_forward)
 
     def vec_lane(owner):
         return aligned(lax.div(owner * shard, TILE), TILE)
@@ -826,6 +883,7 @@
     )
     save_bias.start()
     later(units + 2)
+    e_forward(n_mine - 1)
 
     loop(1, n_f, lambda r: returned(ret_o, table_o, s_o, r_o, r).wait_recv())
 
@@ -857,11 +915,12 @@
 
     def ended_f(k):
         send_v(k).wait_send()
-        send_w(k).wait_send()
+        got_w(k).wait_send()
         for i in range(1, n_x):
             share_x(i, k).wait_send()
         for i in range(n_x):
             share_core(i, k).wait_send()
+        give_back(ret_d, table_d, s_d, r_d, k).wait_send()
         give_back(ret_o, table_o, s_o, r_o, k).wait_send()
         p_vec(k).wait_send()
         p_qv(k).wait_send()
@@ -876,7 +935,7 @@
         for i in range(n_x):
             to_core(i, j, at.core).wait_send()
             to_core(i, j, other).wait_recv()
-        to_self(j).wait()
+            to_self(i, j).wait()
 
     loop(0, n_mine, ended_e)
 
@@ -981,7 +1040,7 @@
         + pairs_of(n_d)
         + pairs_of(n_f)
         + pairs_of(n_f)
-        + [dma((8 + n_mine,)), pltpu.SemaphoreType.REGULAR],
+        + [dma((8 + n_mine,)), dma((n_x, n_mine)), pltpu.SemaphoreType.REGULAR],
         compiler_params=pltpu.CompilerParams(
             collective_id=0, has_side_effects=True, vmem_limit_bytes=63 << 20
         ),
@@ -1016,6 +1075,8 @@
     o_b_out,
     low,
     wide,
+    rows_low,
+    rows_wide,
     s_load,
     s_save,
 ):
@@ -1025,12 +1086,12 @@
     loads = [pltpu.make_async_copy(in_expert.at[t], low.at[t], s_load.at[t]) for t in range(tiles)]
     for load in loads:
         load.start()
-    saves = [
-        pltpu.make_async_copy(in_out, o_out, s_save.at[tiles]),
-        pltpu.make_async_copy(in_tokens, o_tokens, s_save.at[tiles + 1]),
+    rows_in = [
+        pltpu.make_async_copy(in_out, rows_low, s_load.at[tiles]),
+        pltpu.make_async_copy(in_tokens, rows_wide, s_load.at[tiles + 1]),
     ]
-    for save in saves:
-        save.start()
+    for load in rows_in:
+        load.start()
 
     def my_lanes(value, size):
         place = lax.rem(me * size, TILE)
@@ -1042,7 +1103,7 @@
     own = my_lanes(vec[...], shard)
     for row, ref in ((0, o_g1), (1, o_s1), (4, o_bo), (5, o_g2), (6, o_s2)):
         ref[...] = own[row : row + 1, :]
-    o_router[...] = jnp.transpose(own[8 : 8 + experts, :])
+    o_router[...] = own[8 : 8 + experts, :]
     lines = my_lanes(qv[...], 2 * shard)
     o_bqv[...] = jnp.where(me * 2 * shard < WIDTH, lines[2:3, :], lines[3:4, :])
     for pair in range(PAIRS):
@@ -1053,6 +1114,7 @@
     for f in range(tiles // 2):
         o_b_in[:, f * FTILE : (f + 1) * FTILE] = biases[f : f + 1, :]
     o_b_out[...] = biases[4:5, :]
+    saves = []
     for t in range(tiles):
         loads[t].wait()
         wide[t] = low[t].astype(F32)
@@ -1060,7 +1122,14 @@
         dst = o_w_out.at[0, piece, :] if t % 2 else o_w_in.at[0, :, piece]
         saves.append(pltpu.make_async_copy(wide.at[t], dst, s_save.at[t]))
         saves[-1].start()
-    for save in saves:
+    rows_out = [
+        pltpu.make_async_copy(rows_low, o_out, s_save.at[tiles]),
+        pltpu.make_async_copy(rows_wide, o_tokens, s_save.at[tiles + 1]),
+    ]
+    for load, save in zip(rows_in, rows_out):
+        load.wait()
+        save.start()
+    for save in saves + rows_out:
         save.wait()
 
 
@@ -1083,7 +1152,7 @@
             line(1, shard),
             line(1, shard),
             line(1, shard),
-            line(shard, experts),
+            line(experts, shard),
             line(1, WIDTH, hid),
             line(1, hid),
             line(1, hid, WIDTH),
@@ -1094,7 +1163,9 @@
         scratch_shapes=[
             pltpu.VMEM((tiles, FTILE, WIDTH), BF16),
             pltpu.VMEM((tiles, FTILE, WIDTH), F32),
-            pltpu.SemaphoreType.DMA((tiles,)),
+            pltpu.VMEM((SLOTS, WIDTH), BF16),
+            pltpu.VMEM((SLOTS, WIDTH), F32),
+            pltpu.SemaphoreType.DMA((tiles + 2,)),
             pltpu.SemaphoreType.DMA((tiles + 2,)),
         ],
         compiler_params=pltpu.CompilerParams(vmem_limit_bytes=62 << 20),
@@ -1144,12 +1215,14 @@
         line(b_o),
         line(ln2_gain),
         line(ln2_shift),
-        w_router,
+        w_router.T,
     )
     parts = block(n_f, n_d, experts, cap, cap_rows, small, w_in[0], w_out[0], b_in, b_out)
     done = finish(n_f, experts, w_in.shape[2], parts)
     flat = (2, 3, 5, 7, 8, 9)
-    return tuple(value.reshape(-1) if i in flat else value for i, value in enumerate(done))
+    done = [value.reshape(-1) if i in flat else value for i, value in enumerate(done)]
+    done[10] = done[10].T
+    return tuple(done)
 
 
 def solution(mesh):

time: 275 us -> 204 us (0.74)
  Pallas kernels: 268 us -> 200 us
  local copies, waits for them, and re-layouts: 5.32 us -> 2.53 us
    pallas_call x1, Pallas kernels: 70.1 us -> 7.9 us  [finish(): pl.pallas_call(functools.partial(finish_kernel, n_f, experts), out_shape=...]
    pallas_call x1, Pallas kernels: 198 us -> 192 us  [block(): pl.pallas_call(functools.partial(block_kernel, n_f, n_d, experts, cap, ca...]
    unnamed x2 -> x0, local copies, waits for them, and re-layouts: 2.79 us -> none
where the time goes in v4:
time: 204 us; the launch traced here: 203 us
  Pallas kernels  200 us (98%)
  local copies, waits for them, and re-layouts  2.53 us (1%)
    pallas_call x1, Pallas kernels, block(): pl.pallas_call(functools.partial(block_kernel, n_f, n_d, experts, cap, ca...  192 us
    pallas_call x1, Pallas kernels, finish(): pl.pallas_call(functools.partial(finish_kernel, n_f, experts), out_shape=...  7.9 us

profile of v4, /device:TPU:1, one launch (start us, length us, event | category | flops | bytes accessed | tf_op | source)
XLA Modules:
  0.0 203.4 jit_solution(2436130100090187596)
XLA Ops:
  0.6 1.3 reshape.72.segment
  1.9 1.3 reshape.73.pad
  3.2 192.1 %block.1 = (bf16[720,512]{1,0:T(8,128)(2,1)}, f32[720,512]{1,0:T(8,128)}, bf16[8,512,512]{2,1,0:T(8,128)(2,1)}, bf16[16,64,128]{2,1,0:T(8,128)(2,1)}, f32[16,128...) custom-call(bf16[720,512]{1,0:T(8,128)(2,1)} %tok.1, bf16[720,512]{1,0:T(8,128)(2,1)} %cot.1, ...), custom_call_target="tpu_custom_call" | custom-call | tf_op jit(solution)/shard_map/block/pallas_call | solution.py:975
  195.3 7.9 %finish.1 = (bf16[720,512]{1,0:T(8,128)(2,1)}, f32[720,512]{1,0:T(8,128)}, f32[1,64]{1,0:T(1,128)}, f32[1,64]{1,0:T(1,128)}, f32[64,1536]{1,0:T(8,128)}, /*index...) custom-call(bf16[720,512]{1,0:T(8,128)(2,1)} %get-tuple-element.37.i, ...), custom_call_target="tpu_custom_call" | custom-call | tf_op jit(solution)/shard_map/finish/pallas_call | solution.py:1142

commit v5 on v4

--- a/solution.py
+++ b/solution.py
@@ -102,6 +102,10 @@
         return carry
 
     lax.fori_loop(low, high, step, 0)
+
+
+def y_members(n_f):
+    return 1 << ((n_f.bit_length() - 1) // 2)
 
 
 def block_kernel(
@@ -163,8 +167,10 @@
     ew_core,
     ew_x,
     dense_core,
+    dense_y,
+    dense_z,
+    dense_s,
     dense_x,
-    dense_f,
     final,
     pack,
     pack_dp,
@@ -197,10 +203,12 @@
     r_eb,
     s_gc,
     r_gc,
+    s_gy,
+    r_gy,
+    s_gz,
+    r_gz,
     s_gx,
     r_gx,
-    s_gf,
-    r_gf,
     s_gd,
     r_gd,
     s_p,
@@ -234,7 +242,7 @@
     load_out.start()
     at.enter()
 
-    n_y = 1 << ((n_f.bit_length() - 1) // 2)
+    n_y = y_members(n_f)
     n_z = n_f // n_y
     my_z, my_y = lax.div(at.me, n_y), lax.rem(at.me, n_y)
 
@@ -305,7 +313,9 @@
     vec_piece(at.me)[...] = vsh[...]
     loop(1, n_f, lambda k: send_v(k).start())
 
-    seg_r, pad_r, pri_r = (ref[...].astype(F32) for ref in (segment, pad, priority))
+    seg_r, pad_r, pri_r = (
+        ref[...].reshape(1, SLOTS).astype(F32) for ref in (segment, pad, priority)
+    )
     lines = jnp.concatenate([seg_r, pad_r, pri_r, jnp.zeros((5, SLOTS), F32)], axis=0)
     columns = jnp.transpose(lines)
     seg_c, pad_c, pri_c = (columns[:, j : j + 1] for j in range(3))
@@ -340,8 +350,12 @@
     chunk_rows = n_f * cap_rows // CHUNKS
     sources = n_f // CHUNKS
 
-    def position(step):
-        return lax.rem(2 * step, 3) + 3 * lax.div(step, 3)
+    def position(step, side):
+        inner = lax.rem(lax.div(step + 1, 2), 2)
+        near = 1 + 2 * lax.rem(step + 1 + side, 2)
+        return inner * near + (1 - inner) * 2 * lax.div(step, 3)
+
+    z_side = lax.rem(my_z, 2)
 
     def send_rows(buffer, into, send, recv, k):
         return remote(
@@ -356,7 +370,7 @@
         into[0:cap_rows, :] = nn(pick(at.me), source[...]).astype(BF16)
 
         def stage(step):
-            first = position(step) * sources
+            first = position(step, 1 - z_side) * sources
 
             def one(r):
                 @pl.when(r > 0)
@@ -471,6 +485,11 @@
     load_in.wait()
     load_out.wait()
     pack[...] = jnp.zeros_like(pack)
+
+    def clear(t):
+        ew[t] = jnp.zeros((FTILE, WIDTH), BF16)
+
+    loop(0, ew.shape[0], clear)
     router = vecs[8 : 8 + experts, :].astype(BF16)
     f_tiles = w_in.shape[1] // FTILE
     bias_at = 8 + experts
@@ -488,7 +507,7 @@
     acc_o, acc_d = d_middle.at[0:chunk_rows, :], d_middle.at[chunk_rows : 2 * chunk_rows, :]
 
     def expert_chunk(step):
-        pos = position(step)
+        pos = position(step, z_side)
         block = aligned(pos, chunk_rows)
         first = pos * sources
 
@@ -540,7 +559,19 @@
 
         loop(first, first + sources, back)
 
+        @pl.when(step < CHUNKS - 1)
+        def _():
+            loop(0, f_tiles, lambda f: add_tiles(f, block))
+
+    def add_tiles(f, block):
+        lanes = aligned(f, FTILE)
+        product = tn(x_in[block, :], d_pre[block, lanes])
+        ew[2 * f] = (ew[2 * f].astype(F32) + product).astype(BF16)
+        product = tn(hidden[block, lanes], g_in[block, :])
+        ew[2 * f + 1] = (ew[2 * f + 1].astype(F32) + product).astype(BF16)
+
     loop(0, CHUNKS, expert_chunk)
+    last = pl.ds(2 * chunk_rows, chunk_rows)
     mine = aligned(at.me, cap_rows)
     table_d[mine, :] = ret_d[0:cap_rows, :]
 
@@ -583,14 +614,8 @@
 
     n_mine = 2 * per_core
 
-    def grad_tiles(core, f):
-        tile = core * per_core + f
-        lanes = aligned(tile, FTILE)
-        ew[2 * tile] = tn(x_in[...], d_pre[:, lanes]).astype(BF16)
-        ew[2 * tile + 1] = tn(hidden[:, lanes], g_in[...]).astype(BF16)
-
     def theirs(f):
-        grad_tiles(other, f)
+        add_tiles(other * per_core + f, last)
         to_partner(2 * f).start()
         to_partner(2 * f + 1).start()
 
@@ -603,7 +628,7 @@
 
     def tile_row(f):
         theirs(f)
-        grad_tiles(at.core, f)
+        add_tiles(at.core * per_core + f, last)
         sum_cores(2 * f)
         sum_cores(2 * f + 1)
 
@@ -662,7 +687,7 @@
             to_core(i, j, at.core).start()
             to_self(i, j).start()
 
-    loop(0, n_mine // 2, e_spread)
+    loop(0, n_mine - 1, e_spread)
     loop(1, n_f, lambda r: returned(ret_d, table_d, s_d, r_d, r).wait_recv())
 
     loop(1, n_f, lambda k: send_rows(send_g, g_in, s_g, r_g, k).wait_send())
@@ -697,40 +722,54 @@
 
     loop(0, SLOTS // ROWBLK, second_back)
 
-    d_wo = tn(mixed[...], routed[...])
-    for pair in range(PAIRS):
-        hidden[WIDTH * 2 : WIDTH * 3, (4 * pair + 3) * TILE : (4 * pair + 4) * TILE] = d_wo[:, pair * TILE : (pair + 1) * TILE].astype(BF16)
-
     units = 16 // n_d
     pairs_in_unit = PAIRS // units
 
-    def own_rows(owner):
-        return pl.ds(pl.multiple_of(WIDTH * 2 + owner * shard, shard), shard)
+    y_rows = n_z * shard
 
     def dense(tile):
         return hidden.at[WIDTH * 2 : WIDTH * 3, aligned(tile, TILE)]
+
+    def put_dense(tile, value):
+        value = value.astype(BF16)
+        for z in range(n_z):
+            for y in range(n_y):
+                low = (z * n_y + y) * shard
+                row = WIDTH * 2 + (y * n_z + z) * shard
+                hidden[row : row + shard, aligned(tile, TILE)] = value[low : low + shard, :]
+
+    def y_block(tile, y):
+        rows = pl.ds(pl.multiple_of(WIDTH * 2 + y * y_rows, shard), y_rows)
+        return hidden.at[rows, aligned(tile, TILE)]
+
+    def z_piece(tile, z):
+        rows = pl.ds(pl.multiple_of(WIDTH * 2 + (my_y * n_z + z) * shard, shard), shard)
+        return hidden.at[rows, aligned(tile, TILE)]
+
+    def own_tile(u, x):
+        return u * n_d + x * 2 + at.core
 
     def g_core(u, x):
         src = dense(u * n_d + x * 2 + other)
         return remote(src, dense_core.at[u, x], s_gc.at[u, x], r_gc.at[u, x], at.partner())
 
+    def g_y(u, x, j):
+        src = y_block(own_tile(u, x), lax.rem(my_y + j, n_y))
+        sems = s_gy.at[u, x, j - 1], r_gy.at[u, x, j - 1]
+        return remote(src, dense_y.at[u, x, j - 1], *sems, (at.d, member(0, j)))
+
+    def g_z(u, x, i):
+        src = z_piece(own_tile(u, x), lax.rem(my_z + i, n_z))
+        sems = s_gz.at[u, x, i], r_gz.at[u, x, i]
+        return remote(src, dense_z.at[u, x, i], *sems, (at.d, member(i, 0)))
+
     def g_x(u, i):
-        src = dense(u * n_d + at.x_index(i) * 2 + at.core)
-        return remote(
-            src, dense_x.at[u, i - 1], s_gx.at[u, i - 1], r_gx.at[u, i - 1], at.x_peer(i)
-        )
-
-    def g_f(u, k):
-        src = hidden.at[own_rows(at.ahead(k)), aligned(u * n_d + at.d, TILE)]
-        return remote(src, dense_f.at[u, k], s_gf.at[u, k], r_gf.at[u, k], at.fsdp_peer(k))
-
-    def g_d(u, i):
-        src = final.at[u * n_d + at.d]
-        return remote(src, src, s_gd.at[u, i], r_gd.at[u, i], at.dp_peer(i))
-
-    def g_d_from(u, i):
-        dst = final.at[u * n_d + lax.rem(at.d + n_d - i, n_d)]
-        return remote(dst, dst, s_gd.at[u, i], r_gd.at[u, i], at.dp_peer(i))
+        sems = s_gx.at[u, i - 1], r_gx.at[u, i - 1]
+        return remote(dense_s.at[u], dense_x.at[u, i - 1], *sems, at.x_peer(i))
+
+    def g_d(u, core):
+        src = final.at[u, core]
+        return remote(src, src, s_gd.at[u], r_gd.at[u], at.partner())
 
     def first_hop(u):
         for x in range(n_x):
@@ -739,32 +778,45 @@
     def second_hop(u):
         for x in range(n_x):
             g_core(u, x).wait_recv()
-            tile = dense(u * n_d + x * 2 + at.core)
+            tile = dense(own_tile(u, x))
             tile[...] = (tile[...].astype(F32) + dense_core[u, x].astype(F32)).astype(BF16)
+            for j in range(1, n_y):
+                g_y(u, x, j).start()
+
+    def third_hop(u):
+        for x in range(n_x):
+            mine = y_block(own_tile(u, x), my_y)
+            total = mine[...].astype(F32)
+            for j in range(1, n_y):
+                g_y(u, x, j).wait_recv()
+                total = total + dense_y[u, x, j - 1].astype(F32)
+            mine[...] = total.astype(BF16)
+            for i in range(1, n_z):
+                g_z(u, x, i).start()
+
+    def fourth_hop(u):
+        for x in range(n_x):
+            total = z_piece(own_tile(u, x), my_z)[...].astype(F32)
+            for i in range(1, n_z):
+                g_z(u, x, i).wait_recv()
+                total = total + dense_z[u, x, i].astype(F32)
+            dense_s[u, x] = total.astype(BF16)
         for i in range(1, n_x):
             g_x(u, i).start()
 
-    def third_hop(u):
-        tile = dense(u * n_d + at.d)
-        total = tile[...].astype(F32)
+    def fifth_hop(u):
+        total = dense_s[u].astype(F32)
         for i in range(1, n_x):
             g_x(u, i).wait_recv()
             total = total + dense_x[u, i - 1].astype(F32)
-        tile[...] = total.astype(BF16)
-        loop(1, n_f, lambda k: g_f(u, k).start())
-
-    def fourth_hop(u):
-        tile = u * n_d + at.d
-        dense_f[u, 0] = hidden[own_rows(at.me), aligned(tile, TILE)]
-        loop(1, n_f, lambda k: g_f(u, k).wait_recv())
-        total = dense_f[u, 0].astype(F32)
-        for k in range(1, n_f):
-            total = total + dense_f[u, k].astype(F32)
-        final[tile] = total.astype(BF16)
-        for i in range(1, n_d):
-            g_d(u, i).start()
-
-    hops = (first_hop, second_hop, third_hop, fourth_hop)
+        final[u, at.core] = total.astype(BF16)
+        g_d(u, at.core).start()
+
+    hops = (first_hop, second_hop, third_hop, fourth_hop, fifth_hop)
+
+    d_wo = tn(mixed[...], routed[...])
+    for pair in range(PAIRS):
+        put_dense(4 * pair + 3, d_wo[:, pair * TILE : (pair + 1) * TILE])
 
     def attend_back(pair):
         for b, (low, high, row) in enumerate(WINDOWS):
@@ -809,7 +861,7 @@
         pack[3:4, aligned(pair, TILE)] = sums[:, 256:384]
         d_w = tn(normed[...], d_qkv)
         for c in range(3):
-            dense(4 * pair + c)[...] = d_w[:, c * TILE : (c + 1) * TILE].astype(BF16)
+            put_dense(4 * pair + c, d_w[:, c * TILE : (c + 1) * TILE])
 
         @pl.when(lax.rem(pair, pairs_in_unit) == pairs_in_unit - 1)
         def _():
@@ -821,10 +873,6 @@
                     hop(unit - age)
 
         send_lot(pair + 2)
-
-        @pl.when(pair == 1)
-        def _():
-            loop(n_mine // 2, n_mine - 1, e_spread)
 
 
     acc_k, acc_v = bias.at[0:SLOTS, 0:TILE], bias.at[0:SLOTS, TILE : 2 * TILE]
@@ -895,6 +943,7 @@
     loop(0, SLOTS // ROWBLK, combine)
     save_out = pltpu.make_async_copy(routed, o_out, s_own.at[4 + n_mine])
     save_out.start()
+    later(units + 3)
 
     loop(1, n_f, lambda k: [p_vec(k).wait_recv(), p_qv(k).wait_recv()])
     vec_f[0] = pack_dp[0, 0:bias_at, vec_lane(at.me)]
@@ -909,7 +958,7 @@
     save_qv = pltpu.make_async_copy(qv_f.at[0], o_qv, s_own.at[6 + n_mine])
     save_vec.start()
     save_qv.start()
-    loop(0, units, lambda u: [g_d_from(u, i).wait_recv() for i in range(1, n_d)])
+    loop(0, units, lambda u: g_d(u, other).wait_recv())
     save_dense = pltpu.make_async_copy(final, o_dense, s_own.at[7 + n_mine])
     save_dense.start()
 
@@ -942,11 +991,13 @@
     def ended_u(u):
         for x in range(n_x):
             g_core(u, x).wait_send()
+            for j in range(1, n_y):
+                g_y(u, x, j).wait_send()
+            for i in range(1, n_z):
+                g_z(u, x, i).wait_send()
         for i in range(1, n_x):
             g_x(u, i).wait_send()
-        loop(1, n_f, lambda k: g_f(u, k).wait_send())
-        for i in range(1, n_d):
-            g_d(u, i).wait_send()
+        g_d(u, at.core).wait_send()
 
     loop(0, units, ended_u)
     for i in range(1, n_d):
@@ -966,6 +1017,8 @@
     hid = w_in.shape[1]
     units = 16 // n_d
     n_mine = hid // FTILE
+    n_y = y_members(n_f)
+    more_y = max(n_y - 1, 1)
     pack_rows = 8 + experts + 8
     sds = jax.ShapeDtypeStruct
     vm = pltpu.VMEM
@@ -978,7 +1031,7 @@
             sds((SLOTS, WIDTH), BF16),
             sds((SLOTS, WIDTH), F32),
             sds((2 * n_mine, FTILE, WIDTH), BF16),
-            sds((16, shard, TILE), BF16),
+            sds((units, 2, n_x, shard, TILE), BF16),
             sds((8 + experts, TILE), F32),
             sds((8, TILE), F32),
             sds((8, WIDTH), F32),
@@ -1012,9 +1065,11 @@
             vm((n_mine, FTILE, WIDTH), BF16),
             vm((more_x, n_mine, FTILE // n_x, WIDTH), BF16),
             vm((units, n_x, WIDTH, TILE), BF16),
-            vm((units, more_x, WIDTH, TILE), BF16),
-            vm((units, n_f, shard, TILE), BF16),
-            vm((16, shard, TILE), BF16),
+            vm((units, n_x, more_y, n_f // n_y * shard, TILE), BF16),
+            vm((units, n_x, n_f // n_y, shard, TILE), BF16),
+            vm((units, n_x, shard, TILE), BF16),
+            vm((units, more_x, n_x, shard, TILE), BF16),
+            vm((units, 2, n_x, shard, TILE), BF16),
             vm((pack_rows, WIDTH), F32),
             vm((n_d, pack_rows, WIDTH), F32),
             vm((n_f, 8 + experts, TILE), F32),
@@ -1034,9 +1089,10 @@
         + pairs_of(more_x, n_mine)
         + pairs_of(n_x, n_mine)
         + pairs_of(units, n_x)
+        + pairs_of(units, n_x, more_y)
+        + pairs_of(units, n_x, n_f // n_y)
         + pairs_of(units, more_x)
-        + pairs_of(units, n_f)
-        + pairs_of(units, n_d)
+        + pairs_of(units)
         + pairs_of(n_d)
         + pairs_of(n_f)
         + pairs_of(n_f)
@@ -1106,11 +1162,16 @@
     o_router[...] = own[8 : 8 + experts, :]
     lines = my_lanes(qv[...], 2 * shard)
     o_bqv[...] = jnp.where(me * 2 * shard < WIDTH, lines[2:3, :], lines[3:4, :])
+    n_d = 2 * dense.shape[2]
+
+    def tile(t):
+        return dense[t // n_d, t % 2, t % n_d // 2].astype(F32)
+
     for pair in range(PAIRS):
         for c in range(3):
             at = c * WIDTH + pair * TILE
-            o_qkv[:, at : at + TILE] = dense[4 * pair + c].astype(F32)
-        o_wo[:, pair * TILE : (pair + 1) * TILE] = dense[4 * pair + 3].astype(F32)
+            o_qkv[:, at : at + TILE] = tile(4 * pair + c)
+        o_wo[:, pair * TILE : (pair + 1) * TILE] = tile(4 * pair + 3)
     for f in range(tiles // 2):
         o_b_in[:, f * FTILE : (f + 1) * FTILE] = biases[f : f + 1, :]
     o_b_out[...] = biases[4:5, :]
@@ -1203,8 +1264,8 @@
     small = (
         tokens,
         cotangent,
-        line(segment_ids),
-        line(pad_mask),
+        segment_ids,
+        pad_mask,
         expert_ids.T,
         priority,
         w_qkv,

time: 204 us -> 196 us (0.961)
  Pallas kernels: 200 us -> 194 us
  local copies, waits for them, and re-layouts: 2.53 us -> 0 us
    pallas_call x1, Pallas kernels: 192 us -> 186 us  [block(): pl.pallas_call(functools.partial(block_kernel, n_f, n_d, experts, cap, ca...]
    reshape x2 -> x0, local copies, waits for them, and re-layouts: 2.53 us -> none  [shards(): line = lambda vector: vector.reshape(1, -1)]
where the time goes in v5:
time: 196 us; the launch traced here: 194 us
  Pallas kernels  194 us (99%)
    pallas_call x1, Pallas kernels, block(): pl.pallas_call(functools.partial(block_kernel, n_f, n_d, experts, cap, ca...  186 us
    pallas_call x1, Pallas kernels, finish(): pl.pallas_call(functools.partial(finish_kernel, n_f, experts), out_shape=...  7.9 us

profile of v5, /device:TPU:1, one launch (start us, length us, event | category | flops | bytes accessed | tf_op | source)
XLA Modules:
  0.0 194.5 jit_solution(9955440102610889791)
XLA Ops:
  0.7 185.8 %block.1 = (bf16[720,512]{1,0:T(8,128)(2,1)}, f32[720,512]{1,0:T(8,128)}, bf16[8,512,512]{2,1,0:T(8,128)(2,1)}, bf16[4,2,2,64,128]{4,3,2,1,0:T(8,128)(2,1)}, f32...) custom-call(bf16[720,512]{1,0:T(8,128)(2,1)} %tok.1, bf16[720,512]{1,0:T(8,128)(2,1)} %cot.1, s32[720]{0:T(1024)} %segment.1, ...), custom_call_target="tpu_custom_call" | custom-call | tf_op jit(solution)/shard_map/block/pallas_call | solution.py:1028
  186.4 7.9 %finish.1 = (bf16[720,512]{1,0:T(8,128)(2,1)}, f32[720,512]{1,0:T(8,128)}, f32[1,64]{1,0:T(1,128)}, f32[1,64]{1,0:T(1,128)}, f32[64,1536]{1,0:T(8,128)}, /*index...) custom-call(bf16[720,512]{1,0:T(8,128)(2,1)} %get-tuple-element.37.i, ...), custom_call_target="tpu_custom_call" | custom-call | tf_op jit(solution)/shard_map/finish/pallas_call | solution.py:1203

commit v6 on v5

--- a/solution.py
+++ b/solution.py
@@ -114,8 +114,8 @@
     experts,
     cap,
     cap_rows,
-    tok,
-    cot,
+    tok_hbm,
+    cot_hbm,
     segment,
     pad,
     chosen_ids,
@@ -140,6 +140,8 @@
     o_vec,
     o_qv,
     o_bias,
+    tok,
+    cot,
     wfull,
     vsh,
     vecs,
@@ -238,8 +240,10 @@
 
     load_in = pltpu.make_async_copy(w_in_hbm, w_in, s_own.at[0])
     load_out = pltpu.make_async_copy(w_out_hbm, w_out, s_own.at[1])
-    load_in.start()
-    load_out.start()
+    load_tok = pltpu.make_async_copy(tok_hbm, tok, s_own.at[2])
+    load_cot = pltpu.make_async_copy(cot_hbm, cot, s_own.at[3])
+    for load in (load_cot, load_tok, load_in, load_out):
+        load.start()
     at.enter()
 
     n_y = y_members(n_f)
@@ -400,6 +404,7 @@
         pass_on(k)
 
     loop(1, n_z, from_z)
+    load_cot.wait()
     dispatch(cot, send_g, g_in, s_g, r_g)
     loop(n_z, n_f, from_y)
 
@@ -410,6 +415,8 @@
         vecs[...] += vec_piece(owner)[...].astype(F32)
 
     loop(1, n_f, add_vectors)
+
+    load_tok.wait()
 
     def first_norm(i):
         block = aligned(i, ROWBLK)
@@ -650,12 +657,12 @@
 
     def send_lot(lot):
         def one(step):
-            r = 1 + lax.rem(n_f // 2 - 1 + step, n_f - 1)
+            r = 1 + lax.rem(1 + step, n_f - 1)
             give_back(ret_o, table_o, s_o, r_o, r).start()
 
         loop(lax.div((n_f - 1) * lot, LOTS), lax.div((n_f - 1) * (lot + 1), LOTS), one)
 
-    loop(0, 2, send_lot)
+    loop(0, 3, send_lot)
 
     def returned(buffer, into, send, recv, r):
         home = at.ahead(n_f - r)
@@ -872,7 +879,9 @@
                 def _(age=age, hop=hop):
                     hop(unit - age)
 
-        send_lot(pair + 2)
+        @pl.when(pair == 0)
+        def _():
+            loop(3, LOTS, send_lot)
 
 
     acc_k, acc_v = bias.at[0:SLOTS, 0:TILE], bias.at[0:SLOTS, TILE : 2 * TILE]
@@ -884,7 +893,6 @@
                 hop(step - age)
 
     later(units)
-    send_lot(PAIRS + 2)
 
     def first_back(i):
         block = aligned(i, ROWBLK)
@@ -1036,9 +1044,11 @@
             sds((8, TILE), F32),
             sds((8, WIDTH), F32),
         ),
-        in_specs=[vmem] * len(small) + [hbm] * 2 + [vmem] * 2,
+        in_specs=[hbm] * 2 + [vmem] * (len(small) - 2) + [hbm] * 2 + [vmem] * 2,
         out_specs=[hbm] * 7,
         scratch_shapes=[
+            vm((SLOTS, WIDTH), BF16),
+            vm((SLOTS, WIDTH), BF16),
             vm((WIDTH, 4 * WIDTH), BF16),
             vm((vec_rows, WIDTH), BF16),
             vm((vec_rows, WIDTH), F32),

time: 196 us -> 194 us (0.990)
  no operation moved by 1% of the time
where the time goes in v6:
time: 194 us
  Pallas kernels  193 us (99%)
    pallas_call x1, Pallas kernels, block(): pl.pallas_call(functools.partial(block_kernel, n_f, n_d, experts, cap, ca...  185 us
    pallas_call x1, Pallas kernels, finish(): pl.pallas_call(functools.partial(finish_kernel, n_f, experts), out_shape=...  7.9 us

profile of v6, /device:TPU:1, one launch (start us, length us, event | category | flops | bytes accessed | tf_op | source)
XLA Modules:
  0.0 193.9 jit_solution(8343993060186976149)
XLA Ops:
  0.7 185.2 %block.1 = (bf16[720,512]{1,0:T(8,128)(2,1)}, f32[720,512]{1,0:T(8,128)}, bf16[8,512,512]{2,1,0:T(8,128)(2,1)}, bf16[4,2,2,64,128]{4,3,2,1,0:T(8,128)(2,1)}, f32...) custom-call(bf16[720,512]{1,0:T(8,128)(2,1)} %tok_hbm.1, bf16[720,512]{1,0:T(8,128)(2,1)} %cot_hbm.1, ...), custom_call_target="tpu_custom_call" | custom-call | tf_op jit(solution)/shard_map/block/pallas_call | solution.py:1036
  185.9 7.9 %finish.1 = (bf16[720,512]{1,0:T(8,128)(2,1)}, f32[720,512]{1,0:T(8,128)}, f32[1,64]{1,0:T(1,128)}, f32[1,64]{1,0:T(1,128)}, f32[64,1536]{1,0:T(8,128)}, /*index...) custom-call(bf16[720,512]{1,0:T(8,128)(2,1)} %get-tuple-element.37.i, ...), custom_call_target="tpu_custom_call" | custom-call | tf_op jit(solution)/shard_map/finish/pallas_call | solution.py:1213

commit v7 on v6

--- a/solution.py
+++ b/solution.py
@@ -892,7 +892,6 @@
             if 0 <= step - age < units:
                 hop(step - age)
 
-    later(units)
 
     def first_back(i):
         block = aligned(i, ROWBLK)
@@ -903,6 +902,7 @@
         d_middle[block, :] += norm_back(grad, value, inv_std, vecs[0:1, :])
 
     loop(0, SLOTS // ROWBLK, first_back)
+    later(units)
     save_tokens = pltpu.make_async_copy(d_middle.at[0:SLOTS, :], o_tokens, s_own.at[2 + n_mine])
     save_tokens.start()
 

time: 194 us -> 192 us (0.990)
  Pallas kernels: 193 us -> 191 us
where the time goes in v7:
time: 192 us
  Pallas kernels  191 us (99%)
    pallas_call x1, Pallas kernels, block(): pl.pallas_call(functools.partial(block_kernel, n_f, n_d, experts, cap, ca...  184 us
    pallas_call x1, Pallas kernels, finish(): pl.pallas_call(functools.partial(finish_kernel, n_f, experts), out_shape=...  7.9 us

profile of v7, /device:TPU:1, one launch (start us, length us, event | category | flops | bytes accessed | tf_op | source)
XLA Modules:
  0.0 192.3 jit_solution(13426322755556663516)
XLA Ops:
  0.7 183.6 %block.1 = (bf16[720,512]{1,0:T(8,128)(2,1)}, f32[720,512]{1,0:T(8,128)}, bf16[8,512,512]{2,1,0:T(8,128)(2,1)}, bf16[4,2,2,64,128]{4,3,2,1,0:T(8,128)(2,1)}, f32...) custom-call(bf16[720,512]{1,0:T(8,128)(2,1)} %tok_hbm.1, bf16[720,512]{1,0:T(8,128)(2,1)} %cot_hbm.1, ...), custom_call_target="tpu_custom_call" | custom-call | tf_op jit(solution)/shard_map/block/pallas_call | solution.py:1036
  184.2 7.9 %finish.1 = (bf16[720,512]{1,0:T(8,128)(2,1)}, f32[720,512]{1,0:T(8,128)}, f32[1,64]{1,0:T(1,128)}, f32[1,64]{1,0:T(1,128)}, f32[64,1536]{1,0:T(8,128)}, /*index...) custom-call(bf16[720,512]{1,0:T(8,128)(2,1)} %get-tuple-element.37.i, ...), custom_call_target="tpu_custom_call" | custom-call | tf_op jit(solution)/shard_map/finish/pallas_call | solution.py:1213

commit v8 on v7

--- a/solution.py
+++ b/solution.py
@@ -902,7 +902,6 @@
         d_middle[block, :] += norm_back(grad, value, inv_std, vecs[0:1, :])
 
     loop(0, SLOTS // ROWBLK, first_back)
-    later(units)
     save_tokens = pltpu.make_async_copy(d_middle.at[0:SLOTS, :], o_tokens, s_own.at[2 + n_mine])
     save_tokens.start()
 
@@ -911,6 +910,7 @@
 
     for i in range(1, n_d):
         p_dp(i).start()
+    later(units)
     later(units + 1)
     e_spread(n_mine - 1)
     loop(0, n_mine - 1, e_forward)

time: 192 us -> 192 us (level)
  no operation moved by 1% of the time
where the time goes in v8:
time: 192 us; the launch traced here: 191 us
  Pallas kernels  191 us (99%)
    pallas_call x1, Pallas kernels, block(): pl.pallas_call(functools.partial(block_kernel, n_f, n_d, experts, cap, ca...  183 us
    pallas_call x1, Pallas kernels, finish(): pl.pallas_call(functools.partial(finish_kernel, n_f, experts), out_shape=...  7.9 us

profile of v8, /device:TPU:1, one launch (start us, length us, event | category | flops | bytes accessed | tf_op | source)
XLA Modules:
  0.0 191.5 jit_solution(1667521744147399412)
XLA Ops:
  0.7 182.8 %block.1 = (bf16[720,512]{1,0:T(8,128)(2,1)}, f32[720,512]{1,0:T(8,128)}, bf16[8,512,512]{2,1,0:T(8,128)(2,1)}, bf16[4,2,2,64,128]{4,3,2,1,0:T(8,128)(2,1)}, f32...) custom-call(bf16[720,512]{1,0:T(8,128)(2,1)} %tok_hbm.1, bf16[720,512]{1,0:T(8,128)(2,1)} %cot_hbm.1, ...), custom_call_target="tpu_custom_call" | custom-call | tf_op jit(solution)/shard_map/block/pallas_call | solution.py:1036
  183.4 7.9 %finish.1 = (bf16[720,512]{1,0:T(8,128)(2,1)}, f32[720,512]{1,0:T(8,128)}, f32[1,64]{1,0:T(1,128)}, f32[1,64]{1,0:T(1,128)}, f32[64,1536]{1,0:T(8,128)}, /*index...) custom-call(bf16[720,512]{1,0:T(8,128)(2,1)} %get-tuple-element.37.i, ...), custom_call_target="tpu_custom_call" | custom-call | tf_op jit(solution)/shard_map/finish/pallas_call | solution.py:1213
